TPU v7x, 256 devices: a whole 4x4x8 slice. The times are simulated.
256 devices in a mesh: row: 16 (over x, z_lo, core), col: 4 (over z_hi), aux: 4 (over y).
Axes of the slice: x: 4, y: 4, z: 8 (z_hi: 4, z_lo: 2; z = z_hi * 2 + z_lo), core: 2. Of those that a mesh axis runs over, the one named last changes fastest.
Arguments:
- colloc: bfloat16 [4096, 4096], P(('row', 'col'), 'aux'), may hold values from -6 to 6
- coulomb: bfloat16 [4096, 16384], P(('row', 'col'), 'aux'), may hold values from -6 to 6
- geminal: bfloat16 [4096, 20480], P(('row', 'col'), 'aux'), may hold values from -6 to 6
- occupied: bfloat16 [4096, 256], P(('row', 'col')), may hold values from -6 to 6
Outputs:
- pair_field: float32 [4096, 256], P(('row', 'col', 'aux'))
- energy: float32 [256], replicated
All inputs are finite; a program needn't handle non-finite values.
Results may differ from a plain program's by a relative error of at most 0.0057.
Values may be sent and summed in bfloat16 or wider, within the bound.
No kernel may reach another device: no remote copies, remote signals or barrier semaphores. Data moves between devices by JAX's collectives and lax.ppermute only.
A program may use at most 128 MiB of HBM per device.

v0:
```python
import math

import jax
import jax.numpy as jnp
from jax import lax
from jax.sharding import PartitionSpec as P

NBAS = 4096
NAUXC = 16384
NAUXF = 20480


def shards(colloc, coulomb, geminal, occupied):
    aux_count = lax.axis_size("aux")
    row_count = lax.axis_size("row")
    col_count = lax.axis_size("col")
    row_index = lax.axis_index("row")
    col_index = lax.axis_index("col")
    aux_index = lax.axis_index("aux")
    points = colloc.shape[0]
    quarter_rows = points // aux_count
    grid_total = points * row_count * col_count
    tile_rows = points * col_count
    width_cols = row_count * quarter_rows
    row_colloc, row_coul, row_gem = (
        lax.all_gather(colloc, "col", axis=0, tiled=True),
        lax.all_gather(coulomb, "col", axis=0, tiled=True),
        lax.all_gather(geminal, "col", axis=0, tiled=True),
    )

    def by_quarter(values):
        return values.reshape(aux_count, quarter_rows, values.shape[1])

    piece_colloc = lax.all_gather(by_quarter(colloc), "row", axis=1, tiled=True)
    piece_coul = lax.all_gather(by_quarter(coulomb), "row", axis=1, tiled=True)
    piece_gem = lax.all_gather(by_quarter(geminal), "row", axis=1, tiled=True)
    piece_occ = lax.all_gather(by_quarter(occupied), "row", axis=1, tiled=True)
    contrib = jnp.stack(
        [
            jnp.einsum("pm,gqm->pgq", row_colloc, piece_colloc, preferred_element_type=jnp.float32),
            jnp.einsum("pm,gqm->pgq", row_coul, piece_coul, preferred_element_type=jnp.float32),
            jnp.einsum("pm,gqm->pgq", row_gem, piece_gem, preferred_element_type=jnp.float32),
        ]
    )
    fit_tiles = contrib
    occ_cols = piece_occ
    fit_tiles, occ_cols = (fit_tiles, occ_cols)
    quarter = lax.psum_scatter(fit_tiles, "aux", scatter_dimension=2, tiled=True)[:, :, 0]
    basis_gram = quarter[0] / math.sqrt(NBAS)
    coul_fit = quarter[1] / math.sqrt(NAUXC)
    gem_fit = quarter[2] / math.sqrt(NAUXF)
    row_global = row_index * tile_rows + jnp.arange(tile_rows, dtype=jnp.int32)[:, None]
    col_local = jnp.arange(width_cols, dtype=jnp.int32)[None, :]
    col_global = (
        (col_local // quarter_rows * col_count + col_index) * points
        + aux_index * quarter_rows
        + col_local % quarter_rows
    )
    kernel = jnp.where(
        row_global == col_global, jnp.float32(0.0), basis_gram * basis_gram * coul_fit * gem_fit
    ).astype(jnp.bfloat16)
    occ_quarter = lax.dynamic_index_in_dim(occ_cols, aux_index, 0, keepdims=False).astype(
        jnp.float32
    )
    col_weight = (occ_quarter * occ_quarter).astype(jnp.bfloat16)
    partial_field = jnp.dot(kernel, col_weight, preferred_element_type=jnp.float32) / math.sqrt(
        grid_total
    )
    pair_field = lax.psum_scatter(partial_field, ("col", "aux"), scatter_dimension=0, tiled=True)
    own_occ = lax.dynamic_slice_in_dim(occupied, aux_index * quarter_rows, quarter_rows, 0).astype(
        jnp.float32
    )
    own_weight = (own_occ * own_occ).astype(jnp.bfloat16)
    weight_back = lax.optimization_barrier(own_weight).astype(jnp.float32)
    local_energy = jnp.sum(weight_back * pair_field, axis=0) / math.sqrt(grid_total)
    energy = lax.psum(local_energy, ("row", "col", "aux"))
    return (pair_field, energy)


def solution(mesh):
    in_specs = (
        P(("row", "col"), "aux"),
        P(("row", "col"), "aux"),
        P(("row", "col"), "aux"),
        P(("row", "col"), None),
    )
    out_specs = (P(("row", "col", "aux"), None), P())
    return jax.shard_map(shards, mesh=mesh, in_specs=in_specs, out_specs=out_specs, check_vma=False)
```

profile of v0, /device:TPU:1, one launch (start us, length us, event | category | flops | bytes accessed | tf_op | source)
XLA Modules:
  0.0 547.8 jit_solution(9925822597663715358)
XLA Ops:
  7.2 0.0 all-gather.6.cloned.1.call-start
  7.2 0.7 all-gather.6.cloned.1.call-update
  7.9 0.0 all-gather.8.cloned.1.call-start
  7.9 0.7 all-gather.8.cloned.1.call-update
  8.6 0.0 all-gather.10.cloned.1.call-start
  8.7 0.7 all-gather.10.cloned.1.call-update
  9.4 0.0 all-gather.12.cloned.1.call-start
  9.4 0.5 all-gather.12.cloned.1.call-update
  10.0 0.0 all-gather.14.cloned.1.call-start
  10.0 0.5 all-gather.14.cloned.1.call-update
  10.5 0.0 all-reduce.3.cloned.1.call-start
  10.6 18.3 %all_gather.21 = bf16[256,1024]{1,0:T(8,128)(2,1)S(1)} all-gather(bf16[64,1024]{1,0:T(8,128)(2,1)} %param.4), channel_id=1, replica_groups=mesh['row'=16,'col'=4,'aux'=4] {'col'}, dimensions={0}, use_global_device_ids=true | all-gather | bytes 655360 | tf_op jit(solution)/shard_map/all_gather | solution.py:26
  28.8 23.1 %all-gather.6.cloned.1.call-done = bf16[4,256,1024]{2,1,0:T(8,128)(2,1)} async-done(((bf16[4,16,1024]{2,1,0:T(8,128)(2,1)}), bf16[4,256,1024]{2,1,0:T(8,128)(2,1)}) %all-gather.6.cloned.1.call-update) | async-done | bytes 2097168 | tf_op jit(solution)/shard_map/all_gather | solution.py:34
  52.0 2.3 convolution_bitcast_fusion
  54.3 47.0 %all-gather.8.cloned.1.call-done = bf16[256,4096]{1,0:T(8,128)(2,1)} async-done(((bf16[64,4096]{1,0:T(8,128)(2,1)}), bf16[256,4096]{1,0:T(8,128)(2,1)}) %all-gather.8.cloned.1.call-update) | async-done | bytes 2097168 | tf_op jit(solution)/shard_map/all_gather | solution.py:27
  101.3 58.2 %all-gather.10.cloned.1.call-done = bf16[4,256,4096]{2,1,0:T(8,128)(2,1)} async-done(((bf16[4,16,4096]{2,1,0:T(8,128)(2,1)}), bf16[4,256,4096]{2,1,0:T(8,128)(2,1)}) %all-gather.10.cloned.1.call-update) | async-done | bytes 8388624 | tf_op jit(solution)/shard_map/all_gather | solution.py:35
  159.5 6.4 %fusion.4 = f32[1,256,4,256]{3,1,2,0:T(8,128)S(1)} fusion(bf16[4,256,4096]{2,1,0:T(8,128)(2,1)} %all-gather.10.cloned.1.call-done, bf16[256,4096]{1,0:T(8,128)(2,1)} %all-gather.8.cloned.1.call-done), kind=kOutput, calls=%fused_computation.6 | convolution fusion | flops 2147483648 | bytes 11534336 | tf_op jit(solution)/shard_map/pm,gqm->pgq/dot_general | solution.py:41
  165.9 56.1 %all-gather.12.cloned.1.call-done = bf16[256,5120]{1,0:T(8,128)(2,1)} async-done(((bf16[64,5120]{1,0:T(8,128)(2,1)}), bf16[256,5120]{1,0:T(8,128)(2,1)}) %all-gather.12.cloned.1.call-update) | async-done | bytes 2621456 | tf_op jit(solution)/shard_map/all_gather | solution.py:28
  222.0 65.2 %all-gather.14.cloned.1.call-done = bf16[4,256,5120]{2,1,0:T(8,128)(2,1)} async-done(((bf16[4,16,5120]{2,1,0:T(8,128)(2,1)}), bf16[4,256,5120]{2,1,0:T(8,128)(2,1)}) %all-gather.14.cloned.1.call-update) | async-done | bytes 10485776 | tf_op jit(solution)/shard_map/all_gather | solution.py:36
  287.2 6.5 %fusion.7 = f32[1,256,4,256]{3,1,2,0:T(8,128)S(1)} fusion(bf16[4,256,5120]{2,1,0:T(8,128)(2,1)} %all-gather.14.cloned.1.call-done, bf16[256,5120]{1,0:T(8,128)(2,1)} %all-gather.12.cloned.1.call-done), kind=kOutput, calls=%fused_computation.7 | convolution fusion | flops 2684354560 | bytes 14155776 | tf_op jit(solution)/shard_map/pm,gqm->pgq/dot_general | solution.py:42
  293.6 2.0 pad_maximum_fusion
  295.7 0.0 copy-start.1
  295.7 0.0 copy-start
  295.7 0.0 all-reduce.3.cloned.1.call-update
  295.7 0.0 reduce-scatter.5.cloned.1.call-start
  295.8 0.6 copy-done.1
  296.3 0.6 dynamic-slice
  296.9 0.0 copy-done
  296.9 21.2 %all_gather.27 = bf16[4,256,256]{2,1,0:T(8,128)(2,1)S(1)} all-gather(bf16[4,16,256]{2,1,0:T(8,128)(2,1)S(1)} %bitcast.44), channel_id=1, replica_groups=mesh['row'=16,'col'=4,'aux'=4] {'row'}, dimensions={1}, use_global_device_ids=true | all-gather | bytes 557056 | tf_op jit(solution)/shard_map/all_gather | solution.py:37
  318.2 59.0 %all-reduce.3.cloned.1.call-done = f32[3,256,4,256]{3,1,2,0:T(8,128)} async-done(((f32[3,256,4,256]{3,1,2,0:T(8,128)}), f32[3,256,4,256]{3,1,2,0:T(8,128)}) %all-reduce.3.cloned.1.call-update) | async-done | bytes 3145744
  377.2 2.7 convolution_multiply_fusion
  379.9 0.0 reduce-scatter.5.cloned.1.call-update
  379.9 84.7 %reduce-scatter.5.cloned.1.call-done = f32[16,256]{1,0:T(8,128)} async-done(((f32[256,256]{1,0:T(8,128)}), f32[16,256]{1,0:T(8,128)}) %reduce-scatter.5.cloned.1.call-update) | async-done | bytes 16400 | tf_op jit(solution)/shard_map/reduce_scatter | solution.py:69
  464.6 0.7 multiply_reduce_fusion
  465.3 75.6 %psum.7 = f32[256]{0:T(256)} all-reduce(f32[256]{0:T(256)S(1)} %broadcast_multiply_fusion), channel_id=1, replica_groups=mesh['row'=16,'col'=4,'aux'=4] {'row','col','aux'}, use_global_device_ids=true, to_apply=%region_3.4 | all-reduce | flops 256 | bytes 2048 | tf_op jit(solution)/shard_map/psum | solution.py:76
  (3 shorter events, 0.0 us)
Async XLA Ops:
  7.2 44.8 %all-gather.6.cloned.1.call-start = ((), (), s32[]{:S(2)}) async-start(), calls=%async_computation.1 | async-start | bytes 2228224 | tf_op jit(solution)/shard_map/all_gather | solution.py:34
  7.9 93.4 %all-gather.8.cloned.1.call-start = ((), (), s32[]{:S(2)}) async-start(), calls=%async_computation.2 | async-start | bytes 2621440 | tf_op jit(solution)/shard_map/all_gather | solution.py:27
  8.6 150.9 %all-gather.10.cloned.1.call-start = ((), (), s32[]{:S(2)}) async-start(), calls=%async_computation.3 | async-start | bytes 8912896 | tf_op jit(solution)/shard_map/all_gather | solution.py:35
  9.4 212.6 %all-gather.12.cloned.1.call-start = ((), (), s32[]{:S(2)}) async-start(), calls=%async_computation.4 | async-start | bytes 3276800 | tf_op jit(solution)/shard_map/all_gather | solution.py:28
  10.0 277.2 %all-gather.14.cloned.1.call-start = ((), (), s32[]{:S(2)}) async-start(), calls=%async_computation.5 | async-start | bytes 11141120 | tf_op jit(solution)/shard_map/all_gather | solution.py:36
  10.5 366.6 %all-reduce.3.cloned.1.call-start = ((), (), s32[]{:S(2)}) async-start(), calls=%async_computation.7 | async-start | bytes 6291456
  295.7 0.7 copy-start.1
  295.7 1.3 copy-start
  295.7 168.9 %reduce-scatter.5.cloned.1.call-start = ((), (), s32[]{:S(2)}) async-start(), calls=%async_computation.6 | async-start | bytes 278528 | tf_op jit(solution)/shard_map/reduce_scatter | solution.py:69
Sparse Core Ops, SparseCore 0:
  9.8 42.1 all-gather.5
  53.8 47.5 all-gather.7
  103.2 56.3 all-gather.9
  161.2 60.7 all-gather.11
  223.6 63.4 all-gather.13
  295.8 81.3 all-reduce.2
  381.2 83.3 reduce-scatter.4
where the time goes:
time: 548 us
  waiting for transfers between devices  396 us (72%)
  blocking collectives  115 us (21%)
  matrix products  17.9 us (3%)
  between operations  14.2 us (3%)
    reduce_scatter x1, waiting for transfers between devices, shards(): lax.psum_scatter(partial_field, ('col', 'aux'), scatter_dimension=0, tile...  84.7 us
    psum x1, blocking collectives, shards(): energy = lax.psum(local_energy, ('row', 'col', 'aux'))  75.6 us
    all_gather x1, waiting for transfers between devices, shards(): piece_gem = lax.all_gather(by_quarter(geminal), 'row', axis=1, tiled=True)  65.2 us
    unnamed x8, waiting for transfers between devices  62.2 us
    all_gather x1, waiting for transfers between devices, shards(): piece_coul = lax.all_gather(by_quarter(coulomb), 'row', axis=1, tiled=True)  58.2 us
    all_gather x1, waiting for transfers between devices, shards(): lax.all_gather(geminal, 'col', axis=0, tiled=True)  56.1 us
    all_gather x1, waiting for transfers between devices, shards(): lax.all_gather(coulomb, 'col', axis=0, tiled=True)  47 us
    all_gather x1, waiting for transfers between devices, shards(): piece_colloc = lax.all_gather(by_quarter(colloc), 'row', axis=1, tiled=True)  23.1 us
  transfers between devices with their start and end apart: 7, of which 7 were waited for; matrix products, arithmetic and copies ran while one was open for 2% of the time, Pallas kernels for 0%

commit v1 on v0

v1 whole, which is shorter than its diff:
```python
import math

import jax
import jax.numpy as jnp
from jax import lax
from jax.sharding import Mesh, PartitionSpec as P

NBAS = 4096
NAUXC = 16384
NAUXF = 20480
NGRID = 4096
ZN = 8
YN = 4


def z_slot(z):
    return (z % 2) * (ZN // 2) + z // 2


def shift_z(v, d):
    return lax.ppermute(v, ("l", "h"), [(z_slot(z), z_slot((z + d) % ZN)) for z in range(ZN)])


def shift_x(v, d):
    return lax.ppermute(v, "x", [(i, (i + d) % 4) for i in range(4)])


def swap_core(v):
    return lax.ppermute(v, "c", [(0, 1), (1, 0)])


def shards(colloc, coulomb, geminal, occupied):
    points = colloc.shape[0]
    sub = points // YN
    core = lax.axis_index("c")
    xi = lax.axis_index("x")
    yi = lax.axis_index("y")
    z = lax.axis_index("h") * 2 + lax.axis_index("l")

    full = jnp.stack([geminal, jnp.concatenate([coulomb, colloc], axis=1)])

    occ_z = lax.all_gather(occupied, ("l", "h"), axis=0, tiled=False)
    own_occ = lax.dynamic_slice_in_dim(occupied, yi * sub, sub, 0)
    occ_x = lax.all_gather(own_occ, ("x", "c"), axis=0, tiled=True).astype(jnp.float32)
    w_row = (occ_x * occ_x).astype(jnp.bfloat16)

    xf1, xb1 = shift_x(full, 1), shift_x(full, -1)
    f1, b1 = shift_z(full, 1), shift_z(full, -1)
    x2g, x2c = shift_x(xf1[0], 1), shift_x(xb1[1], -1)
    f2, b2 = shift_z(f1, 1), shift_z(b1, -1)
    f3, b3 = shift_z(f2, 1), shift_z(b2, -1)
    f4, b4 = shift_z(f3[0], 1), shift_z(b3[1], -1)

    o0, of1, ob1 = swap_core(full), swap_core(xf1), swap_core(xb1)
    o2g, o2c = swap_core(x2g), swap_core(x2c)

    def rows(blocks):
        return jnp.concatenate([b.reshape(YN, sub, b.shape[-1]) for b in blocks], axis=1)

    row_g = rows([full[0], o0[0], xb1[0], ob1[0], x2g, o2g, xf1[0], of1[0]])
    row_c = rows([full[1], o0[1], xb1[1], ob1[1], x2c, o2c, xf1[1], of1[1]])

    def gram(cg, cc):
        t = jnp.stack(
            [
                jnp.einsum("qk,ypk->yqp", cg, row_g, preferred_element_type=jnp.float32),
                jnp.einsum("qk,ypk->yqp", cc[:, :NAUXC // YN], row_c[:, :, : NAUXC // YN], preferred_element_type=jnp.float32),
                jnp.einsum("qk,ypk->yqp", cc[:, NAUXC // YN :], row_c[:, :, NAUXC // YN :], preferred_element_type=jnp.float32),
            ],
            axis=1,
        )
        s = lax.all_to_all(t, "y", 0, 0, tiled=True).sum(0)
        bas = s[2] / math.sqrt(NBAS)
        return bas * bas * (s[1] / math.sqrt(NAUXC)) * (s[0] / math.sqrt(NAUXF))

    def pair(a, b):
        return jnp.concatenate([a[0], b[0]]), jnp.concatenate([a[1], b[1]])

    k0 = gram(full[0], full[1])
    q = lax.broadcasted_iota(jnp.int32, k0.shape, 0)
    p = lax.broadcasted_iota(jnp.int32, k0.shape, 1)
    k0 = jnp.where((p < sub) & (q == p + yi * sub), jnp.float32(0.0), k0)
    k1 = gram(*pair(f1, b1))
    k2 = gram(*pair(f2, b2))
    k3 = gram(*pair(f3, b3))
    k4 = gram(f4, b4)
    kern = jnp.concatenate([k0, k1, k2, k3, k4], axis=0).astype(jnp.bfloat16)

    order = jnp.array([0, -1, 1, -2, 2, -3, 3, 4], jnp.int32) + z
    order = order % ZN
    occ_c = jnp.take(occ_z, (order % 2) * (ZN // 2) + order // 2, axis=0).astype(jnp.float32)
    w_col = (occ_c * occ_c).astype(jnp.bfloat16).reshape(ZN * points, -1)

    part = lax.dot_general(
        kern, w_col, (((0,), (0,)), ((), ())), preferred_element_type=jnp.float32
    ) / math.sqrt(NGRID)
    part = part.reshape(4, 2, sub, -1)
    gx = (jnp.arange(4, dtype=jnp.int32) - xi) % 4
    part = jnp.take(part, gx, axis=0)
    part = jnp.where(core == 0, part, part[:, ::-1])
    part = part.reshape(8, sub, -1)
    local = jnp.sum(
        w_row.astype(jnp.float32).reshape(8 * sub, -1) * part.reshape(8 * sub, -1), axis=0
    ) / math.sqrt(NGRID)
    send = jnp.concatenate([part, jnp.broadcast_to(local, (8, 8, local.shape[0]))], axis=1)
    got = lax.all_to_all(send, ("x", "c"), 0, 0, tiled=True)
    pair_field = got[:, :sub].sum(0)
    energy = got[:, sub].sum(0)
    energy = lax.all_to_all(
        jnp.broadcast_to(energy, (32, 1, energy.shape[0])), ("l", "h", "y"), 0, 0, tiled=True
    ).sum((0, 1))
    return pair_field, energy


def solution(mesh):
    fine = Mesh(mesh.devices.reshape(4, 2, 2, 4, 4), ("x", "l", "c", "h", "y"))
    grid = ("x", "l", "c", "h")
    in_specs = (P(grid, "y"), P(grid, "y"), P(grid, "y"), P(grid, None))
    out_specs = (P(grid + ("y",), None), P())
    return jax.shard_map(shards, mesh=fine, in_specs=in_specs, out_specs=out_specs, check_vma=False)
```

time: 548 us -> 260 us (0.47)
  waiting for transfers between devices: 396 us -> 57.3 us
  starting transfers between devices: 0.27 us -> 55.7 us
  blocking collectives: 115 us -> 75.9 us
  local copies, waits for them, and re-layouts: 1.18 us -> 31.2 us
  matrix products: 17.9 us -> 32.1 us
  between operations: 14.2 us -> 1.4 us
    all_gather x5 -> x0, waiting for transfers between devices: 250 us -> none  [the longest x1 65.2 us: shards(): piece_gem = lax.all_gather(by_quarter(geminal), 'row', axis=1, tiled=True)]
    reduce_scatter x1 -> x0, waiting for transfers between devices: 84.7 us -> none  [shards(): lax.psum_scatter(partial_field, ('col', 'aux'), scatter_dimension=0, tile...]
    psum x1 -> x0, blocking collectives: 75.6 us -> none  [shards(): energy = lax.psum(local_energy, ('row', 'col', 'aux'))]
    unnamed x8 -> x0, waiting for transfers between devices: 62.2 us -> none
    ppermute x0 -> x17, waiting for transfers between devices: none -> 38.9 us  [the longest x8 37.4 us: shift_z(): lax.ppermute(v, ('l', 'h'), [(z_slot(z), z_slot((z + d) % ZN)) for z in r...]
    ppermute x0 -> x17, starting transfers between devices: none -> 28.4 us  [the longest x5 13.3 us: swap_core(): return lax.ppermute(v, 'c', [(0, 1), (1, 0)])]
    all_to_all x0 -> x6, starting transfers between devices: none -> 27.2 us  [the longest x5 20.8 us: gram(): s = lax.all_to_all(t, 'y', 0, 0, tiled=True).sum(0)]
    all_gather x2, blocking collectives: 39.5 us -> 62.5 us  [the longest x1 48.1 us: shards(): occ_z = lax.all_gather(occupied, ('l', 'h'), axis=0, tiled=False)]
  transfers between devices with their start and end apart: 7 -> 23, of which waited for: 7 -> 9; matrix products, arithmetic and copies ran while one was open for 2% -> 23% of each run, Pallas kernels for 0% -> 0%
where the time goes in v1:
time: 260 us
  blocking collectives  75.9 us (29%)
  waiting for transfers between devices  57.3 us (22%)
  starting transfers between devices  55.7 us (21%)
  matrix products  32.1 us (12%)
  local copies, waits for them, and re-layouts  31.2 us (12%)
  other arithmetic  6.13 us (2%)
    all_gather x1, blocking collectives, shards(): occ_z = lax.all_gather(occupied, ('l', 'h'), axis=0, tiled=False)  48.1 us
    ppermute x8, waiting for transfers between devices, shift_z(): lax.ppermute(v, ('l', 'h'), [(z_slot(z), z_slot((z + d) % ZN)) for z in r...  37.4 us
    all_to_all x5, starting transfers between devices, gram(): s = lax.all_to_all(t, 'y', 0, 0, tiled=True).sum(0)  20.8 us
    dot_general x5, matrix products, gram(): jnp.einsum('qk,ypk->yqp', cg, row_g, preferred_element_type=jnp.float32)  14.7 us
    all_gather x1, blocking collectives, shards(): lax.all_gather(own_occ, ('x', 'c'), axis=0, tiled=True).astype(jnp.float32)  14.4 us
    all_to_all x1, blocking collectives, shards(): got = lax.all_to_all(send, ('x', 'c'), 0, 0, tiled=True)  13.4 us
    ppermute x5, starting transfers between devices, swap_core(): return lax.ppermute(v, 'c', [(0, 1), (1, 0)])  13.3 us
    squeeze x6, local copies, waits for them, and re-layouts, pair(): return (jnp.concatenate([a[0], b[0]]), jnp.concatenate([a[1], b[1]]))  12.7 us
  transfers between devices with their start and end apart: 23, of which 9 were waited for; matrix products, arithmetic and copies ran while one was open for 23% of the time, Pallas kernels for 0%

profile of v1, /device:TPU:1, one launch (start us, length us, event | category | flops | bytes accessed | tf_op | source)
XLA Modules:
  0.0 259.6 jit_solution(6284915284560045183)
XLA Ops:
  0.6 1.1 constant_dynamic-update-slice_fusion.1
  1.8 0.9 constant_dynamic-update-slice_fusion
  2.7 2.3 pad_maximum_fusion
  5.0 3.2 %collective-permute-start = (bf16[2,64,5120]{2,1,0:T(8,128)(2,1)}, bf16[2,64,5120]{2,1,0:T(8,128)(2,1)}, u32[]{:S(2)}, u32[]{:S(2)}) collective-permute-start(bf16[2,64,5120]{2,1,0:T(8,128)(2,1)} %pad_maximum_fusion), channel_id=1, source_target_pairs={{0,16},{16,0},{1,17},{17,1},{2,18},{18,2},{3,19},{19,3},{4,20},{20... | collective-permute-start | bytes 3932168 | tf_op jit(solution)/shard_map/ppermute | solution.py:29
  8.2 0.7 collective-permute-start.1
  9.0 0.7 collective-permute-start.3
  9.7 4.9 %collective-permute-start.10 = (bf16[2,64,5120]{2,1,0:T(8,128)(2,1)}, bf16[2,64,5120]{2,1,0:T(8,128)(2,1)}, u32[]{:S(2)}, u32[]{:S(2)}) collective-permute-start(bf16[2,64,5120]{2,1,0:T(8,128)(2,1)} %pad_maximum_fusion), channel_id=1, source_target_pairs={{0,44},{32,0},{4,32},{36,4},{8,36},{40,8},{12,40},{44,12},{1,45},{... | collective-permute-start | bytes 3932168 | tf_op jit(solution)/shard_map/ppermute | solution.py:21
  15.1 48.1 %all-gather = bf16[512,256]{1,0:T(8,128)(2,1)S(1)} all-gather(bf16[64,256]{1,0:T(8,128)(2,1)} %param.8), channel_id=2, replica_groups=mesh['x'=4,'l'=2,'c'=2,'h'=4,'y'=4] {'l','h'}, dimensions={0}, use_global_device_ids=true | all-gather | bytes 294912 | tf_op jit(solution)/shard_map/all_gather | solution.py:42
  63.2 0.7 compare_and_fusion
  63.9 0.9 constant_dynamic-update-slice_fusion.17
  64.9 0.9 constant_dynamic-update-slice_fusion.9
  67.5 0.9 constant_dynamic-slice_fusion
  68.3 1.7 fusion.110
  70.0 1.9 collective-permute-start.7
  72.2 1.5 fusion.111
  73.9 7.7 %collective-permute-start.2 = (bf16[2,64,5120]{2,1,0:T(8,128)(2,1)}, bf16[2,64,5120]{2,1,0:T(8,128)(2,1)S(1)}, u32[]{:S(2)}, u32[]{:S(2)}) collective-permute-start(bf16[2,64,5120]{2,1,0:T(8,128)(2,1)} %collective-permute-done.1), channel_id=1, source_target_pairs={{0,16},{16,0},{1,17},{17,1},{2,18},{18,2},{3,19},{19,3},{4,20},{20... | collective-permute-start | bytes 3932168 | tf_op jit(solution)/shard_map/ppermute | solution.py:29
  81.8 2.2 slice_bitcast_fusion.10
  84.0 2.2 slice_bitcast_fusion.11
  86.9 2.8 %collective-permute-start.11 = (bf16[2,64,5120]{2,1,0:T(8,128)(2,1)}, bf16[2,64,5120]{2,1,0:T(8,128)(2,1)}, u32[]{:S(2)}, u32[]{:S(2)}) collective-permute-start(bf16[2,64,5120]{2,1,0:T(8,128)(2,1)} %collective-permute-done.9), channel_id=1, source_target_pairs={{0,32},{32,4},{4,36},{36,8},{8,40},{40,12},{12,44},{44,0},{1,33},{... | collective-permute-start | bytes 3932168 | tf_op jit(solution)/shard_map/ppermute | solution.py:21
  89.7 1.9 collective-permute-start.8
  91.8 1.5 collective-permute-done.8
  93.6 1.4 fusion.31
  95.8 2.3 copy-done
  98.1 1.7 convolution_bitcast_fusion.6
  99.9 0.8 copy.35
  100.6 4.2 %all-to-all-start = ((f32[4,3,64,128]{3,2,1,0:T(8,128)}), f32[4,3,64,128]{3,2,1,0:T(8,128)S(1)}, u32[]{:S(2)}, u32[]{:S(2)}) async-start(f32[4,3,64,128]{3,2,1,0:T(8,128)} %copy.35), calls=%async_computation | async-start | bytes 786432 | tf_op jit(solution)/shard_map/all_to_all | solution.py:72
  104.8 1.8 convolution_bitcast_fusion.2
  106.7 3.6 %fusion.22 = f32[4,1,128,128]{2,3,0,1:T(8,128)S(1)} fusion(bf16[4,128,5120]{2,1,0:T(8,128)(2,1)} %copy-done.3, bf16[64,5120]{1,0:T(8,128)(2,1)S(1)} %get-tuple-element.13, bf16[64,5120]{1,0:T(8,128)(2,1)S(1)} %get-tuple-element.15), kind=kOutput, calls=%fused_computation.34 | convolution fusion | flops 538968064 | bytes 5767168 | tf_op jit(solution)/shard_map/qk,ypk->yqp/dot_general | solution.py:67
  110.3 1.5 fusion.21
  111.9 1.0 copy.36
  112.9 1.2 collective-permute-done.12
  114.1 2.2 slice_bitcast_fusion.6
  116.4 3.4 %collective-permute-done.11 = bf16[2,64,5120]{2,1,0:T(8,128)(2,1)} collective-permute-done((bf16[2,64,5120]{2,1,0:T(8,128)(2,1)}, bf16[2,64,5120]{2,1,0:T(8,128)(2,1)}, u32[]{:S(2)}, u32[]{:S(2)}) %collective-permute-start.11) | collective-permute-done | bytes 1310752 | tf_op jit(solution)/shard_map/ppermute | solution.py:21
  119.8 2.2 slice_bitcast_fusion.7
  122.1 1.3 fusion.25
  123.3 4.2 %all-to-all-start.1 = ((f32[4,3,128,128]{2,3,1,0:T(8,128)}), f32[4,3,128,128]{2,3,1,0:T(8,128)S(1)}, u32[]{:S(2)}, u32[]{:S(2)}) async-start(f32[4,3,128,128]{2,3,1,0:T(8,128)} %copy.36), calls=%async_computation.1 | async-start | bytes 1572864 | tf_op jit(solution)/shard_map/all_to_all | solution.py:72
  127.5 1.7 convolution_bitcast_fusion.1
  129.3 4.4 %fusion.20 = f32[4,1,128,128]{2,3,0,1:T(8,128)S(1)} fusion(bf16[4,128,5120]{2,1,0:T(8,128)(2,1)} %copy-done, bf16[64,5120]{1,0:T(8,128)(2,1)} %get-tuple-element.10, bf16[64,5120]{1,0:T(8,128)(2,1)} %get-tuple-element.8), kind=kOutput, calls=%fused_computation.32 | convolution fusion | flops 673710080 | bytes 6815744 | tf_op jit(solution)/shard_map/qk,ypk->yqp/dot_general | solution.py:66
  133.7 0.9 copy.38
  134.7 4.2 %all-to-all-done.1 = f32[4,3,128,128]{2,3,1,0:T(8,128)S(1)} async-done(((f32[4,3,128,128]{2,3,1,0:T(8,128)}), f32[4,3,128,128]{2,3,1,0:T(8,128)S(1)}, u32[]{:S(2)}, u32[]{:S(2)}) %all-to-all-start.1) | async-done | bytes 786464 | tf_op jit(solution)/shard_map/all_to_all | solution.py:72
  138.9 3.5 %all-to-all-start.2 = ((f32[4,3,128,128]{2,3,1,0:T(8,128)}), f32[4,3,128,128]{2,3,1,0:T(8,128)S(1)}, u32[]{:S(2)}, u32[]{:S(2)}) async-start(f32[4,3,128,128]{2,3,1,0:T(8,128)} %copy.38), calls=%async_computation.2 | async-start | bytes 1572864 | tf_op jit(solution)/shard_map/all_to_all | solution.py:72
  142.4 14.4 %all_gather.11 = bf16[128,256]{1,0:T(8,128)(2,1)S(1)} all-gather(bf16[16,256]{1,0:T(8,128)(2,1)S(1)} %constant_dynamic-slice_fusion), channel_id=1, replica_groups=mesh['x'=4,'l'=2,'c'=2,'h'=4,'y'=4] {'x','c'}, dimensions={0}, use_global_device_ids=true | all-gather | bytes 73728 | tf_op jit(solution)/shard_map/all_gather | solution.py:44
  157.0 1.2 collective-permute-start.14
  158.5 1.6 collective-permute-done.13
  160.1 2.2 slice_bitcast_fusion.3
  162.4 25.2 %collective-permute-done.14 = bf16[2,64,5120]{2,1,0:T(8,128)(2,1)} collective-permute-done((bf16[2,64,5120]{2,1,0:T(8,128)(2,1)}, bf16[2,64,5120]{2,1,0:T(8,128)(2,1)}, u32[]{:S(2)}, u32[]{:S(2)}) %collective-permute-start.14) | collective-permute-done | bytes 1310752 | tf_op jit(solution)/shard_map/ppermute | solution.py:21
  187.6 1.5 slice_bitcast_fusion.2
  189.1 4.3 %fusion.19 = f32[4,1,128,128]{2,3,0,1:T(8,128)S(1)} fusion(bf16[4,128,5120]{2,1,0:T(8,128)(2,1)} %copy-done, bf16[64,5120]{1,0:T(8,128)(2,1)S(1)} %get-tuple-element.6, bf16[64,5120]{1,0:T(8,128)(2,1)} %get-tuple-element.4), kind=kOutput, calls=%fused_computation.31 | convolution fusion | flops 673710080 | bytes 6815744 | tf_op jit(solution)/shard_map/qk,ypk->yqp/dot_general | solution.py:66
  193.4 2.4 collective-permute-start.16
  196.3 1.3 fusion.28
  197.6 0.9 copy.40
  198.6 4.5 %all-to-all-start.3 = ((f32[4,3,128,128]{2,3,1,0:T(8,128)}), f32[4,3,128,128]{2,3,1,0:T(8,128)S(1)}, u32[]{:S(2)}, u32[]{:S(2)}) async-start(f32[4,3,128,128]{2,3,1,0:T(8,128)} %copy.40), calls=%async_computation.3 | async-start | bytes 1572864 | tf_op jit(solution)/shard_map/all_to_all | solution.py:72
  203.0 5.9 %collective-permute-done.16 = bf16[64,5120]{1,0:T(8,128)(2,1)} collective-permute-done((bf16[64,5120]{1,0:T(8,128)(2,1)S(1)}, bf16[64,5120]{1,0:T(8,128)(2,1)}, u32[]{:S(2)}, u32[]{:S(2)}) %collective-permute-start.16) | collective-permute-done | bytes 655392 | tf_op jit(solution)/shard_map/ppermute | solution.py:21
  208.9 3.7 %fusion.34 = f32[4,1,64,128]{3,2,0,1:T(8,128)S(1)} fusion(bf16[4,128,5120]{2,1,0:T(8,128)(2,1)} %copy-done.3, bf16[64,5120]{1,0:T(8,128)(2,1)} %collective-permute-done.16), kind=kOutput, calls=%fused_computation.41 | convolution fusion | flops 268435456 | bytes 4849664 | tf_op jit(solution)/shard_map/qk,ypk->yqp/dot_general | solution.py:67
  212.6 1.7 convolution_bitcast_fusion.3
  214.3 2.8 %convolution_bitcast_fusion.5 = f32[4,1,64,128]{3,2,0,1:T(8,128)S(1)} fusion(bf16[4,128,5120]{2,1,0:T(8,128)(2,1)S(1)} %bitcast.193, bf16[64,5120]{1,0:T(8,128)(2,1)} %collective-permute-done.15), kind=kOutput, calls=%fused_computation.45 | convolution fusion | flops 335544320 | bytes 6029312 | tf_op jit(solution)/shard_map/qk,ypk->yqp/dot_general | solution.py:66
  217.1 0.8 copy.42
  217.9 4.5 %all-to-all-start.4 = ((f32[4,3,64,128]{3,2,1,0:T(8,128)}), f32[4,3,64,128]{3,2,1,0:T(8,128)S(1)}, u32[]{:S(2)}, u32[]{:S(2)}) async-start(f32[4,3,64,128]{3,2,1,0:T(8,128)} %copy.42), calls=%async_computation.4 | async-start | bytes 786432 | tf_op jit(solution)/shard_map/all_to_all | solution.py:72
  222.5 6.1 %all-to-all-done.4 = f32[4,3,64,128]{3,2,1,0:T(8,128)S(1)} async-done(((f32[4,3,64,128]{3,2,1,0:T(8,128)}), f32[4,3,64,128]{3,2,1,0:T(8,128)S(1)}, u32[]{:S(2)}, u32[]{:S(2)}) %all-to-all-start.4) | async-done | bytes 393248 | tf_op jit(solution)/shard_map/all_to_all | solution.py:72
  229.9 13.4 %all_to_all.35 = f32[8,24,256]{2,1,0:T(8,128)S(1)} all-to-all(f32[8,24,256]{2,1,0:T(8,128)S(1)} %pad_maximum_fusion.9), channel_id=1, replica_groups=mesh['x'=4,'l'=2,'c'=2,'h'=4,'y'=4] {'x','c'}, dimensions={0} | all-to-all | bytes 393216 | tf_op jit(solution)/shard_map/all_to_all | solution.py:106
  243.3 0.6 broadcast_in_dim.45
  243.9 6.4 %all-to-all-start.6 = ((f32[32,1,256]{2,1,0:T(1,128)}), f32[32,1,256]{2,1,0:T(1,128)S(1)}, u32[]{:S(2)}, u32[]{:S(2)}) async-start(f32[32,1,256]{2,1,0:T(1,128)} %broadcast_in_dim.45), calls=%async_computation.6 | async-start | bytes 65536 | tf_op jit(solution)/shard_map/all_to_all | solution.py:109
  250.4 0.6 slice_reduce_fusion
  251.0 8.0 %all-to-all-done.6 = f32[32,1,256]{2,1,0:T(1,128)S(1)} async-done(((f32[32,1,256]{2,1,0:T(1,128)}), f32[32,1,256]{2,1,0:T(1,128)S(1)}, u32[]{:S(2)}, u32[]{:S(2)}) %all-to-all-start.6) | async-done | bytes 32800 | tf_op jit(solution)/shard_map/all_to_all | solution.py:109
  (124 shorter events, 7.8 us)
Async XLA Ops:
  0.6 64.2 %copy-start.1 = (bf16[64,5120]{1,0:T(8,128)(2,1)S(1)}, bf16[64,5120]{1,0:T(8,128)(2,1)}, u32[]{:S(2)}) copy-start(bf16[64,5120]{1,0:T(8,128)(2,1)} %param.7) | copy-start | bytes 1966084
  5.0 67.3 %collective-permute-start = (bf16[2,64,5120]{2,1,0:T(8,128)(2,1)}, bf16[2,64,5120]{2,1,0:T(8,128)(2,1)}, u32[]{:S(2)}, u32[]{:S(2)}) collective-permute-start(bf16[2,64,5120]{2,1,0:T(8,128)(2,1)} %pad_maximum_fusion), channel_id=1, source_target_pairs={{0,16},{16,0},{1,17},{17,1},{2,18},{18,2},{3,19},{19,3},{4,20},{20... | collective-permute-start | bytes 3932168 | tf_op jit(solution)/shard_map/ppermute | solution.py:29
  8.2 60.1 %collective-permute-start.1 = (bf16[2,64,5120]{2,1,0:T(8,128)(2,1)}, bf16[2,64,5120]{2,1,0:T(8,128)(2,1)}, u32[]{:S(2)}, u32[]{:S(2)}) collective-permute-start(bf16[2,64,5120]{2,1,0:T(8,128)(2,1)} %pad_maximum_fusion), channel_id=1, source_target_pairs={{0,192},{64,0},{128,64},{192,128},{1,193},{65,1},{129,65},{193,129... | collective-permute-start | bytes 3932168 | tf_op jit(solution)/shard_map/ppermute | solution.py:25
  9.0 63.0 %collective-permute-start.3 = (bf16[2,64,5120]{2,1,0:T(8,128)(2,1)}, bf16[2,64,5120]{2,1,0:T(8,128)(2,1)S(1)}, u32[]{:S(2)}, u32[]{:S(2)}) collective-permute-start(bf16[2,64,5120]{2,1,0:T(8,128)(2,1)} %pad_maximum_fusion), channel_id=1, source_target_pairs={{0,64},{64,128},{128,192},{192,0},{1,65},{65,129},{129,193},{193,1... | collective-permute-start | bytes 3932168 | tf_op jit(solution)/shard_map/ppermute | solution.py:25
  9.7 71.9 %collective-permute-start.10 = (bf16[2,64,5120]{2,1,0:T(8,128)(2,1)}, bf16[2,64,5120]{2,1,0:T(8,128)(2,1)}, u32[]{:S(2)}, u32[]{:S(2)}) collective-permute-start(bf16[2,64,5120]{2,1,0:T(8,128)(2,1)} %pad_maximum_fusion), channel_id=1, source_target_pairs={{0,44},{32,0},{4,32},{36,4},{8,36},{40,8},{12,40},{44,12},{1,45},{... | collective-permute-start | bytes 3932168 | tf_op jit(solution)/shard_map/ppermute | solution.py:21
  14.5 69.5 %collective-permute-start.9 = (bf16[2,64,5120]{2,1,0:T(8,128)(2,1)}, bf16[2,64,5120]{2,1,0:T(8,128)(2,1)}, u32[]{:S(2)}, u32[]{:S(2)}) collective-permute-start(bf16[2,64,5120]{2,1,0:T(8,128)(2,1)} %pad_maximum_fusion), channel_id=1, source_target_pairs={{0,32},{32,4},{4,36},{36,8},{8,40},{40,12},{12,44},{44,0},{1,33},{... | collective-permute-start | bytes 3932168 | tf_op jit(solution)/shard_map/ppermute | solution.py:21
  67.5 6.3 %copy-start.2 = (bf16[4,128,5120]{2,1,0:T(8,128)(2,1)S(1)}, bf16[4,128,5120]{2,1,0:T(8,128)(2,1)}, u32[]{:S(2)}) copy-start(bf16[4,128,5120]{2,1,0:T(8,128)(2,1)} %constant_dynamic-update-slice_fusion.17) | copy-start | bytes 15728644
  70.0 16.8 %collective-permute-start.7 = (bf16[64,5120]{1,0:T(8,128)(2,1)S(1)}, bf16[64,5120]{1,0:T(8,128)(2,1)S(1)}, u32[]{:S(2)}, u32[]{:S(2)}) collective-permute-start(bf16[64,5120]{1,0:T(8,128)(2,1)S(1)} %get-tuple-element.24), channel_id=1, source_target_pairs={{0,192},{64,0},{128,64},{192,128},{1,193},{65,1},{129,65},{193,129... | collective-permute-start | bytes 1966088 | tf_op jit(solution)/shard_map/ppermute | solution.py:25
  71.9 14.4 %slice-start = ((s8[5242880]{0:T(1024)(128)(4,1)}), s8[4194304]{0:T(1024)(128)(4,1)S(1)}, s32[]{:S(2)}) async-start(s8[5242880]{0:T(1024)(128)(4,1)} %bitcast.188), calls=%async_computation.7 | async-start | bytes 8388608
  72.1 17.6 %collective-permute-start.4 = (bf16[64,5120]{1,0:T(8,128)(2,1)S(1)}, bf16[64,5120]{1,0:T(8,128)(2,1)S(1)}, u32[]{:S(2)}, u32[]{:S(2)}) collective-permute-start(bf16[64,5120]{1,0:T(8,128)(2,1)S(1)} %get-tuple-element.19), channel_id=1, source_target_pairs={{0,64},{64,128},{128,192},{192,0},{1,65},{65,129},{129,193},{193,1... | collective-permute-start | bytes 1966088 | tf_op jit(solution)/shard_map/ppermute | solution.py:25
  73.8 12.5 %slice-start.1 = ((s8[5242880]{0:T(1024)(128)(4,1)}), s8[1048576]{0:T(1024)(128)(4,1)S(1)}, s32[]{:S(2)}) async-start(s8[5242880]{0:T(1024)(128)(4,1)} %bitcast.188), calls=%async_computation.8 | async-start | bytes 2097152
  73.9 17.8 %collective-permute-start.2 = (bf16[2,64,5120]{2,1,0:T(8,128)(2,1)}, bf16[2,64,5120]{2,1,0:T(8,128)(2,1)S(1)}, u32[]{:S(2)}, u32[]{:S(2)}) collective-permute-start(bf16[2,64,5120]{2,1,0:T(8,128)(2,1)} %collective-permute-done.1), channel_id=1, source_target_pairs={{0,16},{16,0},{1,17},{17,1},{2,18},{18,2},{3,19},{19,3},{4,20},{20... | collective-permute-start | bytes 3932168 | tf_op jit(solution)/shard_map/ppermute | solution.py:29
  81.6 32.6 %collective-permute-start.12 = (bf16[2,64,5120]{2,1,0:T(8,128)(2,1)}, bf16[2,64,5120]{2,1,0:T(8,128)(2,1)}, u32[]{:S(2)}, u32[]{:S(2)}) collective-permute-start(bf16[2,64,5120]{2,1,0:T(8,128)(2,1)} %collective-permute-done.10), channel_id=1, source_target_pairs={{0,44},{32,0},{4,32},{36,4},{8,36},{40,8},{12,40},{44,12},{1,45},{... | collective-permute-start | bytes 3932168 | tf_op jit(solution)/shard_map/ppermute | solution.py:21
  86.4 7.1 %collective-permute-start.6 = (bf16[2,64,5120]{2,1,0:T(8,128)(2,1)S(1)}, bf16[2,64,5120]{2,1,0:T(8,128)(2,1)S(1)}, u32[]{:S(2)}, u32[]{:S(2)}) collective-permute-start(bf16[2,64,5120]{2,1,0:T(8,128)(2,1)S(1)} %collective-permute-done.3), channel_id=1, source_target_pairs={{0,16},{16,0},{1,17},{17,1},{2,18},{18,2},{3,19},{19,3},{4,20},{20... | collective-permute-start | bytes 3932168 | tf_op jit(solution)/shard_map/ppermute | solution.py:29
  86.9 32.9 %collective-permute-start.11 = (bf16[2,64,5120]{2,1,0:T(8,128)(2,1)}, bf16[2,64,5120]{2,1,0:T(8,128)(2,1)}, u32[]{:S(2)}, u32[]{:S(2)}) collective-permute-start(bf16[2,64,5120]{2,1,0:T(8,128)(2,1)} %collective-permute-done.9), channel_id=1, source_target_pairs={{0,32},{32,4},{4,36},{36,8},{8,40},{40,12},{12,44},{44,0},{1,33},{... | collective-permute-start | bytes 3932168 | tf_op jit(solution)/shard_map/ppermute | solution.py:21
  89.7 3.6 %collective-permute-start.8 = (bf16[64,5120]{1,0:T(8,128)(2,1)S(1)}, bf16[64,5120]{1,0:T(8,128)(2,1)S(1)}, u32[]{:S(2)}, u32[]{:S(2)}) collective-permute-start(bf16[64,5120]{1,0:T(8,128)(2,1)S(1)} %collective-permute-done.7), channel_id=1, source_target_pairs={{0,16},{16,0},{1,17},{17,1},{2,18},{18,2},{3,19},{19,3},{4,20},{20... | collective-permute-start | bytes 1966088 | tf_op jit(solution)/shard_map/ppermute | solution.py:29
  91.6 4.0 %collective-permute-start.5 = (bf16[64,5120]{1,0:T(8,128)(2,1)S(1)}, bf16[64,5120]{1,0:T(8,128)(2,1)S(1)}, u32[]{:S(2)}, u32[]{:S(2)}) collective-permute-start(bf16[64,5120]{1,0:T(8,128)(2,1)S(1)} %collective-permute-done.4), channel_id=1, source_target_pairs={{0,16},{16,0},{1,17},{17,1},{2,18},{18,2},{3,19},{19,3},{4,20},{20... | collective-permute-start | bytes 1966088 | tf_op jit(solution)/shard_map/ppermute | solution.py:29
  91.7 1.9 copy-start.6
  93.5 1.6 copy-start.7
  93.6 6.2 %copy-start.3 = (bf16[4,128,5120]{2,1,0:T(8,128)(2,1)}, bf16[4,128,5120]{2,1,0:T(8,128)(2,1)S(1)}, u32[]{:S(2)}) copy-start(bf16[4,128,5120]{2,1,0:T(8,128)(2,1)S(1)} %constant_dynamic-update-slice_fusion.10) | copy-start | bytes 15728644
  95.8 2.3 copy-start
  100.6 22.7 %all-to-all-start = ((f32[4,3,64,128]{3,2,1,0:T(8,128)}), f32[4,3,64,128]{3,2,1,0:T(8,128)S(1)}, u32[]{:S(2)}, u32[]{:S(2)}) async-start(f32[4,3,64,128]{3,2,1,0:T(8,128)} %copy.35), calls=%async_computation | async-start | bytes 786432 | tf_op jit(solution)/shard_map/all_to_all | solution.py:72
  104.8 5.5 %slice-start.2 = ((s8[5242880]{0:T(1024)(128)(4,1)}), s8[4194304]{0:T(1024)(128)(4,1)S(1)}, s32[]{:S(2)}) async-start(s8[5242880]{0:T(1024)(128)(4,1)} %bitcast.190), calls=%async_computation.9 | async-start | bytes 8388608
  106.6 3.6 %slice-start.3 = ((s8[5242880]{0:T(1024)(128)(4,1)}), s8[1048576]{0:T(1024)(128)(4,1)S(1)}, s32[]{:S(2)}) async-start(s8[5242880]{0:T(1024)(128)(4,1)} %bitcast.190), calls=%async_computation.10 | async-start | bytes 2097152
  106.7 3.6 %copy-start.4 = (bf16[64,5120]{1,0:T(8,128)(2,1)S(1)}, bf16[64,5120]{1,0:T(8,128)(2,1)}, u32[]{:S(2)}) copy-start(bf16[64,5120]{1,0:T(8,128)(2,1)} %get-tuple-element.14) | copy-start | bytes 1966084
  106.7 3.6 %copy-start.5 = (bf16[64,5120]{1,0:T(8,128)(2,1)S(1)}, bf16[64,5120]{1,0:T(8,128)(2,1)}, u32[]{:S(2)}) copy-start(bf16[64,5120]{1,0:T(8,128)(2,1)} %get-tuple-element.12) | copy-start | bytes 1966084
  110.3 11.8 %slice-start.6 = ((s8[5242880]{0:T(1024)(128)(4,1)}), s8[4194304]{0:T(1024)(128)(4,1)S(1)}, s32[]{:S(2)}) async-start(s8[5242880]{0:T(1024)(128)(4,1)} %bitcast.198), calls=%async_computation.13 | async-start | bytes 8388608
  110.3 11.7 %slice-start.7 = ((s8[5242880]{0:T(1024)(128)(4,1)}), s8[1048576]{0:T(1024)(128)(4,1)S(1)}, s32[]{:S(2)}) async-start(s8[5242880]{0:T(1024)(128)(4,1)} %bitcast.198), calls=%async_computation.14 | async-start | bytes 2097152
  123.3 15.6 %all-to-all-start.1 = ((f32[4,3,128,128]{2,3,1,0:T(8,128)}), f32[4,3,128,128]{2,3,1,0:T(8,128)S(1)}, u32[]{:S(2)}, u32[]{:S(2)}) async-start(f32[4,3,128,128]{2,3,1,0:T(8,128)} %copy.36), calls=%async_computation.1 | async-start | bytes 1572864 | tf_op jit(solution)/shard_map/all_to_all | solution.py:72
  129.2 30.9 %collective-permute-start.13 = (bf16[2,64,5120]{2,1,0:T(8,128)(2,1)}, bf16[2,64,5120]{2,1,0:T(8,128)(2,1)}, u32[]{:S(2)}, u32[]{:S(2)}) collective-permute-start(bf16[2,64,5120]{2,1,0:T(8,128)(2,1)} %collective-permute-done.11), channel_id=1, source_target_pairs={{0,32},{32,4},{4,36},{36,8},{8,40},{40,12},{12,44},{44,0},{1,33},{... | collective-permute-start | bytes 3932168 | tf_op jit(solution)/shard_map/ppermute | solution.py:21
  129.3 27.5 %copy-start.10 = (s32[4]{0:T(128)S(1)}, s32[4]{0:T(128)}, u32[]{:S(2)}) copy-start(s32[4]{0:T(128)} %fusion.97) | copy-start | bytes 52
  129.3 27.6 %copy-start.9 = (pred[512]{0:T(512)(128)(4,1)S(1)}, pred[512]{0:T(512)(128)(4,1)}, u32[]{:S(2)}) copy-start(pred[512]{0:T(512)(128)(4,1)} %broadcast_in_dim.39) | copy-start | bytes 1540
  133.7 24.6 %copy-start.8 = (s32[128]{0:T(128)S(1)}, s32[128]{0:T(128)}, u32[]{:S(2)}) copy-start(s32[128]{0:T(128)} %iota_add_fusion) | copy-start | bytes 1540
  138.9 19.5 %all-to-all-start.2 = ((f32[4,3,128,128]{2,3,1,0:T(8,128)}), f32[4,3,128,128]{2,3,1,0:T(8,128)S(1)}, u32[]{:S(2)}, u32[]{:S(2)}) async-start(f32[4,3,128,128]{2,3,1,0:T(8,128)} %copy.38), calls=%async_computation.2 | async-start | bytes 1572864 | tf_op jit(solution)/shard_map/all_to_all | solution.py:72
  157.0 30.6 %collective-permute-start.14 = (bf16[2,64,5120]{2,1,0:T(8,128)(2,1)}, bf16[2,64,5120]{2,1,0:T(8,128)(2,1)}, u32[]{:S(2)}, u32[]{:S(2)}) collective-permute-start(bf16[2,64,5120]{2,1,0:T(8,128)(2,1)} %collective-permute-done.12), channel_id=1, source_target_pairs={{0,44},{32,0},{4,32},{36,4},{8,36},{40,8},{12,40},{44,12},{1,45},{... | collective-permute-start | bytes 3932168 | tf_op jit(solution)/shard_map/ppermute | solution.py:21
  162.4 51.9 %collective-permute-start.15 = (bf16[64,5120]{1,0:T(8,128)(2,1)}, bf16[64,5120]{1,0:T(8,128)(2,1)}, u32[]{:S(2)}, u32[]{:S(2)}) collective-permute-start(bf16[64,5120]{1,0:T(8,128)(2,1)} %get-tuple-element.4), channel_id=1, source_target_pairs={{0,32},{32,4},{4,36},{36,8},{8,40},{40,12},{12,44},{44,0},{1,33},{... | collective-permute-start | bytes 1966088 | tf_op jit(solution)/shard_map/ppermute | solution.py:21
  187.6 8.3 %slice-start.8 = ((s8[5242880]{0:T(1024)(128)(4,1)}), s8[4194304]{0:T(1024)(128)(4,1)S(1)}, s32[]{:S(2)}) async-start(s8[5242880]{0:T(1024)(128)(4,1)} %bitcast.200), calls=%async_computation.15 | async-start | bytes 8388608
  189.1 6.7 %slice-start.9 = ((s8[5242880]{0:T(1024)(128)(4,1)}), s8[1048576]{0:T(1024)(128)(4,1)S(1)}, s32[]{:S(2)}) async-start(s8[5242880]{0:T(1024)(128)(4,1)} %bitcast.200), calls=%async_computation.16 | async-start | bytes 2097152
  193.4 15.5 %collective-permute-start.16 = (bf16[64,5120]{1,0:T(8,128)(2,1)S(1)}, bf16[64,5120]{1,0:T(8,128)(2,1)}, u32[]{:S(2)}, u32[]{:S(2)}) collective-permute-start(bf16[64,5120]{1,0:T(8,128)(2,1)S(1)} %get-tuple-element.7), channel_id=1, source_target_pairs={{0,44},{32,0},{4,32},{36,4},{8,36},{40,8},{12,40},{44,12},{1,45},{... | collective-permute-start | bytes 1966088 | tf_op jit(solution)/shard_map/ppermute | solution.py:21
  197.6 16.6 %slice-start.4 = ((s8[5242880]{0:T(1024)(128)(4,1)}), s8[1048576]{0:T(1024)(128)(4,1)S(1)}, s32[]{:S(2)}) async-start(s8[5242880]{0:T(1024)(128)(4,1)} %bitcast.192), calls=%async_computation.11 | async-start | bytes 2097152
  198.6 19.4 %all-to-all-start.3 = ((f32[4,3,128,128]{2,3,1,0:T(8,128)}), f32[4,3,128,128]{2,3,1,0:T(8,128)S(1)}, u32[]{:S(2)}, u32[]{:S(2)}) async-start(f32[4,3,128,128]{2,3,1,0:T(8,128)} %copy.40), calls=%async_computation.3 | async-start | bytes 1572864 | tf_op jit(solution)/shard_map/all_to_all | solution.py:72
  203.0 11.3 %slice-start.5 = ((s8[5242880]{0:T(1024)(128)(4,1)}), s8[4194304]{0:T(1024)(128)(4,1)S(1)}, s32[]{:S(2)}) async-start(s8[5242880]{0:T(1024)(128)(4,1)} %bitcast.192), calls=%async_computation.12 | async-start | bytes 8388608
  217.9 10.7 %all-to-all-start.4 = ((f32[4,3,64,128]{3,2,1,0:T(8,128)}), f32[4,3,64,128]{3,2,1,0:T(8,128)S(1)}, u32[]{:S(2)}, u32[]{:S(2)}) async-start(f32[4,3,64,128]{3,2,1,0:T(8,128)} %copy.42), calls=%async_computation.4 | async-start | bytes 786432 | tf_op jit(solution)/shard_map/all_to_all | solution.py:72
  243.9 15.1 %all-to-all-start.6 = ((f32[32,1,256]{2,1,0:T(1,128)}), f32[32,1,256]{2,1,0:T(1,128)S(1)}, u32[]{:S(2)}, u32[]{:S(2)}) async-start(f32[32,1,256]{2,1,0:T(1,128)} %broadcast_in_dim.45), calls=%async_computation.6 | async-start | bytes 65536 | tf_op jit(solution)/shard_map/all_to_all | solution.py:109

commit v2 on v1

--- a/solution.py
+++ b/solution.py
@@ -29,6 +29,10 @@
     return lax.ppermute(v, "c", [(0, 1), (1, 0)])
 
 
+def spread(v, axes, count):
+    return lax.all_to_all(jnp.broadcast_to(v, (count,) + v.shape), axes, 0, 0, tiled=True)
+
+
 def shards(colloc, coulomb, geminal, occupied):
     points = colloc.shape[0]
     sub = points // YN
@@ -39,9 +43,9 @@
 
     full = jnp.stack([geminal, jnp.concatenate([coulomb, colloc], axis=1)])
 
-    occ_z = lax.all_gather(occupied, ("l", "h"), axis=0, tiled=False)
+    occ_z = spread(occupied, ("l", "h"), ZN)
     own_occ = lax.dynamic_slice_in_dim(occupied, yi * sub, sub, 0)
-    occ_x = lax.all_gather(own_occ, ("x", "c"), axis=0, tiled=True).astype(jnp.float32)
+    occ_x = spread(own_occ, ("x", "c"), 8).astype(jnp.float32)
     w_row = (occ_x * occ_x).astype(jnp.bfloat16)
 
     xf1, xb1 = shift_x(full, 1), shift_x(full, -1)

time: 260 us -> 230 us (0.88)
  blocking collectives: 75.9 us -> 9.06 us
  waiting for transfers between devices: 57.3 us -> 83.7 us
  starting transfers between devices: 55.7 us -> 71.6 us
  local copies, waits for them, and re-layouts: 31.2 us -> 26.1 us
    all_gather x2 -> x0, blocking collectives: 62.5 us -> none  [the longest x1 48.1 us: shards(): occ_z = lax.all_gather(occupied, ('l', 'h'), axis=0, tiled=False)]
    ppermute x4, waiting for transfers between devices: 0.01 us -> 18.7 us  [shift_x(): return lax.ppermute(v, 'x', [(i, (i + d) % 4) for i in range(4)])]
    all_to_all x0 -> x2, starting transfers between devices: none -> 18 us  [spread(): lax.all_to_all(jnp.broadcast_to(v, (count,) + v.shape), axes, 0, 0, tiled...]
    ppermute x5, starting transfers between devices: 13.3 us -> 7.18 us  [swap_core(): return lax.ppermute(v, 'c', [(0, 1), (1, 0)])]
    ppermute x8, starting transfers between devices: 11.7 us -> 17.4 us  [shift_z(): lax.ppermute(v, ('l', 'h'), [(z_slot(z), z_slot((z + d) % ZN)) for z in r...]
    all_to_all x1, blocking collectives: 13.4 us -> 9.06 us  [shards(): got = lax.all_to_all(send, ('x', 'c'), 0, 0, tiled=True)]
    squeeze x6, local copies, waits for them, and re-layouts: 12.7 us -> 8.81 us  [pair(): return (jnp.concatenate([a[0], b[0]]), jnp.concatenate([a[1], b[1]]))]
    all_to_all x0 -> x2, waiting for transfers between devices: none -> 3.66 us  [spread(): lax.all_to_all(jnp.broadcast_to(v, (count,) + v.shape), axes, 0, 0, tiled...]
  transfers between devices with their start and end apart: 23 -> 25, of which waited for: 9 -> 15; matrix products, arithmetic and copies ran while one was open for 23% -> 25% of each run, Pallas kernels for 0% -> 0%
where the time goes in v2:
time: 230 us; the launch traced here: 228 us
  waiting for transfers between devices  83.7 us (36%)
  starting transfers between devices  71.6 us (31%)
  matrix products  31.1 us (14%)
  local copies, waits for them, and re-layouts  26.1 us (11%)
  blocking collectives  9.06 us (4%)
  other arithmetic  5.53 us (2%)
    ppermute x8, waiting for transfers between devices, shift_z(): lax.ppermute(v, ('l', 'h'), [(z_slot(z), z_slot((z + d) % ZN)) for z in r...  38.3 us
    all_to_all x5, starting transfers between devices, gram(): s = lax.all_to_all(t, 'y', 0, 0, tiled=True).sum(0)  18.9 us
    ppermute x4, waiting for transfers between devices, shift_x(): return lax.ppermute(v, 'x', [(i, (i + d) % 4) for i in range(4)])  18.7 us
    all_to_all x2, starting transfers between devices, spread(): lax.all_to_all(jnp.broadcast_to(v, (count,) + v.shape), axes, 0, 0, tiled...  18 us
    ppermute x8, starting transfers between devices, shift_z(): lax.ppermute(v, ('l', 'h'), [(z_slot(z), z_slot((z + d) % ZN)) for z in r...  17.4 us
    dot_general x5, matrix products, gram(): jnp.einsum('qk,ypk->yqp', cg, row_g, preferred_element_type=jnp.float32)  14.5 us
    all_to_all x5, waiting for transfers between devices, gram(): s = lax.all_to_all(t, 'y', 0, 0, tiled=True).sum(0)  13.4 us
    dot_general x5, matrix products, gram(): jnp.einsum('qk,ypk->yqp', cc[:, :NAUXC // YN], row_c[:, :, :NAUXC // YN],...  11.8 us
  transfers between devices with their start and end apart: 25, of which 15 were waited for; matrix products, arithmetic and copies ran while one was open for 25% of the time, Pallas kernels for 0%

profile of v2, /device:TPU:1, one launch (start us, length us, event | category | flops | bytes accessed | tf_op | source)
XLA Modules:
  0.0 228.4 jit_solution(6532094407766338349)
XLA Ops:
  0.6 1.1 constant_dynamic-update-slice_fusion.1
  1.8 0.9 constant_dynamic-update-slice_fusion
  2.7 2.2 pad_maximum_fusion
  5.0 3.2 %collective-permute-start = (bf16[2,64,5120]{2,1,0:T(8,128)(2,1)}, bf16[2,64,5120]{2,1,0:T(8,128)(2,1)}, u32[]{:S(2)}, u32[]{:S(2)}) collective-permute-start(bf16[2,64,5120]{2,1,0:T(8,128)(2,1)} %pad_maximum_fusion), channel_id=1, source_target_pairs={{0,16},{16,0},{1,17},{17,1},{2,18},{18,2},{3,19},{19,3},{4,20},{20... | collective-permute-start | bytes 3932168 | tf_op jit(solution)/shard_map/ppermute | solution.py:29
  9.7 4.9 %collective-permute-start.10 = (bf16[2,64,5120]{2,1,0:T(8,128)(2,1)}, bf16[2,64,5120]{2,1,0:T(8,128)(2,1)}, u32[]{:S(2)}, u32[]{:S(2)}) collective-permute-start(bf16[2,64,5120]{2,1,0:T(8,128)(2,1)} %pad_maximum_fusion), channel_id=1, source_target_pairs={{0,44},{32,0},{4,32},{36,4},{8,36},{40,8},{12,40},{44,12},{1,45},{... | collective-permute-start | bytes 3932168 | tf_op jit(solution)/shard_map/ppermute | solution.py:21
  14.5 1.5 broadcast_in_dim.47
  16.0 4.1 %all-to-all-start.5 = ((bf16[8,64,256]{2,1,0:T(8,128)(2,1)}), bf16[8,64,256]{2,1,0:T(8,128)(2,1)S(1)}, u32[]{:S(2)}, u32[]{:S(2)}) async-start(bf16[8,64,256]{2,1,0:T(8,128)(2,1)} %broadcast_in_dim.47), calls=%async_computation.5 | async-start | bytes 524288 | tf_op jit(solution)/shard_map/all_to_all | solution.py:33
  20.1 1.2 compare_and_fusion
  21.3 0.9 constant_dynamic-update-slice_fusion.17
  22.2 0.9 constant_dynamic-update-slice_fusion.9
  23.1 15.8 %collective-permute-done.1 = bf16[2,64,5120]{2,1,0:T(8,128)(2,1)} collective-permute-done((bf16[2,64,5120]{2,1,0:T(8,128)(2,1)}, bf16[2,64,5120]{2,1,0:T(8,128)(2,1)}, u32[]{:S(2)}, u32[]{:S(2)}) %collective-permute-start.1) | collective-permute-done | bytes 1310752 | tf_op jit(solution)/shard_map/ppermute | solution.py:25
  38.9 1.4 fusion.109
  40.4 2.0 collective-permute-start.7
  42.7 1.5 fusion.110
  44.3 1.2 collective-permute-start.2
  46.1 4.9 %collective-permute-start.12 = (bf16[2,64,5120]{2,1,0:T(8,128)(2,1)}, bf16[2,64,5120]{2,1,0:T(8,128)(2,1)S(1)}, u32[]{:S(2)}, u32[]{:S(2)}) collective-permute-start(bf16[2,64,5120]{2,1,0:T(8,128)(2,1)} %collective-permute-done.10), channel_id=1, source_target_pairs={{0,44},{32,0},{4,32},{36,4},{8,36},{40,8},{12,40},{44,12},{1,45},{... | collective-permute-start | bytes 3932168 | tf_op jit(solution)/shard_map/ppermute | solution.py:21
  51.0 1.4 slice_bitcast_fusion.10
  52.4 1.4 slice_bitcast_fusion.11
  53.9 0.8 collective-permute-start.6
  54.8 1.2 collective-permute-done.7
  55.9 1.4 collective-permute-start.11
  57.3 1.7 collective-permute-done.4
  59.0 2.0 collective-permute-start.8
  61.2 1.5 collective-permute-done.8
  63.1 1.4 fusion.31
  65.2 1.7 convolution_bitcast_fusion.6
  66.9 0.8 copy.35
  67.7 1.3 fusion.22
  69.4 9.6 %collective-permute-done.12 = bf16[2,64,5120]{2,1,0:T(8,128)(2,1)S(1)} collective-permute-done((bf16[2,64,5120]{2,1,0:T(8,128)(2,1)}, bf16[2,64,5120]{2,1,0:T(8,128)(2,1)S(1)}, u32[]{:S(2)}, u32[]{:S(2)}) %collective-permute-start.12) | collective-permute-done | bytes 1310752 | tf_op jit(solution)/shard_map/ppermute | solution.py:21
  79.1 9.8 %collective-permute-done.11 = bf16[2,64,5120]{2,1,0:T(8,128)(2,1)} collective-permute-done((bf16[2,64,5120]{2,1,0:T(8,128)(2,1)}, bf16[2,64,5120]{2,1,0:T(8,128)(2,1)}, u32[]{:S(2)}, u32[]{:S(2)}) %collective-permute-start.11) | collective-permute-done | bytes 1310752 | tf_op jit(solution)/shard_map/ppermute | solution.py:21
  89.0 2.2 slice_bitcast_fusion.7
  91.2 1.5 fusion.21
  92.8 1.0 copy.36
  93.8 4.2 %all-to-all-start = ((f32[4,3,64,128]{3,2,1,0:T(8,128)}), f32[4,3,64,128]{3,2,1,0:T(8,128)S(1)}, u32[]{:S(2)}, u32[]{:S(2)}) async-start(f32[4,3,64,128]{3,2,1,0:T(8,128)} %copy.35), calls=%async_computation | async-start | bytes 786432 | tf_op jit(solution)/shard_map/all_to_all | solution.py:76
  98.0 4.1 %fusion.25 = f32[4,1,128,128]{2,3,0,1:T(8,128)} fusion(bf16[4,128,5120]{2,1,0:T(8,128)(2,1)} %copy-done.3, bf16[64,5120]{1,0:T(8,128)(2,1)S(1)} %get-tuple-element.9, bf16[64,5120]{1,0:T(8,128)(2,1)S(1)} %get-tuple-element.11), kind=kOutput, calls=%fused_computation.35 | convolution fusion | flops 538968064 | bytes 5767168 | tf_op jit(solution)/shard_map/qk,ypk->yqp/dot_general | solution.py:71
  102.1 2.1 all-to-all-done
  104.2 3.5 %all-to-all-start.1 = ((f32[4,3,128,128]{2,3,1,0:T(8,128)}), f32[4,3,128,128]{2,3,1,0:T(8,128)S(1)}, u32[]{:S(2)}, u32[]{:S(2)}) async-start(f32[4,3,128,128]{2,3,1,0:T(8,128)} %copy.36), calls=%async_computation.1 | async-start | bytes 1572864 | tf_op jit(solution)/shard_map/all_to_all | solution.py:76
  107.7 4.2 %fusion.20 = f32[4,1,128,128]{2,3,0,1:T(8,128)S(1)} fusion(bf16[4,128,5120]{2,1,0:T(8,128)(2,1)} %copy-done, bf16[64,5120]{1,0:T(8,128)(2,1)S(1)} %get-tuple-element.10, bf16[64,5120]{1,0:T(8,128)(2,1)} %get-tuple-element.8), kind=kOutput, calls=%fused_computation.32 | convolution fusion | flops 673710080 | bytes 6815744 | tf_op jit(solution)/shard_map/qk,ypk->yqp/dot_general | solution.py:70
  111.9 1.7 convolution_bitcast_fusion.1
  113.7 0.9 copy.38
  114.6 1.4 all-to-all-done.1
  116.0 3.5 %all-to-all-start.2 = ((f32[4,3,128,128]{2,3,1,0:T(8,128)}), f32[4,3,128,128]{2,3,1,0:T(8,128)S(1)}, u32[]{:S(2)}, u32[]{:S(2)}) async-start(f32[4,3,128,128]{2,3,1,0:T(8,128)} %copy.38), calls=%async_computation.2 | async-start | bytes 1572864 | tf_op jit(solution)/shard_map/all_to_all | solution.py:76
  121.1 2.7 %collective-permute-start.14 = (bf16[2,64,5120]{2,1,0:T(8,128)(2,1)}, bf16[2,64,5120]{2,1,0:T(8,128)(2,1)}, u32[]{:S(2)}, u32[]{:S(2)}) collective-permute-start(bf16[2,64,5120]{2,1,0:T(8,128)(2,1)} %copy-done.4), channel_id=1, source_target_pairs={{0,44},{32,0},{4,32},{36,4},{8,36},{40,8},{12,40},{44,12},{1,45},{... | collective-permute-start | bytes 3932168 | tf_op jit(solution)/shard_map/ppermute | solution.py:21
  124.1 3.8 %all-to-all-done.2 = f32[4,3,128,128]{2,3,1,0:T(8,128)S(1)} async-done(((f32[4,3,128,128]{2,3,1,0:T(8,128)}), f32[4,3,128,128]{2,3,1,0:T(8,128)S(1)}, u32[]{:S(2)}, u32[]{:S(2)}) %all-to-all-start.2) | async-done | bytes 786464 | tf_op jit(solution)/shard_map/all_to_all | solution.py:76
  127.9 2.2 slice_bitcast_fusion.3
  130.2 16.9 %collective-permute-done.14 = bf16[2,64,5120]{2,1,0:T(8,128)(2,1)} collective-permute-done((bf16[2,64,5120]{2,1,0:T(8,128)(2,1)}, bf16[2,64,5120]{2,1,0:T(8,128)(2,1)}, u32[]{:S(2)}, u32[]{:S(2)}) %collective-permute-start.14) | collective-permute-done | bytes 1310752 | tf_op jit(solution)/shard_map/ppermute | solution.py:21
  147.1 1.5 slice_bitcast_fusion.2
  148.6 4.3 %fusion.19 = f32[4,1,128,128]{2,3,0,1:T(8,128)S(1)} fusion(bf16[4,128,5120]{2,1,0:T(8,128)(2,1)} %copy-done, bf16[64,5120]{1,0:T(8,128)(2,1)S(1)} %get-tuple-element.6, bf16[64,5120]{1,0:T(8,128)(2,1)} %get-tuple-element.4), kind=kOutput, calls=%fused_computation.31 | convolution fusion | flops 673710080 | bytes 6815744 | tf_op jit(solution)/shard_map/qk,ypk->yqp/dot_general | solution.py:70
  152.9 3.5 %collective-permute-start.16 = (bf16[64,5120]{1,0:T(8,128)(2,1)S(1)}, bf16[64,5120]{1,0:T(8,128)(2,1)}, u32[]{:S(2)}, u32[]{:S(2)}) collective-permute-start(bf16[64,5120]{1,0:T(8,128)(2,1)S(1)} %get-tuple-element.7), channel_id=1, source_target_pairs={{0,44},{32,0},{4,32},{36,4},{8,36},{40,8},{12,40},{44,12},{1,45},{... | collective-permute-start | bytes 1966088 | tf_op jit(solution)/shard_map/ppermute | solution.py:21
  156.8 1.3 fusion.28
  158.2 0.9 copy.40
  159.1 3.9 %all-to-all-start.3 = ((f32[4,3,128,128]{2,3,1,0:T(8,128)}), f32[4,3,128,128]{2,3,1,0:T(8,128)S(1)}, u32[]{:S(2)}, u32[]{:S(2)}) async-start(f32[4,3,128,128]{2,3,1,0:T(8,128)} %copy.40), calls=%async_computation.3 | async-start | bytes 1572864 | tf_op jit(solution)/shard_map/all_to_all | solution.py:76
  163.0 1.3 collective-permute-done.16
  164.3 3.7 %fusion.34 = f32[4,1,64,128]{3,2,0,1:T(8,128)S(1)} fusion(bf16[4,128,5120]{2,1,0:T(8,128)(2,1)} %copy-done.3, bf16[64,5120]{1,0:T(8,128)(2,1)} %collective-permute-done.16), kind=kOutput, calls=%fused_computation.41 | convolution fusion | flops 268435456 | bytes 4849664 | tf_op jit(solution)/shard_map/qk,ypk->yqp/dot_general | solution.py:71
  168.0 1.7 convolution_bitcast_fusion.3
  169.7 2.8 %convolution_bitcast_fusion.5 = f32[4,1,64,128]{3,2,0,1:T(8,128)S(1)} fusion(bf16[4,128,5120]{2,1,0:T(8,128)(2,1)S(1)} %bitcast.187, bf16[64,5120]{1,0:T(8,128)(2,1)} %collective-permute-done.15), kind=kOutput, calls=%fused_computation.45 | convolution fusion | flops 335544320 | bytes 6029312 | tf_op jit(solution)/shard_map/qk,ypk->yqp/dot_general | solution.py:70
  172.5 0.8 copy.42
  173.3 3.8 %all-to-all-start.4 = ((f32[4,3,64,128]{3,2,1,0:T(8,128)}), f32[4,3,64,128]{3,2,1,0:T(8,128)S(1)}, u32[]{:S(2)}, u32[]{:S(2)}) async-start(f32[4,3,64,128]{3,2,1,0:T(8,128)} %copy.42), calls=%async_computation.4 | async-start | bytes 786432 | tf_op jit(solution)/shard_map/all_to_all | solution.py:76
  177.2 6.1 %all-to-all-done.4 = f32[4,3,64,128]{3,2,1,0:T(8,128)S(1)} async-done(((f32[4,3,64,128]{3,2,1,0:T(8,128)}), f32[4,3,64,128]{3,2,1,0:T(8,128)S(1)}, u32[]{:S(2)}, u32[]{:S(2)}) %all-to-all-start.4) | async-done | bytes 393248 | tf_op jit(solution)/shard_map/all_to_all | solution.py:76
  184.0 13.9 %all-to-all-start.6 = ((bf16[8,16,256]{2,1,0:T(8,128)(2,1)}), bf16[8,16,256]{2,1,0:T(8,128)(2,1)S(1)}, u32[]{:S(2)}, u32[]{:S(2)}) async-start(bf16[8,16,256]{2,1,0:T(8,128)(2,1)} %broadcast_in_dim.51), calls=%async_computation.6 | async-start | bytes 131072 | tf_op jit(solution)/shard_map/all_to_all | solution.py:33
  199.1 3.7 %all-to-all-done.6 = bf16[8,16,256]{2,1,0:T(8,128)(2,1)S(1)} async-done(((bf16[8,16,256]{2,1,0:T(8,128)(2,1)}), bf16[8,16,256]{2,1,0:T(8,128)(2,1)S(1)}, u32[]{:S(2)}, u32[]{:S(2)}) %all-to-all-start.6) | async-done | bytes 65568 | tf_op jit(solution)/shard_map/all_to_all | solution.py:33
  202.8 9.1 %all_to_all.45 = f32[8,24,256]{2,1,0:T(8,128)S(1)} all-to-all(f32[8,24,256]{2,1,0:T(8,128)S(1)} %pad_maximum_fusion.9), channel_id=1, replica_groups=mesh['x'=4,'l'=2,'c'=2,'h'=4,'y'=4] {'x','c'}, dimensions={0} | all-to-all | bytes 393216 | tf_op jit(solution)/shard_map/all_to_all | solution.py:110
  212.5 6.6 %all-to-all-start.8 = ((f32[32,1,256]{2,1,0:T(1,128)}), f32[32,1,256]{2,1,0:T(1,128)S(1)}, u32[]{:S(2)}, u32[]{:S(2)}) async-start(f32[32,1,256]{2,1,0:T(1,128)} %broadcast_in_dim.53), calls=%async_computation.8 | async-start | bytes 65536 | tf_op jit(solution)/shard_map/all_to_all | solution.py:113
  219.7 8.1 %all-to-all-done.8 = f32[32,1,256]{2,1,0:T(1,128)S(1)} async-done(((f32[32,1,256]{2,1,0:T(1,128)}), f32[32,1,256]{2,1,0:T(1,128)S(1)}, u32[]{:S(2)}, u32[]{:S(2)}) %all-to-all-start.8) | async-done | bytes 32800 | tf_op jit(solution)/shard_map/all_to_all | solution.py:113
  (114 shorter events, 10.6 us)
Async XLA Ops:
  0.6 21.6 %copy-start.1 = (bf16[64,5120]{1,0:T(8,128)(2,1)S(1)}, bf16[64,5120]{1,0:T(8,128)(2,1)}, u32[]{:S(2)}) copy-start(bf16[64,5120]{1,0:T(8,128)(2,1)} %param.7) | copy-start | bytes 1966084
  5.0 37.7 %collective-permute-start = (bf16[2,64,5120]{2,1,0:T(8,128)(2,1)}, bf16[2,64,5120]{2,1,0:T(8,128)(2,1)}, u32[]{:S(2)}, u32[]{:S(2)}) collective-permute-start(bf16[2,64,5120]{2,1,0:T(8,128)(2,1)} %pad_maximum_fusion), channel_id=1, source_target_pairs={{0,16},{16,0},{1,17},{17,1},{2,18},{18,2},{3,19},{19,3},{4,20},{20... | collective-permute-start | bytes 3932168 | tf_op jit(solution)/shard_map/ppermute | solution.py:29
  8.2 30.7 %collective-permute-start.1 = (bf16[2,64,5120]{2,1,0:T(8,128)(2,1)}, bf16[2,64,5120]{2,1,0:T(8,128)(2,1)}, u32[]{:S(2)}, u32[]{:S(2)}) collective-permute-start(bf16[2,64,5120]{2,1,0:T(8,128)(2,1)} %pad_maximum_fusion), channel_id=1, source_target_pairs={{0,192},{64,0},{128,64},{192,128},{1,193},{65,1},{129,65},{193,129... | collective-permute-start | bytes 3932168 | tf_op jit(solution)/shard_map/ppermute | solution.py:25
  8.9 33.5 %collective-permute-start.3 = (bf16[2,64,5120]{2,1,0:T(8,128)(2,1)}, bf16[2,64,5120]{2,1,0:T(8,128)(2,1)S(1)}, u32[]{:S(2)}, u32[]{:S(2)}) collective-permute-start(bf16[2,64,5120]{2,1,0:T(8,128)(2,1)} %pad_maximum_fusion), channel_id=1, source_target_pairs={{0,64},{64,128},{128,192},{192,0},{1,65},{65,129},{129,193},{193,1... | collective-permute-start | bytes 3932168 | tf_op jit(solution)/shard_map/ppermute | solution.py:25
  9.7 36.4 %collective-permute-start.10 = (bf16[2,64,5120]{2,1,0:T(8,128)(2,1)}, bf16[2,64,5120]{2,1,0:T(8,128)(2,1)}, u32[]{:S(2)}, u32[]{:S(2)}) collective-permute-start(bf16[2,64,5120]{2,1,0:T(8,128)(2,1)} %pad_maximum_fusion), channel_id=1, source_target_pairs={{0,44},{32,0},{4,32},{36,4},{8,36},{40,8},{12,40},{44,12},{1,45},{... | collective-permute-start | bytes 3932168 | tf_op jit(solution)/shard_map/ppermute | solution.py:21
  14.5 37.9 %collective-permute-start.9 = (bf16[2,64,5120]{2,1,0:T(8,128)(2,1)}, bf16[2,64,5120]{2,1,0:T(8,128)(2,1)}, u32[]{:S(2)}, u32[]{:S(2)}) collective-permute-start(bf16[2,64,5120]{2,1,0:T(8,128)(2,1)} %pad_maximum_fusion), channel_id=1, source_target_pairs={{0,32},{32,4},{4,36},{36,8},{8,40},{40,12},{12,44},{44,0},{1,33},{... | collective-permute-start | bytes 3932168 | tf_op jit(solution)/shard_map/ppermute | solution.py:21
  16.0 77.8 %all-to-all-start.5 = ((bf16[8,64,256]{2,1,0:T(8,128)(2,1)}), bf16[8,64,256]{2,1,0:T(8,128)(2,1)S(1)}, u32[]{:S(2)}, u32[]{:S(2)}) async-start(bf16[8,64,256]{2,1,0:T(8,128)(2,1)} %broadcast_in_dim.47), calls=%async_computation.5 | async-start | bytes 524288 | tf_op jit(solution)/shard_map/all_to_all | solution.py:33
  23.1 21.1 %copy-start.2 = (bf16[4,128,5120]{2,1,0:T(8,128)(2,1)S(1)}, bf16[4,128,5120]{2,1,0:T(8,128)(2,1)}, u32[]{:S(2)}) copy-start(bf16[4,128,5120]{2,1,0:T(8,128)(2,1)} %constant_dynamic-update-slice_fusion.17) | copy-start | bytes 15728644
  40.4 15.6 %collective-permute-start.7 = (bf16[64,5120]{1,0:T(8,128)(2,1)S(1)}, bf16[64,5120]{1,0:T(8,128)(2,1)S(1)}, u32[]{:S(2)}, u32[]{:S(2)}) collective-permute-start(bf16[64,5120]{1,0:T(8,128)(2,1)S(1)} %get-tuple-element.24), channel_id=1, source_target_pairs={{0,192},{64,0},{128,64},{192,128},{1,193},{65,1},{129,65},{193,129... | collective-permute-start | bytes 1966088 | tf_op jit(solution)/shard_map/ppermute | solution.py:25
  42.4 11.4 %slice-start = ((s8[5242880]{0:T(1024)(128)(4,1)}), s8[4194304]{0:T(1024)(128)(4,1)S(1)}, s32[]{:S(2)}) async-start(s8[5242880]{0:T(1024)(128)(4,1)} %bitcast.184), calls=%async_computation.9 | async-start | bytes 8388608
  42.6 16.4 %collective-permute-start.4 = (bf16[64,5120]{1,0:T(8,128)(2,1)S(1)}, bf16[64,5120]{1,0:T(8,128)(2,1)S(1)}, u32[]{:S(2)}, u32[]{:S(2)}) collective-permute-start(bf16[64,5120]{1,0:T(8,128)(2,1)S(1)} %get-tuple-element.19), channel_id=1, source_target_pairs={{0,64},{64,128},{128,192},{192,0},{1,65},{65,129},{129,193},{193,1... | collective-permute-start | bytes 1966088 | tf_op jit(solution)/shard_map/ppermute | solution.py:25
  44.2 9.6 %slice-start.1 = ((s8[5242880]{0:T(1024)(128)(4,1)}), s8[1048576]{0:T(1024)(128)(4,1)S(1)}, s32[]{:S(2)}) async-start(s8[5242880]{0:T(1024)(128)(4,1)} %bitcast.184), calls=%async_computation.10 | async-start | bytes 2097152
  44.3 16.7 %collective-permute-start.2 = (bf16[2,64,5120]{2,1,0:T(8,128)(2,1)}, bf16[2,64,5120]{2,1,0:T(8,128)(2,1)S(1)}, u32[]{:S(2)}, u32[]{:S(2)}) collective-permute-start(bf16[2,64,5120]{2,1,0:T(8,128)(2,1)} %collective-permute-done.1), channel_id=1, source_target_pairs={{0,16},{16,0},{1,17},{17,1},{2,18},{18,2},{3,19},{19,3},{4,20},{20... | collective-permute-start | bytes 3932168 | tf_op jit(solution)/shard_map/ppermute | solution.py:29
  46.1 33.0 %collective-permute-start.12 = (bf16[2,64,5120]{2,1,0:T(8,128)(2,1)}, bf16[2,64,5120]{2,1,0:T(8,128)(2,1)S(1)}, u32[]{:S(2)}, u32[]{:S(2)}) collective-permute-start(bf16[2,64,5120]{2,1,0:T(8,128)(2,1)} %collective-permute-done.10), channel_id=1, source_target_pairs={{0,44},{32,0},{4,32},{36,4},{8,36},{40,8},{12,40},{44,12},{1,45},{... | collective-permute-start | bytes 3932168 | tf_op jit(solution)/shard_map/ppermute | solution.py:21
  53.9 8.9 %collective-permute-start.6 = (bf16[2,64,5120]{2,1,0:T(8,128)(2,1)S(1)}, bf16[2,64,5120]{2,1,0:T(8,128)(2,1)S(1)}, u32[]{:S(2)}, u32[]{:S(2)}) collective-permute-start(bf16[2,64,5120]{2,1,0:T(8,128)(2,1)S(1)} %collective-permute-done.3), channel_id=1, source_target_pairs={{0,16},{16,0},{1,17},{17,1},{2,18},{18,2},{3,19},{19,3},{4,20},{20... | collective-permute-start | bytes 3932168 | tf_op jit(solution)/shard_map/ppermute | solution.py:29
  55.9 33.1 %collective-permute-start.11 = (bf16[2,64,5120]{2,1,0:T(8,128)(2,1)}, bf16[2,64,5120]{2,1,0:T(8,128)(2,1)}, u32[]{:S(2)}, u32[]{:S(2)}) collective-permute-start(bf16[2,64,5120]{2,1,0:T(8,128)(2,1)} %collective-permute-done.9), channel_id=1, source_target_pairs={{0,32},{32,4},{4,36},{36,8},{8,40},{40,12},{12,44},{44,0},{1,33},{... | collective-permute-start | bytes 3932168 | tf_op jit(solution)/shard_map/ppermute | solution.py:21
  59.0 3.7 %collective-permute-start.8 = (bf16[64,5120]{1,0:T(8,128)(2,1)S(1)}, bf16[64,5120]{1,0:T(8,128)(2,1)S(1)}, u32[]{:S(2)}, u32[]{:S(2)}) collective-permute-start(bf16[64,5120]{1,0:T(8,128)(2,1)S(1)} %collective-permute-done.7), channel_id=1, source_target_pairs={{0,16},{16,0},{1,17},{17,1},{2,18},{18,2},{3,19},{19,3},{4,20},{20... | collective-permute-start | bytes 1966088 | tf_op jit(solution)/shard_map/ppermute | solution.py:29
  61.0 3.5 %collective-permute-start.5 = (bf16[64,5120]{1,0:T(8,128)(2,1)S(1)}, bf16[64,5120]{1,0:T(8,128)(2,1)S(1)}, u32[]{:S(2)}, u32[]{:S(2)}) collective-permute-start(bf16[64,5120]{1,0:T(8,128)(2,1)S(1)} %collective-permute-done.4), channel_id=1, source_target_pairs={{0,16},{16,0},{1,17},{17,1},{2,18},{18,2},{3,19},{19,3},{4,20},{20... | collective-permute-start | bytes 1966088 | tf_op jit(solution)/shard_map/ppermute | solution.py:29
  61.1 1.9 copy-start.5
  63.0 6.4 %copy-start.3 = (bf16[4,128,5120]{2,1,0:T(8,128)(2,1)}, bf16[4,128,5120]{2,1,0:T(8,128)(2,1)S(1)}, u32[]{:S(2)}) copy-start(bf16[4,128,5120]{2,1,0:T(8,128)(2,1)S(1)} %constant_dynamic-update-slice_fusion.10) | copy-start | bytes 15728644
  63.1 1.6 copy-start.7
  64.7 26.5 %copy-start = (bf16[4,128,5120]{2,1,0:T(8,128)(2,1)}, bf16[4,128,5120]{2,1,0:T(8,128)(2,1)S(1)}, u32[]{:S(2)}) copy-start(bf16[4,128,5120]{2,1,0:T(8,128)(2,1)S(1)} %constant_dynamic-update-slice_fusion.2) | copy-start | bytes 15728644
  79.0 14.7 %copy-start.4 = (bf16[2,64,5120]{2,1,0:T(8,128)(2,1)}, bf16[2,64,5120]{2,1,0:T(8,128)(2,1)S(1)}, u32[]{:S(2)}) copy-start(bf16[2,64,5120]{2,1,0:T(8,128)(2,1)S(1)} %collective-permute-done.12) | copy-start | bytes 3932164
  93.8 34.1 %collective-permute-start.13 = (bf16[2,64,5120]{2,1,0:T(8,128)(2,1)}, bf16[2,64,5120]{2,1,0:T(8,128)(2,1)}, u32[]{:S(2)}, u32[]{:S(2)}) collective-permute-start(bf16[2,64,5120]{2,1,0:T(8,128)(2,1)} %collective-permute-done.11), channel_id=1, source_target_pairs={{0,32},{32,4},{4,36},{36,8},{8,40},{40,12},{12,44},{44,0},{1,33},{... | collective-permute-start | bytes 3932168 | tf_op jit(solution)/shard_map/ppermute | solution.py:21
  93.8 10.4 %all-to-all-start = ((f32[4,3,64,128]{3,2,1,0:T(8,128)}), f32[4,3,64,128]{3,2,1,0:T(8,128)S(1)}, u32[]{:S(2)}, u32[]{:S(2)}) async-start(f32[4,3,64,128]{3,2,1,0:T(8,128)} %copy.35), calls=%async_computation | async-start | bytes 786432 | tf_op jit(solution)/shard_map/all_to_all | solution.py:76
  104.2 11.8 %all-to-all-start.1 = ((f32[4,3,128,128]{2,3,1,0:T(8,128)}), f32[4,3,128,128]{2,3,1,0:T(8,128)S(1)}, u32[]{:S(2)}, u32[]{:S(2)}) async-start(f32[4,3,128,128]{2,3,1,0:T(8,128)} %copy.36), calls=%async_computation.1 | async-start | bytes 1572864 | tf_op jit(solution)/shard_map/all_to_all | solution.py:76
  107.7 5.9 %copy-start.6 = (f32[4,1,128,128]{2,3,0,1:T(8,128)S(1)}, f32[4,1,128,128]{2,3,0,1:T(8,128)}, u32[]{:S(2)}) copy-start(f32[4,1,128,128]{2,3,0,1:T(8,128)} %fusion.25) | copy-start | bytes 786436
  111.9 7.6 %copy-start.8 = (pred[8]{0:T(512)(128)(4,1)S(1)}, pred[8]{0:T(512)(128)(4,1)}, u32[]{:S(2)}) copy-start(pred[8]{0:T(512)(128)(4,1)} %get-tuple-element.2) | copy-start | bytes 28
  116.0 11.8 %all-to-all-start.2 = ((f32[4,3,128,128]{2,3,1,0:T(8,128)}), f32[4,3,128,128]{2,3,1,0:T(8,128)S(1)}, u32[]{:S(2)}, u32[]{:S(2)}) async-start(f32[4,3,128,128]{2,3,1,0:T(8,128)} %copy.38), calls=%async_computation.2 | async-start | bytes 1572864 | tf_op jit(solution)/shard_map/all_to_all | solution.py:76
  121.1 25.9 %collective-permute-start.14 = (bf16[2,64,5120]{2,1,0:T(8,128)(2,1)}, bf16[2,64,5120]{2,1,0:T(8,128)(2,1)}, u32[]{:S(2)}, u32[]{:S(2)}) collective-permute-start(bf16[2,64,5120]{2,1,0:T(8,128)(2,1)} %copy-done.4), channel_id=1, source_target_pairs={{0,44},{32,0},{4,32},{36,4},{8,36},{40,8},{12,40},{44,12},{1,45},{... | collective-permute-start | bytes 3932168 | tf_op jit(solution)/shard_map/ppermute | solution.py:21
  130.2 39.5 %collective-permute-start.15 = (bf16[64,5120]{1,0:T(8,128)(2,1)}, bf16[64,5120]{1,0:T(8,128)(2,1)}, u32[]{:S(2)}, u32[]{:S(2)}) collective-permute-start(bf16[64,5120]{1,0:T(8,128)(2,1)} %get-tuple-element.4), channel_id=1, source_target_pairs={{0,32},{32,4},{4,36},{36,8},{8,40},{40,12},{12,44},{44,0},{1,33},{... | collective-permute-start | bytes 1966088 | tf_op jit(solution)/shard_map/ppermute | solution.py:21
  147.0 9.3 %slice-start.4 = ((s8[5242880]{0:T(1024)(128)(4,1)}), s8[4194304]{0:T(1024)(128)(4,1)S(1)}, s32[]{:S(2)}) async-start(s8[5242880]{0:T(1024)(128)(4,1)} %bitcast.192), calls=%async_computation.13 | async-start | bytes 8388608
  148.6 7.8 %slice-start.5 = ((s8[5242880]{0:T(1024)(128)(4,1)}), s8[1048576]{0:T(1024)(128)(4,1)S(1)}, s32[]{:S(2)}) async-start(s8[5242880]{0:T(1024)(128)(4,1)} %bitcast.192), calls=%async_computation.14 | async-start | bytes 2097152
  152.9 11.4 %collective-permute-start.16 = (bf16[64,5120]{1,0:T(8,128)(2,1)S(1)}, bf16[64,5120]{1,0:T(8,128)(2,1)}, u32[]{:S(2)}, u32[]{:S(2)}) collective-permute-start(bf16[64,5120]{1,0:T(8,128)(2,1)S(1)} %get-tuple-element.7), channel_id=1, source_target_pairs={{0,44},{32,0},{4,32},{36,4},{8,36},{40,8},{12,40},{44,12},{1,45},{... | collective-permute-start | bytes 1966088 | tf_op jit(solution)/shard_map/ppermute | solution.py:21
  158.2 11.5 %slice-start.2 = ((s8[5242880]{0:T(1024)(128)(4,1)}), s8[1048576]{0:T(1024)(128)(4,1)S(1)}, s32[]{:S(2)}) async-start(s8[5242880]{0:T(1024)(128)(4,1)} %bitcast.186), calls=%async_computation.11 | async-start | bytes 2097152
  159.1 14.2 %all-to-all-start.3 = ((f32[4,3,128,128]{2,3,1,0:T(8,128)}), f32[4,3,128,128]{2,3,1,0:T(8,128)S(1)}, u32[]{:S(2)}, u32[]{:S(2)}) async-start(f32[4,3,128,128]{2,3,1,0:T(8,128)} %copy.40), calls=%async_computation.3 | async-start | bytes 1572864 | tf_op jit(solution)/shard_map/all_to_all | solution.py:76
  163.0 6.7 %slice-start.3 = ((s8[5242880]{0:T(1024)(128)(4,1)}), s8[4194304]{0:T(1024)(128)(4,1)S(1)}, s32[]{:S(2)}) async-start(s8[5242880]{0:T(1024)(128)(4,1)} %bitcast.186), calls=%async_computation.12 | async-start | bytes 8388608
  173.3 10.0 %all-to-all-start.4 = ((f32[4,3,64,128]{3,2,1,0:T(8,128)}), f32[4,3,64,128]{3,2,1,0:T(8,128)S(1)}, u32[]{:S(2)}, u32[]{:S(2)}) async-start(f32[4,3,64,128]{3,2,1,0:T(8,128)} %copy.42), calls=%async_computation.4 | async-start | bytes 786432 | tf_op jit(solution)/shard_map/all_to_all | solution.py:76
  184.0 18.8 %all-to-all-start.6 = ((bf16[8,16,256]{2,1,0:T(8,128)(2,1)}), bf16[8,16,256]{2,1,0:T(8,128)(2,1)S(1)}, u32[]{:S(2)}, u32[]{:S(2)}) async-start(bf16[8,16,256]{2,1,0:T(8,128)(2,1)} %broadcast_in_dim.51), calls=%async_computation.6 | async-start | bytes 131072 | tf_op jit(solution)/shard_map/all_to_all | solution.py:33
  212.5 15.3 %all-to-all-start.8 = ((f32[32,1,256]{2,1,0:T(1,128)}), f32[32,1,256]{2,1,0:T(1,128)S(1)}, u32[]{:S(2)}, u32[]{:S(2)}) async-start(f32[32,1,256]{2,1,0:T(1,128)} %broadcast_in_dim.53), calls=%async_computation.8 | async-start | bytes 65536 | tf_op jit(solution)/shard_map/all_to_all | solution.py:113

commit v3 on v2

v3 whole, which is shorter than its diff:
```python
import functools
import math

import jax
import jax.numpy as jnp
from jax import lax
from jax.experimental import pallas as pl
from jax.experimental.pallas import tpu as pltpu
from jax.sharding import Mesh, PartitionSpec as P

NBAS = 4096
NAUXC = 16384
NAUXF = 20480
NGRID = 4096
ZN = 8
XN = 4
YN = 4
LANES = 128
GROUP = 4
SCALES = (math.sqrt(NAUXF), math.sqrt(NAUXC), math.sqrt(NBAS))
VMEM = pl.BlockSpec(memory_space=pltpu.VMEM)
SMEM = pl.BlockSpec(memory_space=pltpu.SMEM)


def tie(*values):
    return lax.optimization_barrier(values)


def z_slot(z):
    return (z % 2) * (ZN // 2) + z // 2


def shift_z(v, d):
    return lax.ppermute(v, ("l", "h"), [(z_slot(z), z_slot((z + d) % ZN)) for z in range(ZN)])


def shift_x(v, d):
    return lax.ppermute(v, "x", [(i, (i + d) % XN) for i in range(XN)])


def swap_core(v):
    return lax.ppermute(v, "c", [(0, 1), (1, 0)])


def spread(v, axes, count):
    return lax.all_to_all(jnp.broadcast_to(v, (count,) + v.shape), axes, 0, 0, tiled=True)


def over_y(t):
    return lax.all_to_all(t, "y", 0, 0, tiled=True)


def squared(v):
    v = v.astype(jnp.float32)
    return (v * v).astype(jnp.bfloat16)


def call(body, out, args):
    several = isinstance(out, tuple)
    return pl.pallas_call(
        body,
        out_shape=out,
        in_specs=[SMEM] + [VMEM] * (len(args) - 1),
        out_specs=tuple(VMEM for _ in out) if several else VMEM,
        cost_estimate=pl.CostEstimate(flops=0, bytes_accessed=0, transcendentals=0),
        compiler_params=pltpu.CompilerParams(vmem_limit_bytes=32 * 1024 * 1024),
    )(*args)


def pack_body(place, *refs):
    parts, (kept, given) = refs[:-2], refs[-2:]
    core = place[0]
    slab = 0
    for ref in parts:
        half = ref.shape[1] // 2
        for i in range(half // LANES):
            for out, which in ((kept, core), (given, 1 - core)):
                start = pl.multiple_of(which * half + i * LANES, LANES)
                out[slab] = ref[:, pl.ds(start, LANES)]
            slab += 1


def merge_body(place, kept, got, occ, out):
    core = place[0]
    n, points, _ = kept.shape
    out[:n, pl.ds(pl.multiple_of(core * points, points), points)] = kept[...]
    out[:n, pl.ds(pl.multiple_of((1 - core) * points, points), points)] = got[...]
    out[n, :points] = occ[:, :LANES]
    out[n, points:] = occ[:, LANES:]


def tile_body(cuts, sizes, place, *refs):
    blocks = []
    for n in sizes:
        blocks.append(refs[:n])
        refs = refs[n:]
    keep, *send = refs

    def slab(block, t):
        first = block[0].shape[0]
        return block[0][t] if len(block) == 1 or t < first else block[1][t - first]

    rows, cols = blocks[:XN], blocks[XN:]
    points = keep.shape[2] // len(cols)
    sub = points // YN
    core = place[0]
    for j, (a, b) in enumerate(zip(cuts, cuts[1:])):
        acc = None
        for s in range(a, b, GROUP):
            r, q = [], []
            for t in range(s, s + GROUP):
                slabs = [slab(x, t) for x in rows]
                r.append(
                    jnp.concatenate(
                        [
                            x[c * points + y * sub : c * points + (y + 1) * sub]
                            for y in range(YN)
                            for x in slabs
                            for c in range(2)
                        ]
                    )
                )
                q.append(jnp.concatenate([slab(x, t) for x in cols]))
            part = lax.dot_general(
                jnp.concatenate(q, axis=1),
                jnp.concatenate(r, axis=1),
                (((1,), (1,)), ((), ())),
                preferred_element_type=jnp.float32,
            )
            acc = part if acc is None else acc + part
        width = 2 * points
        for n in range(len(cols)):
            first = acc[2 * n * points : (2 * n + 1) * points]
            second = acc[(2 * n + 1) * points : (2 * n + 2) * points]
            to, at = (send[0], j) if len(send) == 1 else (send[j], 0)
            for out, i, t in (
                (keep, j, jnp.where(core == 0, first, second)),
                (to, at, jnp.where(core == 0, second, first)),
            ):
                for y in range(YN):
                    out[y, i, n * points : (n + 1) * points] = t[:, y * width : (y + 1) * width]


def tiles(cuts, place, rows, cols, split=False):
    points = rows[0][0].shape[1] // 2
    blocks = tuple(rows) + tuple(cols)

    def out(n):
        return jax.ShapeDtypeStruct((YN, n, len(cols) * points, 2 * points), jnp.float32)

    outs = (out(3),) + ((out(1),) * 3 if split else (out(3),))
    body = functools.partial(tile_body, cuts, tuple(len(b) for b in blocks))
    return call(body, outs, (place,) + tuple(ref for b in blocks for ref in b))


def add_body(place, a, *refs):
    *others, out = refs
    if len(others) == 1:
        out[...] = a[...] + others[0][...]
    else:
        for j, other in enumerate(others):
            out[:, j] = a[:, j] + other[:, 0]


def add(place, a, *others):
    return call(add_body, jax.ShapeDtypeStruct(a.shape, a.dtype), (place, a) + others)


def orbitals_body(place, *refs):
    for i, ref in enumerate(refs[:-1]):
        refs[-1][i] = ref[0]


def orbitals(place, blocks):
    n, width = len(blocks), blocks[0].shape[1:]

    def last(b):
        at = b.shape[0] - 1
        return pl.BlockSpec((1,) + width, lambda i: (at, 0, 0))

    return pl.pallas_call(
        orbitals_body,
        out_shape=jax.ShapeDtypeStruct((n,) + width, blocks[0].dtype),
        grid=(1,),
        in_specs=[SMEM] + [last(b) for b in blocks],
        out_specs=pl.BlockSpec((n,) + width, lambda i: (0, 0, 0)),
        cost_estimate=pl.CostEstimate(flops=0, bytes_accessed=0, transcendentals=0),
    )(place, *blocks)


def field(place, s, cols, diagonal):
    t = s[0] + s[1] + s[2] + s[3]
    bas = t[2] / SCALES[2]
    kern = bas * bas * (t[1] / SCALES[1]) * (t[0] / SCALES[0])
    points = cols[0].shape[1] // 2
    sub = points // YN
    if diagonal:
        q = lax.broadcasted_iota(jnp.int32, kern.shape, 0)
        p = lax.broadcasted_iota(jnp.int32, kern.shape, 1) - place[0] * sub
        kern = jnp.where((p >= 0) & (p < sub) & (q == p + place[1] * sub), jnp.float32(0.0), kern)
    last = [c[c.shape[0] - 1] for c in cols]
    w = squared(jnp.concatenate([jnp.concatenate([c[:points], c[points:]], axis=1) for c in last]))
    return lax.dot_general(
        kern.astype(jnp.bfloat16), w, (((0,), (0,)), ((), ())), preferred_element_type=jnp.float32
    )


def apply_body(diagonal, place, s, *refs):
    refs[-1][...] = field(place, s, refs[:-1], diagonal)


def apply(place, s, cols, diagonal=False):
    out = jax.ShapeDtypeStruct((s.shape[-1], 2 * LANES), jnp.float32)
    return call(functools.partial(apply_body, diagonal), out, (place, s) + tuple(cols))


def last_body(place, s, col, p1, p2, p3, own, other, out):
    part = (field(place, s, [col], False) + p1[...] + p2[...] + p3[...]) / math.sqrt(NGRID)
    core, y, x = place[0], place[1], place[2]
    points = own.shape[1] // 2
    sub = points // YN
    energy = jnp.zeros((sub, part.shape[1]), jnp.float32)
    at = pl.multiple_of(y * sub, sub)
    for i in range(XN):
        for c in range(2):
            w = jnp.concatenate(
                [
                    jnp.where(core == c, own[i, pl.ds(o + at, sub)], other[i, pl.ds(o + at, sub)])
                    for o in (0, points)
                ],
                axis=1,
            )
            mine = part[(2 * i + c) * sub : (2 * i + c + 1) * sub]
            energy += squared(w).astype(jnp.float32) * mine
            out[2 * ((i + x) % XN) + c, :sub] = mine
    total = jnp.sum(energy, axis=0, keepdims=True) / math.sqrt(NGRID)
    for g in range(2 * XN):
        out[g, sub:] = jnp.broadcast_to(total, (8, total.shape[1]))


def shards(colloc, coulomb, geminal, occupied):
    points = colloc.shape[0]
    sub = points // YN
    place = jnp.stack([lax.axis_index("c"), lax.axis_index("y"), lax.axis_index("x")]).astype(jnp.int32)

    n_slabs = (geminal.shape[1] + coulomb.shape[1] + colloc.shape[1]) // (2 * LANES)
    half = geminal.shape[1] // (2 * LANES)
    cuts = (0, half, half + coulomb.shape[1] // (2 * LANES), n_slabs)
    piece = jax.ShapeDtypeStruct((n_slabs, points, LANES), jnp.bfloat16)
    kept, given = call(pack_body, (piece, piece), (place, geminal, coulomb, colloc))
    block = call(
        merge_body,
        jax.ShapeDtypeStruct((n_slabs + 1, 2 * points, LANES), jnp.bfloat16),
        (place, kept, swap_core(given), occupied),
    )

    f1, b1 = shift_z(block, 1), shift_z(block, -1)
    xf1, xb1 = shift_x(block, 1), shift_x(block, -1)
    f1, b1, xf1, xb1 = tie(f1, b1, xf1, xb1)

    f2, b2 = shift_z(f1, 1), shift_z(b1, -1)
    x2a, x2b = shift_x(xf1[:half], 1), shift_x(xb1[half:], -1)
    rows = ((block,), (xb1,), (x2a, x2b), (xf1,))
    keep, send = tiles(cuts, place, rows, ((block,), (f1,), (b1,)))
    t1 = add(place, keep, swap_core(send))
    f2, b2, t1 = tie(f2, b2, t1)

    f3, b3 = shift_z(f2, 1), shift_z(b2, -1)
    s1 = over_y(t1)
    keep, send = tiles(cuts, place, rows, ((f2,), (b2,)))
    t2 = add(place, keep, swap_core(send))
    own = orbitals(place, (block, xb1, x2b, xf1))
    other = swap_core(own)
    f3, b3, s1, t2, other = tie(f3, b3, s1, t2, other)

    f4, b4 = shift_z(f3[:half], 1), shift_z(b3[half:], -1)
    s2 = over_y(t2)
    keep, *send = tiles(cuts, place, rows, ((f3,), (b3,)), split=True)
    t3 = add(place, keep, *[swap_core(v) for v in send])
    p1 = apply(place, s1, (block, f1, b1), diagonal=True)
    f4, b4, s2, t3, p1 = tie(f4, b4, s2, t3, p1)

    s3 = over_y(t3)
    keep, send = tiles(cuts, place, rows, ((f4, b4),))
    s4 = over_y(add(place, keep, swap_core(send)))
    p2 = apply(place, s2, (f2, b2))
    p3 = apply(place, s3, (f3, b3))
    sent = call(
        last_body,
        jax.ShapeDtypeStruct((2 * XN, sub + 8, 2 * LANES), jnp.float32),
        (place, s4, b4, p1, p2, p3, own, other),
    )
    got = lax.all_to_all(sent, ("x", "c"), 0, 0, tiled=True)
    pair_field = got[:, :sub].sum(0)
    energy = got[:, sub].sum(0)
    energy = spread(energy[None], ("l", "h", "y"), ZN * YN).sum((0, 1))
    return pair_field, energy


def solution(mesh):
    fine = Mesh(mesh.devices.reshape(4, 2, 2, 4, 4), ("x", "l", "c", "h", "y"))
    grid = ("x", "l", "c", "h")
    in_specs = (P(grid, "y"), P(grid, "y"), P(grid, "y"), P(grid, None))
    out_specs = (P(grid + ("y",), None), P())
    return jax.shard_map(shards, mesh=fine, in_specs=in_specs, out_specs=out_specs, check_vma=False)
```

time: 230 us -> 191 us (0.83)
  matrix products: 31.1 us -> 0 us
  Pallas kernels: 0 us -> 27 us
  starting transfers between devices: 71.6 us -> 55.7 us
  waiting for transfers between devices: 83.7 us -> 69.5 us
  other arithmetic: 5.53 us -> 1.33 us
  blocking collectives: 9.06 us -> 12.1 us
  local copies, waits for them, and re-layouts: 26.1 us -> 23.5 us
    dot_general x16 -> x0, matrix products: 31.1 us -> none  [the longest x5 14.5 us: gram(): jnp.einsum('qk,ypk->yqp', cg, row_g, preferred_element_type=jnp.float32)]
    pallas_call x0 -> x15, Pallas kernels: none -> 27 us  [the longest x14 25.6 us: call(): pl.pallas_call(body, out_shape=out, in_specs=[SMEM] + [VMEM] * (len(args)...]
    all_to_all x6 -> x4, waiting for transfers between devices: 21.5 us -> 5.23 us  [over_y(): return lax.all_to_all(t, 'y', 0, 0, tiled=True)]
    unnamed x45 -> x64, local copies, waits for them, and re-layouts: 3.51 us -> 18.7 us
    all_to_all x2 -> x1, starting transfers between devices: 18 us -> 6.19 us  [spread(): lax.all_to_all(jnp.broadcast_to(v, (count,) + v.shape), axes, 0, 0, tiled...]
    all_to_all x6 -> x4, starting transfers between devices: 25.4 us -> 16.5 us  [over_y(): return lax.all_to_all(t, 'y', 0, 0, tiled=True)]
    ppermute x5 -> x8, starting transfers between devices: 7.18 us -> 16.1 us  [swap_core(): return lax.ppermute(v, 'c', [(0, 1), (1, 0)])]
    squeeze x6 -> x0, local copies, waits for them, and re-layouts: 8.81 us -> none  [pair(): return (jnp.concatenate([a[0], b[0]]), jnp.concatenate([a[1], b[1]]))]
  transfers between devices with their start and end apart: 25 -> 25, of which waited for: 15 -> 12; matrix products, arithmetic and copies ran while one was open for 25% -> 1% of each run, Pallas kernels for 0% -> 13%
where the time goes in v3:
time: 191 us; the launch traced here: 190 us
  waiting for transfers between devices  69.5 us (36%)
  starting transfers between devices  55.7 us (29%)
  Pallas kernels  27 us (14%)
  local copies, waits for them, and re-layouts  23.5 us (12%)
  blocking collectives  12.1 us (6%)
    ppermute x8, waiting for transfers between devices, shift_z(): lax.ppermute(v, ('l', 'h'), [(z_slot(z), z_slot((z + d) % ZN)) for z in r...  35.3 us
    pallas_call x14, Pallas kernels, call(): pl.pallas_call(body, out_shape=out, in_specs=[SMEM] + [VMEM] * (len(args)...  25.6 us
    unnamed x64, local copies, waits for them, and re-layouts  18.7 us
    all_to_all x4, starting transfers between devices, over_y(): return lax.all_to_all(t, 'y', 0, 0, tiled=True)  16.5 us
    ppermute x8, starting transfers between devices, swap_core(): return lax.ppermute(v, 'c', [(0, 1), (1, 0)])  16.1 us
    ppermute x4, waiting for transfers between devices, shift_x(): return lax.ppermute(v, 'x', [(i, (i + d) % XN) for i in range(XN)])  14.8 us
    all_to_all x1, blocking collectives, shards(): got = lax.all_to_all(sent, ('x', 'c'), 0, 0, tiled=True)  12.1 us
    ppermute x8, starting transfers between devices, shift_z(): lax.ppermute(v, ('l', 'h'), [(z_slot(z), z_slot((z + d) % ZN)) for z in r...  11.8 us
  transfers between devices with their start and end apart: 25, of which 12 were waited for; matrix products, arithmetic and copies ran while one was open for 1% of the time, Pallas kernels for 13%

profile of v3, /device:TPU:1, one launch (start us, length us, event | category | flops | bytes accessed | tf_op | source)
XLA Modules:
  0.0 190.1 jit_solution(10854757348695900883)
XLA Ops:
  0.7 1.1 copy-done.23
  1.8 1.0 copy-done.24
  2.8 0.9 copy-done.26
  3.8 0.9 shard_map.59
  4.6 3.3 %collective-permute-start = (bf16[40,64,128]{2,1,0:T(8,128)(2,1)S(1)}, bf16[40,64,128]{2,1,0:T(8,128)(2,1)S(1)}, u32[]{:S(2)}, u32[]{:S(2)}) collective-permute-start(bf16[40,64,128]{2,1,0:T(8,128)(2,1)S(1)} %get-tuple-element.32), channel_id=1, source_target_pairs={{0,16},{16,0},{1,17},{17,1},{2,18},{18,2},{3,19},{19,3},{4,20},{20... | collective-permute-start | bytes 1966088 | tf_op jit(solution)/shard_map/ppermute | solution.py:42
  8.0 1.7 collective-permute-done.got
  9.7 0.8 copy-done.31
  10.5 0.6 shard_map.60.refs_0_.refs_5_
  11.2 3.9 %collective-permute-start.2 = (bf16[41,128,128]{2,1,0:T(8,128)(2,1)S(1)}, bf16[41,128,128]{2,1,0:T(8,128)(2,1)S(1)}, u32[]{:S(2)}, u32[]{:S(2)}) collective-permute-start(bf16[41,128,128]{2,1,0:T(8,128)(2,1)S(1)} %shard_map.60.refs_0_.refs_5_), channel_id=1, source_target_pairs={{0,44},{32,0},{4,32},{36,4},{8,36},{40,8},{12,40},{44,12},{1,45},{... | collective-permute-start | bytes 4030472 | tf_op jit(solution)/shard_map/ppermute | solution.py:34
  15.1 1.2 collective-permute-start.3
  16.3 1.5 collective-permute-start.4
  17.8 26.8 %collective-permute-done.1.refs_6_.refs_1_ = bf16[41,128,128]{2,1,0:T(8,128)(2,1)S(1)} collective-permute-done((bf16[41,128,128]{2,1,0:T(8,128)(2,1)S(1)}, bf16[41,128,128]{2,1,0:T(8,128)(2,1)S(1)}, u32[]{:S(2)}, u32[]{:S(2)}) %collective-permute-start.1) | collective-permute-done | bytes 1343520 | tf_op jit(solution)/shard_map/ppermute | solution.py:34
  44.6 2.1 %collective-permute-done.3.refs_4_.refs_3_ = bf16[41,128,128]{2,1,0:T(8,128)(2,1)S(1)} collective-permute-done((bf16[41,128,128]{2,1,0:T(8,128)(2,1)S(1)}, bf16[41,128,128]{2,1,0:T(8,128)(2,1)S(1)}, u32[]{:S(2)}, u32[]{:S(2)}) %collective-permute-start.3) | collective-permute-done | bytes 1343520 | tf_op jit(solution)/shard_map/ppermute | solution.py:38
  46.7 2.4 %collective-permute-start.6 = (bf16[21,128,128]{2,1,0:T(8,128)(2,1)S(1)}, bf16[21,128,128]{2,1,0:T(8,128)(2,1)S(1)}, u32[]{:S(2)}, u32[]{:S(2)}) collective-permute-start(bf16[21,128,128]{2,1,0:T(8,128)(2,1)S(1)} %slice.19), channel_id=1, source_target_pairs={{0,192},{64,0},{128,64},{192,128},{1,193},{65,1},{129,65},{193,129... | collective-permute-start | bytes 2064392 | tf_op jit(solution)/shard_map/ppermute | solution.py:38
  49.4 2.7 %collective-permute-start.8 = (bf16[41,128,128]{2,1,0:T(8,128)(2,1)S(1)}, bf16[41,128,128]{2,1,0:T(8,128)(2,1)}, u32[]{:S(2)}, u32[]{:S(2)}) collective-permute-start(bf16[41,128,128]{2,1,0:T(8,128)(2,1)S(1)} %collective-permute-done.2.refs_7_.refs_2_), channel_id=1, source_target_pairs={{0,44},{32,0},{4,32},{36,4},{8,36},{40,8},{12,40},{44,12},{1,45},{... | collective-permute-start | bytes 4030472 | tf_op jit(solution)/shard_map/ppermute | solution.py:34
  52.1 12.6 %collective-permute-done.5.refs_2_ = bf16[20,128,128]{2,1,0:T(8,128)(2,1)S(1)} collective-permute-done((bf16[20,128,128]{2,1,0:T(8,128)(2,1)S(1)}, bf16[20,128,128]{2,1,0:T(8,128)(2,1)S(1)}, u32[]{:S(2)}, u32[]{:S(2)}) %collective-permute-start.5) | collective-permute-done | bytes 655392 | tf_op jit(solution)/shard_map/ppermute | solution.py:38
  64.7 2.8 %shard_map.61 = (f32[4,3,192,128]{3,2,1,0:T(8,128)S(1)}, f32[4,3,192,128]{3,2,1,0:T(8,128)S(1)}) custom-call(s32[3]{0:T(128)S(1)} %pad_add_fusion.place, bf16[41,128,128]{2,1,0:T(8,128)(2,1)S(1)} %shard_map.60.refs_0_.refs_5_, bf16[41,128,128]{2,1,0:T(8,128)(2,1)S(1)} %collective-permute-done.4.refs_1_, ...), custom_call_target="tpu_custom_call" | custom-call | tf_op jit(solution)/shard_map/pallas_call | solution.py:60
  67.5 1.1 copy-done.4
  68.6 1.1 copy-done.14
  69.7 1.1 copy-done.16
  70.8 3.0 %collective-permute-start.9 = (f32[4,3,192,128]{3,2,1,0:T(8,128)S(1)}, f32[4,3,192,128]{3,2,1,0:T(8,128)S(1)}, u32[]{:S(2)}, u32[]{:S(2)}) collective-permute-start(f32[4,3,192,128]{3,2,1,0:T(8,128)S(1)} %get-tuple-element.38), channel_id=1, source_target_pairs={{0,16},{16,0},{1,17},{17,1},{2,18},{18,2},{3,19},{19,3},{4,20},{20... | collective-permute-start | bytes 3538952 | tf_op jit(solution)/shard_map/ppermute | solution.py:42
  73.7 2.5 %collective-permute-done.9.refs_0_ = f32[4,3,192,128]{3,2,1,0:T(8,128)S(1)} collective-permute-done((f32[4,3,192,128]{3,2,1,0:T(8,128)S(1)}, f32[4,3,192,128]{3,2,1,0:T(8,128)S(1)}, u32[]{:S(2)}, u32[]{:S(2)}) %collective-permute-start.9) | collective-permute-done | bytes 1179680 | tf_op jit(solution)/shard_map/ppermute | solution.py:42
  76.2 0.7 shard_map.62
  76.9 1.0 copy-done.18
  77.9 1.6 collective-permute-done.7.refs_5_.refs_0_
  79.6 2.7 %collective-permute-start.11 = (bf16[41,128,128]{2,1,0:T(8,128)(2,1)}, bf16[41,128,128]{2,1,0:T(8,128)(2,1)}, u32[]{:S(2)}, u32[]{:S(2)}) collective-permute-start(bf16[41,128,128]{2,1,0:T(8,128)(2,1)} %collective-permute-done.8.refs_6_.refs_1_), channel_id=1, source_target_pairs={{0,44},{32,0},{4,32},{36,4},{8,36},{40,8},{12,40},{44,12},{1,45},{... | collective-permute-start | bytes 4030472 | tf_op jit(solution)/shard_map/ppermute | solution.py:34
  82.2 4.3 %all-to-all-start = ((f32[4,3,192,128]{3,2,1,0:T(8,128)}), f32[4,3,192,128]{3,2,1,0:T(8,128)}, u32[]{:S(2)}, u32[]{:S(2)}) async-start(f32[4,3,192,128]{3,2,1,0:T(8,128)} %copy-done.18), calls=%async_computation | async-start | bytes 2359296 | tf_op jit(solution)/shard_map/all_to_all | solution.py:50
  86.6 1.3 copy-done.5
  87.9 1.1 copy-done.11
  89.0 4.2 %shard_map.63 = (f32[4,3,128,128]{3,2,1,0:T(8,128)S(1)}, f32[4,3,128,128]{3,2,1,0:T(8,128)}) custom-call(s32[3]{0:T(128)S(1)} %pad_add_fusion.place, bf16[41,128,128]{2,1,0:T(8,128)(2,1)S(1)} %shard_map.60.refs_0_.refs_5_, bf16[41,128,128]{2,1,0:T(8,128)(2,1)S(1)} %collective-permute-done.4.refs_1_, bf16[20,128,128]{2,1,0:T(8,128)(2,1)S(1)} %copy-done.11, ...), custom_call_target="tpu_custom_call" | custom-call | tf_op jit(solution)/shard_map/pallas_call | solution.py:60
  93.2 0.9 copy-done.21
  94.1 3.8 %collective-permute-start.12 = (f32[4,3,128,128]{3,2,1,0:T(8,128)}, f32[4,3,128,128]{3,2,1,0:T(8,128)S(1)}, u32[]{:S(2)}, u32[]{:S(2)}) collective-permute-start(f32[4,3,128,128]{3,2,1,0:T(8,128)} %get-tuple-element.43), channel_id=1, source_target_pairs={{0,16},{16,0},{1,17},{17,1},{2,18},{18,2},{3,19},{19,3},{4,20},{20... | collective-permute-start | bytes 2359304 | tf_op jit(solution)/shard_map/ppermute | solution.py:42
  97.9 1.5 shard_map.65.own
  100.0 0.6 shard_map.64
  100.7 0.9 copy-done.19
  101.5 0.6 copy-done.27
  102.2 6.8 %collective-permute-done.10.refs_5_.refs_0_ = bf16[41,128,128]{2,1,0:T(8,128)(2,1)} collective-permute-done((bf16[41,128,128]{2,1,0:T(8,128)(2,1)}, bf16[41,128,128]{2,1,0:T(8,128)(2,1)}, u32[]{:S(2)}, u32[]{:S(2)}) %collective-permute-start.10) | collective-permute-done | bytes 1343520 | tf_op jit(solution)/shard_map/ppermute | solution.py:34
  109.0 2.1 %slice.21 = bf16[21,128,128]{2,1,0:T(8,128)(2,1)} slice(bf16[41,128,128]{2,1,0:T(8,128)(2,1)} %collective-permute-done.11.refs_6_.refs_1_), slice={[20:41], [0:128], [0:128]} | slice | bytes 1376256 | tf_op jit(solution)/shard_map/slice | solution.py:276
  111.1 2.4 %collective-permute-start.15 = (bf16[21,128,128]{2,1,0:T(8,128)(2,1)}, bf16[21,128,128]{2,1,0:T(8,128)(2,1)}, u32[]{:S(2)}, u32[]{:S(2)}) collective-permute-start(bf16[21,128,128]{2,1,0:T(8,128)(2,1)} %slice.21), channel_id=1, source_target_pairs={{0,44},{32,0},{4,32},{36,4},{8,36},{40,8},{12,40},{44,12},{1,45},{... | collective-permute-start | bytes 2064392 | tf_op jit(solution)/shard_map/ppermute | solution.py:34
  113.5 2.0 %slice.20 = bf16[20,128,128]{2,1,0:T(8,128)(2,1)} slice(bf16[41,128,128]{2,1,0:T(8,128)(2,1)} %collective-permute-done.10.refs_5_.refs_0_), slice={[0:20], [0:128], [0:128]} | slice | bytes 1310720 | tf_op jit(solution)/shard_map/slice | solution.py:276
  115.5 4.2 %all-to-all-start.1 = ((f32[4,3,128,128]{3,2,1,0:T(8,128)}), f32[4,3,128,128]{3,2,1,0:T(8,128)}, u32[]{:S(2)}, u32[]{:S(2)}) async-start(f32[4,3,128,128]{3,2,1,0:T(8,128)} %copy-done.19), calls=%async_computation.1 | async-start | bytes 1572864 | tf_op jit(solution)/shard_map/all_to_all | solution.py:50
  119.8 1.3 copy-done.6
  121.1 1.1 copy-done.12
  122.2 3.4 %shard_map.66 = (f32[4,3,128,128]{3,2,1,0:T(8,128)S(1)}, f32[4,1,128,128]{3,2,1,0:T(8,128)S(1)}, f32[4,1,128,128]{3,2,1,0:T(8,128)S(1)}, f32[4,1,128,128]{3,2,1,0:T(8,128)S(1)}) custom-call(s32[3]{0:T(128)S(1)} %copy-done.30, bf16[41,128,128]{2,1,0:T(8,128)(2,1)S(1)} %copy-done.1, bf16[41,128,128]{2,1,0:T(8,128)(2,1)S(1)} %copy-done.3, ...), custom_call_target="tpu_custom_call" | custom-call | tf_op jit(solution)/shard_map/pallas_call | solution.py:60
  125.6 4.9 %collective-permute-start.16 = (f32[4,1,128,128]{3,2,1,0:T(8,128)S(1)}, f32[4,1,128,128]{3,2,1,0:T(8,128)S(1)}, u32[]{:S(2)}, u32[]{:S(2)}) collective-permute-start(f32[4,1,128,128]{3,2,1,0:T(8,128)S(1)} %get-tuple-element.48), channel_id=1, source_target_pairs={{0,16},{16,0},{1,17},{17,1},{2,18},{18,2},{3,19},{19,3},{4,20},{20... | collective-permute-start | bytes 786440 | tf_op jit(solution)/shard_map/ppermute | solution.py:42
  131.0 1.5 shard_map.68.p1
  132.5 0.7 shard_map.67
  133.2 0.9 copy-done.20
  134.1 4.5 %all-to-all-start.3 = ((f32[4,3,128,128]{3,2,1,0:T(8,128)}), f32[4,3,128,128]{3,2,1,0:T(8,128)}, u32[]{:S(2)}, u32[]{:S(2)}) async-start(f32[4,3,128,128]{3,2,1,0:T(8,128)} %copy-done.20), calls=%async_computation.3 | async-start | bytes 1572864 | tf_op jit(solution)/shard_map/all_to_all | solution.py:50
  138.6 1.3 copy-done.7
  139.9 1.1 copy-done.13
  141.0 3.1 %shard_map.69 = (f32[4,3,64,128]{3,2,1,0:T(8,128)S(1)}, f32[4,3,64,128]{3,2,1,0:T(8,128)S(1)}) custom-call(s32[3]{0:T(128)S(1)} %copy-done.30, bf16[41,128,128]{2,1,0:T(8,128)(2,1)S(1)} %copy-done.1, bf16[41,128,128]{2,1,0:T(8,128)(2,1)S(1)} %copy-done.3, bf16[20,128,128]{2,1,0:T(8,128)(2,1)S(1)} %copy-done.13, bf16[21,128,128]{2,1,0:T(8,128)(2,1)S(1)} %copy-done.9, ...), custom_call_target="tpu_custom_call" | custom-call | tf_op jit(solution)/shard_map/pallas_call | solution.py:60
  144.7 1.3 collective-permute-done.19.refs_0_
  146.1 1.3 shard_map.70
  147.4 3.2 %all-to-all-done.3.s = f32[4,3,128,128]{3,2,1,0:T(8,128)} async-done(((f32[4,3,128,128]{3,2,1,0:T(8,128)}), f32[4,3,128,128]{3,2,1,0:T(8,128)}, u32[]{:S(2)}, u32[]{:S(2)}) %all-to-all-start.3) | async-done | bytes 786464 | tf_op jit(solution)/shard_map/all_to_all | solution.py:50
  150.6 3.5 %all-to-all-start.2 = ((f32[4,3,64,128]{3,2,1,0:T(8,128)}), f32[4,3,64,128]{3,2,1,0:T(8,128)S(1)}, u32[]{:S(2)}, u32[]{:S(2)}) async-start(f32[4,3,64,128]{3,2,1,0:T(8,128)} %shard_map.70), calls=%async_computation.2 | async-start | bytes 786432 | tf_op jit(solution)/shard_map/all_to_all | solution.py:50
  154.1 2.2 %shard_map.71.p2 = f32[128,256]{1,0:T(8,128)S(1)} custom-call(s32[3]{0:T(128)S(1)} %copy-done.30, f32[4,3,128,128]{3,2,1,0:T(8,128)} %all-to-all-done.1.s, bf16[41,128,128]{2,1,0:T(8,128)(2,1)} %collective-permute-done.7.refs_5_.refs_0_, bf16[41,128,128]{2,1,0:T(8,128)(2,1)} %collective-permute-done.8.refs_6_.refs_1_), custom_call_target="tpu_custom_call" | custom-call | tf_op jit(solution)/shard_map/pallas_call | solution.py:60
  156.3 2.2 %shard_map.72.p3 = f32[128,256]{1,0:T(8,128)S(1)} custom-call(s32[3]{0:T(128)S(1)} %copy-done.30, f32[4,3,128,128]{3,2,1,0:T(8,128)} %all-to-all-done.3.s, bf16[41,128,128]{2,1,0:T(8,128)(2,1)} %collective-permute-done.10.refs_5_.refs_0_, bf16[41,128,128]{2,1,0:T(8,128)(2,1)} %collective-permute-done.11.refs_6_.refs_1_), custom_call_target="tpu_custom_call" | custom-call | tf_op jit(solution)/shard_map/pallas_call | solution.py:60
  158.6 2.0 %all-to-all-done.2.s = f32[4,3,64,128]{3,2,1,0:T(8,128)S(1)} async-done(((f32[4,3,64,128]{3,2,1,0:T(8,128)}), f32[4,3,64,128]{3,2,1,0:T(8,128)S(1)}, u32[]{:S(2)}, u32[]{:S(2)}) %all-to-all-start.2) | async-done | bytes 393248 | tf_op jit(solution)/shard_map/all_to_all | solution.py:50
  160.5 1.3 shard_map.73
  161.9 12.1 %all_to_all.30 = f32[8,24,256]{2,1,0:T(8,128)S(1)} all-to-all(f32[8,24,256]{2,1,0:T(8,128)S(1)} %shard_map.73), channel_id=1, replica_groups=mesh['x'=4,'l'=2,'c'=2,'h'=4,'y'=4] {'x','c'}, dimensions={0} | all-to-all | bytes 393216 | tf_op jit(solution)/shard_map/all_to_all | solution.py:293
  174.0 0.6 broadcast_in_dim.4
  174.6 6.2 %all-to-all-start.5 = ((f32[32,1,256]{2,1,0:T(1,128)}), f32[32,1,256]{2,1,0:T(1,128)S(1)}, u32[]{:S(2)}, u32[]{:S(2)}) async-start(f32[32,1,256]{2,1,0:T(1,128)} %broadcast_in_dim.4), calls=%async_computation.5 | async-start | bytes 65536 | tf_op jit(solution)/shard_map/all_to_all | solution.py:46
  181.4 8.1 %all-to-all-done.5 = f32[32,1,256]{2,1,0:T(1,128)S(1)} async-done(((f32[32,1,256]{2,1,0:T(1,128)}), f32[32,1,256]{2,1,0:T(1,128)S(1)}, u32[]{:S(2)}, u32[]{:S(2)}) %all-to-all-start.5) | async-done | bytes 32800 | tf_op jit(solution)/shard_map/all_to_all | solution.py:46
  (75 shorter events, 3.6 us)
Async XLA Ops:
  0.7 1.1 copy-start.23
  1.8 1.0 copy-start.24
  2.8 0.9 copy-start.26
  3.7 82.8 %copy-start.29 = (s32[3]{0:T(128)}, s32[3]{0:T(128)S(1)}, u32[]{:S(2)}) copy-start(s32[3]{0:T(128)S(1)} %pad_add_fusion.place) | copy-start | bytes 40
  4.6 5.1 %collective-permute-start = (bf16[40,64,128]{2,1,0:T(8,128)(2,1)S(1)}, bf16[40,64,128]{2,1,0:T(8,128)(2,1)S(1)}, u32[]{:S(2)}, u32[]{:S(2)}) collective-permute-start(bf16[40,64,128]{2,1,0:T(8,128)(2,1)S(1)} %get-tuple-element.32), channel_id=1, source_target_pairs={{0,16},{16,0},{1,17},{17,1},{2,18},{18,2},{3,19},{19,3},{4,20},{20... | collective-permute-start | bytes 1966088 | tf_op jit(solution)/shard_map/ppermute | solution.py:42
  9.7 0.8 copy-start.31
  11.1 75.5 %copy-start = (bf16[41,128,128]{2,1,0:T(8,128)(2,1)}, bf16[41,128,128]{2,1,0:T(8,128)(2,1)S(1)}, u32[]{:S(2)}) copy-start(bf16[41,128,128]{2,1,0:T(8,128)(2,1)S(1)} %shard_map.60.refs_0_.refs_5_) | copy-start | bytes 4030468
  11.1 33.5 %collective-permute-start.1 = (bf16[41,128,128]{2,1,0:T(8,128)(2,1)S(1)}, bf16[41,128,128]{2,1,0:T(8,128)(2,1)S(1)}, u32[]{:S(2)}, u32[]{:S(2)}) collective-permute-start(bf16[41,128,128]{2,1,0:T(8,128)(2,1)S(1)} %shard_map.60.refs_0_.refs_5_), channel_id=1, source_target_pairs={{0,32},{32,4},{4,36},{36,8},{8,40},{40,12},{12,44},{44,0},{1,33},{... | collective-permute-start | bytes 4030472 | tf_op jit(solution)/shard_map/ppermute | solution.py:34
  11.2 33.4 %collective-permute-start.2 = (bf16[41,128,128]{2,1,0:T(8,128)(2,1)S(1)}, bf16[41,128,128]{2,1,0:T(8,128)(2,1)S(1)}, u32[]{:S(2)}, u32[]{:S(2)}) collective-permute-start(bf16[41,128,128]{2,1,0:T(8,128)(2,1)S(1)} %shard_map.60.refs_0_.refs_5_), channel_id=1, source_target_pairs={{0,44},{32,0},{4,32},{36,4},{8,36},{40,8},{12,40},{44,12},{1,45},{... | collective-permute-start | bytes 4030472 | tf_op jit(solution)/shard_map/ppermute | solution.py:34
  15.1 31.6 %collective-permute-start.3 = (bf16[41,128,128]{2,1,0:T(8,128)(2,1)S(1)}, bf16[41,128,128]{2,1,0:T(8,128)(2,1)S(1)}, u32[]{:S(2)}, u32[]{:S(2)}) collective-permute-start(bf16[41,128,128]{2,1,0:T(8,128)(2,1)S(1)} %shard_map.60.refs_0_.refs_5_), channel_id=1, source_target_pairs={{0,64},{64,128},{128,192},{192,0},{1,65},{65,129},{129,193},{193,1... | collective-permute-start | bytes 4030472 | tf_op jit(solution)/shard_map/ppermute | solution.py:38
  16.3 30.4 %collective-permute-start.4 = (bf16[41,128,128]{2,1,0:T(8,128)(2,1)S(1)}, bf16[41,128,128]{2,1,0:T(8,128)(2,1)S(1)}, u32[]{:S(2)}, u32[]{:S(2)}) collective-permute-start(bf16[41,128,128]{2,1,0:T(8,128)(2,1)S(1)} %shard_map.60.refs_0_.refs_5_), channel_id=1, source_target_pairs={{0,192},{64,0},{128,64},{192,128},{1,193},{65,1},{129,65},{193,129... | collective-permute-start | bytes 4030472 | tf_op jit(solution)/shard_map/ppermute | solution.py:38
  46.7 39.9 %copy-start.2 = (bf16[41,128,128]{2,1,0:T(8,128)(2,1)}, bf16[41,128,128]{2,1,0:T(8,128)(2,1)S(1)}, u32[]{:S(2)}) copy-start(bf16[41,128,128]{2,1,0:T(8,128)(2,1)S(1)} %collective-permute-done.4.refs_1_) | copy-start | bytes 4030468
  46.7 18.0 %collective-permute-start.6 = (bf16[21,128,128]{2,1,0:T(8,128)(2,1)S(1)}, bf16[21,128,128]{2,1,0:T(8,128)(2,1)S(1)}, u32[]{:S(2)}, u32[]{:S(2)}) collective-permute-start(bf16[21,128,128]{2,1,0:T(8,128)(2,1)S(1)} %slice.19), channel_id=1, source_target_pairs={{0,192},{64,0},{128,64},{192,128},{1,193},{65,1},{129,65},{193,129... | collective-permute-start | bytes 2064392 | tf_op jit(solution)/shard_map/ppermute | solution.py:38
  49.2 15.5 %collective-permute-start.5 = (bf16[20,128,128]{2,1,0:T(8,128)(2,1)S(1)}, bf16[20,128,128]{2,1,0:T(8,128)(2,1)S(1)}, u32[]{:S(2)}, u32[]{:S(2)}) collective-permute-start(bf16[20,128,128]{2,1,0:T(8,128)(2,1)S(1)} %slice.18), channel_id=1, source_target_pairs={{0,64},{64,128},{128,192},{192,0},{1,65},{65,129},{129,193},{193,1... | collective-permute-start | bytes 1966088 | tf_op jit(solution)/shard_map/ppermute | solution.py:38
  49.3 30.2 %collective-permute-start.7 = (bf16[41,128,128]{2,1,0:T(8,128)(2,1)S(1)}, bf16[41,128,128]{2,1,0:T(8,128)(2,1)}, u32[]{:S(2)}, u32[]{:S(2)}) collective-permute-start(bf16[41,128,128]{2,1,0:T(8,128)(2,1)S(1)} %collective-permute-done.1.refs_6_.refs_1_), channel_id=1, source_target_pairs={{0,32},{32,4},{4,36},{36,8},{8,40},{40,12},{12,44},{44,0},{1,33},{... | collective-permute-start | bytes 4030472 | tf_op jit(solution)/shard_map/ppermute | solution.py:34
  49.4 30.1 %collective-permute-start.8 = (bf16[41,128,128]{2,1,0:T(8,128)(2,1)S(1)}, bf16[41,128,128]{2,1,0:T(8,128)(2,1)}, u32[]{:S(2)}, u32[]{:S(2)}) collective-permute-start(bf16[41,128,128]{2,1,0:T(8,128)(2,1)S(1)} %collective-permute-done.2.refs_7_.refs_2_), channel_id=1, source_target_pairs={{0,44},{32,0},{4,32},{36,4},{8,36},{40,8},{12,40},{44,12},{1,45},{... | collective-permute-start | bytes 4030472 | tf_op jit(solution)/shard_map/ppermute | solution.py:34
  64.7 2.8 %copy-start.10 = (bf16[20,128,128]{2,1,0:T(8,128)(2,1)}, bf16[20,128,128]{2,1,0:T(8,128)(2,1)S(1)}, u32[]{:S(2)}) copy-start(bf16[20,128,128]{2,1,0:T(8,128)(2,1)S(1)} %collective-permute-done.5.refs_2_) | copy-start | bytes 1966084
  64.7 21.8 %copy-start.8 = (bf16[21,128,128]{2,1,0:T(8,128)(2,1)}, bf16[21,128,128]{2,1,0:T(8,128)(2,1)S(1)}, u32[]{:S(2)}) copy-start(bf16[21,128,128]{2,1,0:T(8,128)(2,1)S(1)} %collective-permute-done.6.refs_3_.refs_2_) | copy-start | bytes 2064388
  67.5 1.1 copy-start.4
  68.6 1.1 copy-start.14
  69.7 1.1 copy-start.16
  70.8 5.4 %collective-permute-start.9 = (f32[4,3,192,128]{3,2,1,0:T(8,128)S(1)}, f32[4,3,192,128]{3,2,1,0:T(8,128)S(1)}, u32[]{:S(2)}, u32[]{:S(2)}) collective-permute-start(f32[4,3,192,128]{3,2,1,0:T(8,128)S(1)} %get-tuple-element.38), channel_id=1, source_target_pairs={{0,16},{16,0},{1,17},{17,1},{2,18},{18,2},{3,19},{19,3},{4,20},{20... | collective-permute-start | bytes 3538952 | tf_op jit(solution)/shard_map/ppermute | solution.py:42
  76.9 1.0 copy-start.18
  79.6 29.4 %collective-permute-start.10 = (bf16[41,128,128]{2,1,0:T(8,128)(2,1)}, bf16[41,128,128]{2,1,0:T(8,128)(2,1)}, u32[]{:S(2)}, u32[]{:S(2)}) collective-permute-start(bf16[41,128,128]{2,1,0:T(8,128)(2,1)} %collective-permute-done.7.refs_5_.refs_0_), channel_id=1, source_target_pairs={{0,32},{32,4},{4,36},{36,8},{8,40},{40,12},{12,44},{44,0},{1,33},{... | collective-permute-start | bytes 4030472 | tf_op jit(solution)/shard_map/ppermute | solution.py:34
  79.6 29.4 %collective-permute-start.11 = (bf16[41,128,128]{2,1,0:T(8,128)(2,1)}, bf16[41,128,128]{2,1,0:T(8,128)(2,1)}, u32[]{:S(2)}, u32[]{:S(2)}) collective-permute-start(bf16[41,128,128]{2,1,0:T(8,128)(2,1)} %collective-permute-done.8.refs_6_.refs_1_), channel_id=1, source_target_pairs={{0,44},{32,0},{4,32},{36,4},{8,36},{40,8},{12,40},{44,12},{1,45},{... | collective-permute-start | bytes 4030472 | tf_op jit(solution)/shard_map/ppermute | solution.py:34
  82.2 20.0 %all-to-all-start = ((f32[4,3,192,128]{3,2,1,0:T(8,128)}), f32[4,3,192,128]{3,2,1,0:T(8,128)}, u32[]{:S(2)}, u32[]{:S(2)}) async-start(f32[4,3,192,128]{3,2,1,0:T(8,128)} %copy-done.18), calls=%async_computation | async-start | bytes 2359296 | tf_op jit(solution)/shard_map/all_to_all | solution.py:50
  86.6 1.3 copy-start.5
  87.9 1.1 copy-start.11
  93.2 0.9 copy-start.21
  94.1 5.9 %copy-start.22 = (f32[4,3,128,128]{3,2,1,0:T(8,128)S(1)}, f32[4,3,128,128]{3,2,1,0:T(8,128)}, u32[]{:S(2)}) copy-start(f32[4,3,128,128]{3,2,1,0:T(8,128)} %copy-done.21) | copy-start | bytes 2359300
  94.1 5.9 %copy-start.30 = (s32[3]{0:T(128)S(1)}, s32[3]{0:T(128)}, u32[]{:S(2)}) copy-start(s32[3]{0:T(128)} %copy-done.29) | copy-start | bytes 40
  94.1 5.9 %collective-permute-start.12 = (f32[4,3,128,128]{3,2,1,0:T(8,128)}, f32[4,3,128,128]{3,2,1,0:T(8,128)S(1)}, u32[]{:S(2)}, u32[]{:S(2)}) collective-permute-start(f32[4,3,128,128]{3,2,1,0:T(8,128)} %get-tuple-element.43), channel_id=1, source_target_pairs={{0,16},{16,0},{1,17},{17,1},{2,18},{18,2},{3,19},{19,3},{4,20},{20... | collective-permute-start | bytes 2359304 | tf_op jit(solution)/shard_map/ppermute | solution.py:42
  99.4 2.2 %collective-permute-start.13 = (bf16[4,128,128]{2,1,0:T(8,128)(2,1)}, bf16[4,128,128]{2,1,0:T(8,128)(2,1)S(1)}, u32[]{:S(2)}, u32[]{:S(2)}) collective-permute-start(bf16[4,128,128]{2,1,0:T(8,128)(2,1)} %shard_map.65.own), channel_id=1, source_target_pairs={{0,16},{16,0},{1,17},{17,1},{2,18},{18,2},{3,19},{19,3},{4,20},{20... | collective-permute-start | bytes 393224 | tf_op jit(solution)/shard_map/ppermute | solution.py:42
  100.6 0.9 copy-start.19
  101.5 0.7 copy-start.27
  109.0 10.7 %copy-start.9 = (bf16[21,128,128]{2,1,0:T(8,128)(2,1)S(1)}, bf16[21,128,128]{2,1,0:T(8,128)(2,1)}, u32[]{:S(2)}) copy-start(bf16[21,128,128]{2,1,0:T(8,128)(2,1)} %copy-done.8) | copy-start | bytes 2064388
  111.1 8.6 %copy-start.1 = (bf16[41,128,128]{2,1,0:T(8,128)(2,1)S(1)}, bf16[41,128,128]{2,1,0:T(8,128)(2,1)}, u32[]{:S(2)}) copy-start(bf16[41,128,128]{2,1,0:T(8,128)(2,1)} %copy-done) | copy-start | bytes 4030468
  111.1 8.6 %copy-start.3 = (bf16[41,128,128]{2,1,0:T(8,128)(2,1)S(1)}, bf16[41,128,128]{2,1,0:T(8,128)(2,1)}, u32[]{:S(2)}) copy-start(bf16[41,128,128]{2,1,0:T(8,128)(2,1)} %copy-done.2) | copy-start | bytes 4030468
  111.1 23.0 %collective-permute-start.15 = (bf16[21,128,128]{2,1,0:T(8,128)(2,1)}, bf16[21,128,128]{2,1,0:T(8,128)(2,1)}, u32[]{:S(2)}, u32[]{:S(2)}) collective-permute-start(bf16[21,128,128]{2,1,0:T(8,128)(2,1)} %slice.21), channel_id=1, source_target_pairs={{0,44},{32,0},{4,32},{36,4},{8,36},{40,8},{12,40},{44,12},{1,45},{... | collective-permute-start | bytes 2064392 | tf_op jit(solution)/shard_map/ppermute | solution.py:34
  115.5 18.6 %collective-permute-start.14 = (bf16[20,128,128]{2,1,0:T(8,128)(2,1)}, bf16[20,128,128]{2,1,0:T(8,128)(2,1)}, u32[]{:S(2)}, u32[]{:S(2)}) collective-permute-start(bf16[20,128,128]{2,1,0:T(8,128)(2,1)} %slice.20), channel_id=1, source_target_pairs={{0,32},{32,4},{4,36},{36,8},{8,40},{40,12},{12,44},{44,0},{1,33},{... | collective-permute-start | bytes 1966088 | tf_op jit(solution)/shard_map/ppermute | solution.py:34
  115.5 18.6 %all-to-all-start.1 = ((f32[4,3,128,128]{3,2,1,0:T(8,128)}), f32[4,3,128,128]{3,2,1,0:T(8,128)}, u32[]{:S(2)}, u32[]{:S(2)}) async-start(f32[4,3,128,128]{3,2,1,0:T(8,128)} %copy-done.19), calls=%async_computation.1 | async-start | bytes 1572864 | tf_op jit(solution)/shard_map/all_to_all | solution.py:50
  119.8 1.3 copy-start.6
  121.1 1.1 copy-start.12
  122.2 8.8 %copy-start.15 = (bf16[41,128,128]{2,1,0:T(8,128)(2,1)S(1)}, bf16[41,128,128]{2,1,0:T(8,128)(2,1)}, u32[]{:S(2)}) copy-start(bf16[41,128,128]{2,1,0:T(8,128)(2,1)} %copy-done.14) | copy-start | bytes 4030468
  122.2 8.8 %copy-start.17 = (bf16[41,128,128]{2,1,0:T(8,128)(2,1)S(1)}, bf16[41,128,128]{2,1,0:T(8,128)(2,1)}, u32[]{:S(2)}) copy-start(bf16[41,128,128]{2,1,0:T(8,128)(2,1)} %copy-done.16) | copy-start | bytes 4030468
  125.6 6.9 %collective-permute-start.16 = (f32[4,1,128,128]{3,2,1,0:T(8,128)S(1)}, f32[4,1,128,128]{3,2,1,0:T(8,128)S(1)}, u32[]{:S(2)}, u32[]{:S(2)}) collective-permute-start(f32[4,1,128,128]{3,2,1,0:T(8,128)S(1)} %get-tuple-element.48), channel_id=1, source_target_pairs={{0,16},{16,0},{1,17},{17,1},{2,18},{18,2},{3,19},{19,3},{4,20},{20... | collective-permute-start | bytes 786440 | tf_op jit(solution)/shard_map/ppermute | solution.py:42
  130.5 2.1 %collective-permute-start.17 = (f32[4,1,128,128]{3,2,1,0:T(8,128)S(1)}, f32[4,1,128,128]{3,2,1,0:T(8,128)S(1)}, u32[]{:S(2)}, u32[]{:S(2)}) collective-permute-start(f32[4,1,128,128]{3,2,1,0:T(8,128)S(1)} %get-tuple-element.49), channel_id=1, source_target_pairs={{0,16},{16,0},{1,17},{17,1},{2,18},{18,2},{3,19},{19,3},{4,20},{20... | collective-permute-start | bytes 786440 | tf_op jit(solution)/shard_map/ppermute | solution.py:42
  130.6 2.0 %collective-permute-start.18 = (f32[4,1,128,128]{3,2,1,0:T(8,128)S(1)}, f32[4,1,128,128]{3,2,1,0:T(8,128)S(1)}, u32[]{:S(2)}, u32[]{:S(2)}) collective-permute-start(f32[4,1,128,128]{3,2,1,0:T(8,128)S(1)} %get-tuple-element.50), channel_id=1, source_target_pairs={{0,16},{16,0},{1,17},{17,1},{2,18},{18,2},{3,19},{19,3},{4,20},{20... | collective-permute-start | bytes 786440 | tf_op jit(solution)/shard_map/ppermute | solution.py:42
  133.2 0.9 copy-start.20
  134.1 16.5 %all-to-all-start.3 = ((f32[4,3,128,128]{3,2,1,0:T(8,128)}), f32[4,3,128,128]{3,2,1,0:T(8,128)}, u32[]{:S(2)}, u32[]{:S(2)}) async-start(f32[4,3,128,128]{3,2,1,0:T(8,128)} %copy-done.20), calls=%async_computation.3 | async-start | bytes 1572864 | tf_op jit(solution)/shard_map/all_to_all | solution.py:50
  138.6 1.3 copy-start.7
  139.9 1.1 copy-start.13
  144.1 1.9 %collective-permute-start.19 = (f32[4,3,64,128]{3,2,1,0:T(8,128)S(1)}, f32[4,3,64,128]{3,2,1,0:T(8,128)S(1)}, u32[]{:S(2)}, u32[]{:S(2)}) collective-permute-start(f32[4,3,64,128]{3,2,1,0:T(8,128)S(1)} %get-tuple-element.55), channel_id=1, source_target_pairs={{0,16},{16,0},{1,17},{17,1},{2,18},{18,2},{3,19},{19,3},{4,20},{20... | collective-permute-start | bytes 1179656 | tf_op jit(solution)/shard_map/ppermute | solution.py:42
  150.6 9.9 %all-to-all-start.2 = ((f32[4,3,64,128]{3,2,1,0:T(8,128)}), f32[4,3,64,128]{3,2,1,0:T(8,128)S(1)}, u32[]{:S(2)}, u32[]{:S(2)}) async-start(f32[4,3,64,128]{3,2,1,0:T(8,128)} %shard_map.70), calls=%async_computation.2 | async-start | bytes 786432 | tf_op jit(solution)/shard_map/all_to_all | solution.py:50
  156.3 4.2 %copy-start.25 = (bf16[4,128,128]{2,1,0:T(8,128)(2,1)S(1)}, bf16[4,128,128]{2,1,0:T(8,128)(2,1)}, u32[]{:S(2)}) copy-start(bf16[4,128,128]{2,1,0:T(8,128)(2,1)} %shard_map.65.own) | copy-start | bytes 393220
  156.3 4.2 %copy-start.28 = (bf16[4,128,128]{2,1,0:T(8,128)(2,1)S(1)}, bf16[4,128,128]{2,1,0:T(8,128)(2,1)}, u32[]{:S(2)}) copy-start(bf16[4,128,128]{2,1,0:T(8,128)(2,1)} %copy-done.27) | copy-start | bytes 393220
  174.6 14.9 %all-to-all-start.5 = ((f32[32,1,256]{2,1,0:T(1,128)}), f32[32,1,256]{2,1,0:T(1,128)S(1)}, u32[]{:S(2)}, u32[]{:S(2)}) async-start(f32[32,1,256]{2,1,0:T(1,128)} %broadcast_in_dim.4), calls=%async_computation.5 | async-start | bytes 65536 | tf_op jit(solution)/shard_map/all_to_all | solution.py:46

commit v4 on v3

--- a/solution.py
+++ b/solution.py
@@ -67,17 +67,21 @@
     )(*args)
 
 
-def pack_body(place, *refs):
-    parts, (kept, given) = refs[:-2], refs[-2:]
-    core = place[0]
+def pack_body(given, place, *refs):
+    parts, out = refs[:-1], refs[-1]
+    which = 1 - place[0] if given else place[0]
     slab = 0
     for ref in parts:
-        half = ref.shape[1] // 2
-        for i in range(half // LANES):
-            for out, which in ((kept, core), (given, 1 - core)):
-                start = pl.multiple_of(which * half + i * LANES, LANES)
-                out[slab] = ref[:, pl.ds(start, LANES)]
+        width = ref.shape[1] // 2
+        for i in range(width // LANES):
+            out[slab] = ref[:, pl.ds(pl.multiple_of(which * width + i * LANES, LANES), LANES)]
             slab += 1
+
+
+def pack(place, parts, given):
+    slabs = sum(v.shape[1] for v in parts) // (2 * LANES)
+    out = jax.ShapeDtypeStruct((slabs, parts[0].shape[0], LANES), parts[0].dtype)
+    return call(functools.partial(pack_body, given), out, (place,) + parts)
 
 
 def merge_body(place, kept, got, occ, out):
@@ -87,6 +91,34 @@
     out[:n, pl.ds(pl.multiple_of((1 - core) * points, points), points)] = got[...]
     out[n, :points] = occ[:, :LANES]
     out[n, points:] = occ[:, LANES:]
+
+
+def halves_body(half, place, a, b, first, second, sems):
+    copies = [
+        pltpu.make_async_copy(a.at[:half], first, sems.at[0]),
+        pltpu.make_async_copy(b.at[half:], second, sems.at[1]),
+    ]
+    for copy in copies:
+        copy.start()
+    for copy in copies:
+        copy.wait()
+
+
+def halves(half, place, a, b):
+    anywhere = pl.BlockSpec(memory_space=pl.ANY)
+    n = a.shape[0]
+    return pl.pallas_call(
+        functools.partial(halves_body, half),
+        out_shape=(
+            jax.ShapeDtypeStruct((half,) + a.shape[1:], a.dtype),
+            jax.ShapeDtypeStruct((n - half,) + a.shape[1:], a.dtype),
+        ),
+        in_specs=[SMEM, anywhere, anywhere],
+        out_specs=(VMEM, VMEM),
+        scratch_shapes=[pltpu.SemaphoreType.DMA((2,))],
+        cost_estimate=pl.CostEstimate(flops=0, bytes_accessed=0, transcendentals=0),
+        compiler_params=pltpu.CompilerParams(vmem_limit_bytes=32 * 1024 * 1024),
+    )(place, a, b)
 
 
 def tile_body(cuts, sizes, place, *refs):
@@ -166,30 +198,54 @@
     return call(add_body, jax.ShapeDtypeStruct(a.shape, a.dtype), (place, a) + others)
 
 
+def call_last(body, out, args, blocks):
+    def whole(v):
+        zeros = (0,) * len(v.shape)
+        return pl.BlockSpec(v.shape, lambda i: zeros)
+
+    def last(b):
+        at = b.shape[0] - 1
+        return pl.BlockSpec((1,) + b.shape[1:], lambda i: (at, 0, 0))
+
+    return pl.pallas_call(
+        body,
+        out_shape=out,
+        grid=(1,),
+        in_specs=[SMEM] + [whole(v) for v in args[1:]] + [last(b) for b in blocks],
+        out_specs=whole(out),
+        cost_estimate=pl.CostEstimate(flops=0, bytes_accessed=0, transcendentals=0),
+        compiler_params=pltpu.CompilerParams(vmem_limit_bytes=32 * 1024 * 1024),
+    )(*args, *blocks)
+
+
 def orbitals_body(place, *refs):
     for i, ref in enumerate(refs[:-1]):
         refs[-1][i] = ref[0]
 
 
 def orbitals(place, blocks):
-    n, width = len(blocks), blocks[0].shape[1:]
-
-    def last(b):
-        at = b.shape[0] - 1
-        return pl.BlockSpec((1,) + width, lambda i: (at, 0, 0))
-
-    return pl.pallas_call(
-        orbitals_body,
-        out_shape=jax.ShapeDtypeStruct((n,) + width, blocks[0].dtype),
-        grid=(1,),
-        in_specs=[SMEM] + [last(b) for b in blocks],
-        out_specs=pl.BlockSpec((n,) + width, lambda i: (0, 0, 0)),
-        cost_estimate=pl.CostEstimate(flops=0, bytes_accessed=0, transcendentals=0),
-    )(place, *blocks)
+    out = jax.ShapeDtypeStruct((len(blocks),) + blocks[0].shape[1:], blocks[0].dtype)
+    return call_last(orbitals_body, out, (place,), blocks)
+
+
+def shift_y(v, d):
+    return lax.ppermute(v, "y", [(i, (i + d) % YN) for i in range(YN)])
+
+
+def add_ring_body(place, a, b, *outs):
+    for k, out in enumerate(outs):
+        i = (place[1] + k) % YN
+        out[...] = a[i] + b[i]
+
+
+def over_y_ring(place, a, b):
+    out = jax.ShapeDtypeStruct(a.shape[1:], a.dtype)
+    terms = call(add_ring_body, (out,) * YN, (place, a, b))
+    return tuple(shift_y(v, k) if k else v for k, v in enumerate(terms))
 
 
 def field(place, s, cols, diagonal):
-    t = s[0] + s[1] + s[2] + s[3]
+    t = s[0][...] + s[1][...] + s[2][...] + s[3][...]
     bas = t[2] / SCALES[2]
     kern = bas * bas * (t[1] / SCALES[1]) * (t[0] / SCALES[0])
     points = cols[0].shape[1] // 2
@@ -198,7 +254,7 @@
         q = lax.broadcasted_iota(jnp.int32, kern.shape, 0)
         p = lax.broadcasted_iota(jnp.int32, kern.shape, 1) - place[0] * sub
         kern = jnp.where((p >= 0) & (p < sub) & (q == p + place[1] * sub), jnp.float32(0.0), kern)
-    last = [c[c.shape[0] - 1] for c in cols]
+    last = [c[0] for c in cols]
     w = squared(jnp.concatenate([jnp.concatenate([c[:points], c[points:]], axis=1) for c in last]))
     return lax.dot_general(
         kern.astype(jnp.bfloat16), w, (((0,), (0,)), ((), ())), preferred_element_type=jnp.float32
@@ -211,11 +267,11 @@
 
 def apply(place, s, cols, diagonal=False):
     out = jax.ShapeDtypeStruct((s.shape[-1], 2 * LANES), jnp.float32)
-    return call(functools.partial(apply_body, diagonal), out, (place, s) + tuple(cols))
-
-
-def last_body(place, s, col, p1, p2, p3, own, other, out):
-    part = (field(place, s, [col], False) + p1[...] + p2[...] + p3[...]) / math.sqrt(NGRID)
+    return call_last(functools.partial(apply_body, diagonal), out, (place, s), tuple(cols))
+
+
+def last_body(place, s0, s1, s2, s3, p1, p2, p3, own, other, col, out):
+    part = (field(place, (s0, s1, s2, s3), [col], False) + p1[...] + p2[...] + p3[...]) / math.sqrt(NGRID)
     core, y, x = place[0], place[1], place[2]
     points = own.shape[1] // 2
     sub = points // YN
@@ -246,17 +302,16 @@
     n_slabs = (geminal.shape[1] + coulomb.shape[1] + colloc.shape[1]) // (2 * LANES)
     half = geminal.shape[1] // (2 * LANES)
     cuts = (0, half, half + coulomb.shape[1] // (2 * LANES), n_slabs)
-    piece = jax.ShapeDtypeStruct((n_slabs, points, LANES), jnp.bfloat16)
-    kept, given = call(pack_body, (piece, piece), (place, geminal, coulomb, colloc))
+    parts = (geminal, coulomb, colloc)
+    given = swap_core(pack(place, parts, True))
     block = call(
         merge_body,
         jax.ShapeDtypeStruct((n_slabs + 1, 2 * points, LANES), jnp.bfloat16),
-        (place, kept, swap_core(given), occupied),
+        (place, pack(place, parts, False), given, occupied),
     )
 
     f1, b1 = shift_z(block, 1), shift_z(block, -1)
     xf1, xb1 = shift_x(block, 1), shift_x(block, -1)
-    f1, b1, xf1, xb1 = tie(f1, b1, xf1, xb1)
 
     f2, b2 = shift_z(f1, 1), shift_z(b1, -1)
     x2a, x2b = shift_x(xf1[:half], 1), shift_x(xb1[half:], -1)
@@ -273,7 +328,8 @@
     other = swap_core(own)
     f3, b3, s1, t2, other = tie(f3, b3, s1, t2, other)
 
-    f4, b4 = shift_z(f3[:half], 1), shift_z(b3[half:], -1)
+    f4, b4 = halves(half, place, f3, b3)
+    f4, b4 = shift_z(f4, 1), shift_z(b4, -1)
     s2 = over_y(t2)
     keep, *send = tiles(cuts, place, rows, ((f3,), (b3,)), split=True)
     t3 = add(place, keep, *[swap_core(v) for v in send])
@@ -282,13 +338,14 @@
 
     s3 = over_y(t3)
     keep, send = tiles(cuts, place, rows, ((f4, b4),))
-    s4 = over_y(add(place, keep, swap_core(send)))
+    s4 = over_y_ring(place, keep, swap_core(send))
     p2 = apply(place, s2, (f2, b2))
     p3 = apply(place, s3, (f3, b3))
-    sent = call(
+    sent = call_last(
         last_body,
         jax.ShapeDtypeStruct((2 * XN, sub + 8, 2 * LANES), jnp.float32),
-        (place, s4, b4, p1, p2, p3, own, other),
+        (place,) + s4 + (p1, p2, p3, own, other),
+        (b4,),
     )
     got = lax.all_to_all(sent, ("x", "c"), 0, 0, tiled=True)
     pair_field = got[:, :sub].sum(0)

time: 191 us -> 183 us (0.958)
  local copies, waits for them, and re-layouts: 23.5 us -> 15.2 us
    ppermute x4, waiting for transfers between devices: 14.8 us -> 34.6 us  [shift_x(): return lax.ppermute(v, 'x', [(i, (i + d) % XN) for i in range(XN)])]
    ppermute x8, waiting for transfers between devices: 35.3 us -> 21.3 us  [shift_z(): lax.ppermute(v, ('l', 'h'), [(z_slot(z), z_slot((z + d) % ZN)) for z in r...]
    pallas_call x14 -> x11, Pallas kernels: 25.6 us -> 17.3 us  [call(): pl.pallas_call(body, out_shape=out, in_specs=[SMEM] + [VMEM] * (len(args)...]
    pallas_call x1 -> x6, Pallas kernels: 1.47 us -> 8.81 us  [the longest x5 5.88 us: call_last(): pl.pallas_call(body, out_shape=out, grid=(1,), in_specs=[SMEM] + [whole(v...]
    ppermute x0 -> x3, starting transfers between devices: none -> 5.37 us  [shift_y(): return lax.ppermute(v, 'y', [(i, (i + d) % YN) for i in range(YN)])]
    all_to_all x4 -> x3, waiting for transfers between devices: 5.23 us -> 0.3 us  [over_y(): return lax.all_to_all(t, 'y', 0, 0, tiled=True)]
    unnamed x64 -> x48, local copies, waits for them, and re-layouts: 18.7 us -> 14.4 us
    slice x2 -> x0, local copies, waits for them, and re-layouts: 4.09 us -> none  [shards(): f4, b4 = (shift_z(f3[:half], 1), shift_z(b3[half:], -1))]
  transfers between devices with their start and end apart: 25 -> 27, of which waited for: 12 -> 12; matrix products, arithmetic and copies ran while one was open for 1% -> 0% of each run, Pallas kernels for 13% -> 11%
where the time goes in v4:
time: 183 us; the launch traced here: 182 us
  waiting for transfers between devices  71.1 us (39%)
  starting transfers between devices  57.1 us (31%)
  Pallas kernels  26.1 us (14%)
  local copies, waits for them, and re-layouts  15.2 us (8%)
  blocking collectives  10.7 us (6%)
    ppermute x4, waiting for transfers between devices, shift_x(): return lax.ppermute(v, 'x', [(i, (i + d) % XN) for i in range(XN)])  34.6 us
    ppermute x8, waiting for transfers between devices, shift_z(): lax.ppermute(v, ('l', 'h'), [(z_slot(z), z_slot((z + d) % ZN)) for z in r...  21.3 us
    pallas_call x11, Pallas kernels, call(): pl.pallas_call(body, out_shape=out, in_specs=[SMEM] + [VMEM] * (len(args)...  17.3 us
    unnamed x48, local copies, waits for them, and re-layouts  14.4 us
    ppermute x8, starting transfers between devices, swap_core(): return lax.ppermute(v, 'c', [(0, 1), (1, 0)])  13.9 us
    ppermute x8, starting transfers between devices, shift_z(): lax.ppermute(v, ('l', 'h'), [(z_slot(z), z_slot((z + d) % ZN)) for z in r...  13.2 us
    all_to_all x3, starting transfers between devices, over_y(): return lax.all_to_all(t, 'y', 0, 0, tiled=True)  13 us
    all_to_all x1, blocking collectives, shards(): got = lax.all_to_all(sent, ('x', 'c'), 0, 0, tiled=True)  10.7 us
  transfers between devices with their start and end apart: 27, of which 12 were waited for; matrix products, arithmetic and copies ran while one was open for 0% of the time, Pallas kernels for 11%

profile of v4, /device:TPU:1, one launch (start us, length us, event | category | flops | bytes accessed | tf_op | source)
XLA Modules:
  0.0 182.5 jit_solution(4450341320985086199)
XLA Ops:
  0.7 1.1 copy-done.16
  1.8 1.0 copy-done.17
  2.8 0.9 copy-done.18
  3.7 0.7 shard_map.60
  4.5 3.3 %collective-permute-start = (bf16[40,64,128]{2,1,0:T(8,128)(2,1)S(1)}, bf16[40,64,128]{2,1,0:T(8,128)(2,1)S(1)}, u32[]{:S(2)}, u32[]{:S(2)}) collective-permute-start(bf16[40,64,128]{2,1,0:T(8,128)(2,1)S(1)} %shard_map.60), channel_id=1, source_target_pairs={{0,16},{16,0},{1,17},{17,1},{2,18},{18,2},{3,19},{19,3},{4,20},{20... | collective-permute-start | bytes 1966088 | tf_op jit(solution)/shard_map/ppermute | solution.py:42
  7.8 0.7 shard_map.59.kept
  8.5 1.0 collective-permute-done.got
  9.5 0.6 shard_map.61.refs_0_.refs_5_
  10.2 0.8 collective-permute-start.1
  11.0 0.7 collective-permute-start.2
  11.7 0.9 collective-permute-start.5
  12.6 3.9 %collective-permute-start.7 = (bf16[41,128,128]{2,1,0:T(8,128)(2,1)S(1)}, bf16[41,128,128]{2,1,0:T(8,128)(2,1)S(1)}, u32[]{:S(2)}, u32[]{:S(2)}) collective-permute-start(bf16[41,128,128]{2,1,0:T(8,128)(2,1)S(1)} %shard_map.61.refs_0_.refs_5_), channel_id=1, source_target_pairs={{0,44},{32,0},{4,32},{36,4},{8,36},{40,8},{12,40},{44,12},{1,45},{... | collective-permute-start | bytes 4030472 | tf_op jit(solution)/shard_map/ppermute | solution.py:34
  16.6 24.4 %collective-permute-done.1.refs_1_ = bf16[41,128,128]{2,1,0:T(8,128)(2,1)S(1)} collective-permute-done((bf16[41,128,128]{2,1,0:T(8,128)(2,1)S(1)}, bf16[41,128,128]{2,1,0:T(8,128)(2,1)S(1)}, u32[]{:S(2)}, u32[]{:S(2)}) %collective-permute-start.1) | collective-permute-done | bytes 1343520 | tf_op jit(solution)/shard_map/ppermute | solution.py:38
  41.0 2.0 %collective-permute-start.4 = (bf16[21,128,128]{2,1,0:T(8,128)(2,1)S(1)}, bf16[21,128,128]{2,1,0:T(8,128)(2,1)S(1)}, u32[]{:S(2)}, u32[]{:S(2)}) collective-permute-start(bf16[21,128,128]{2,1,0:T(8,128)(2,1)S(1)} %slice.17), channel_id=1, source_target_pairs={{0,192},{64,0},{128,64},{192,128},{1,193},{65,1},{129,65},{193,129... | collective-permute-start | bytes 2064392 | tf_op jit(solution)/shard_map/ppermute | solution.py:38
  43.2 2.6 %collective-permute-done.5.refs_6_.refs_1_ = bf16[41,128,128]{2,1,0:T(8,128)(2,1)S(1)} collective-permute-done((bf16[41,128,128]{2,1,0:T(8,128)(2,1)S(1)}, bf16[41,128,128]{2,1,0:T(8,128)(2,1)S(1)}, u32[]{:S(2)}, u32[]{:S(2)}) %collective-permute-start.5) | collective-permute-done | bytes 1343520 | tf_op jit(solution)/shard_map/ppermute | solution.py:34
  45.8 3.1 %collective-permute-start.8 = (bf16[41,128,128]{2,1,0:T(8,128)(2,1)S(1)}, bf16[41,128,128]{2,1,0:T(8,128)(2,1)}, u32[]{:S(2)}, u32[]{:S(2)}) collective-permute-start(bf16[41,128,128]{2,1,0:T(8,128)(2,1)S(1)} %collective-permute-done.7.refs_7_.refs_2_), channel_id=1, source_target_pairs={{0,44},{32,0},{4,32},{36,4},{8,36},{40,8},{12,40},{44,12},{1,45},{... | collective-permute-start | bytes 4030472 | tf_op jit(solution)/shard_map/ppermute | solution.py:34
  49.0 10.3 %collective-permute-done.3.refs_2_ = bf16[20,128,128]{2,1,0:T(8,128)(2,1)S(1)} collective-permute-done((bf16[20,128,128]{2,1,0:T(8,128)(2,1)S(1)}, bf16[20,128,128]{2,1,0:T(8,128)(2,1)S(1)}, u32[]{:S(2)}, u32[]{:S(2)}) %collective-permute-start.3) | collective-permute-done | bytes 655392 | tf_op jit(solution)/shard_map/ppermute | solution.py:38
  59.2 2.8 %shard_map.62 = (f32[4,3,192,128]{3,2,1,0:T(8,128)S(1)}, f32[4,3,192,128]{3,2,1,0:T(8,128)S(1)}) custom-call(s32[3]{0:T(128)S(1)} %pad_add_fusion.place, bf16[41,128,128]{2,1,0:T(8,128)(2,1)S(1)} %shard_map.61.refs_0_.refs_5_, bf16[41,128,128]{2,1,0:T(8,128)(2,1)S(1)} %collective-permute-done.1.refs_1_, ...), custom_call_target="tpu_custom_call" | custom-call | tf_op jit(solution)/shard_map/pallas_call | solution.py:60
  62.0 2.4 %collective-permute-start.9 = (f32[4,3,192,128]{3,2,1,0:T(8,128)S(1)}, f32[4,3,192,128]{3,2,1,0:T(8,128)S(1)}, u32[]{:S(2)}, u32[]{:S(2)}) collective-permute-start(f32[4,3,192,128]{3,2,1,0:T(8,128)S(1)} %get-tuple-element.32), channel_id=1, source_target_pairs={{0,16},{16,0},{1,17},{17,1},{2,18},{18,2},{3,19},{19,3},{4,20},{20... | collective-permute-start | bytes 3538952 | tf_op jit(solution)/shard_map/ppermute | solution.py:42
  64.4 2.5 %collective-permute-done.9.refs_0_ = f32[4,3,192,128]{3,2,1,0:T(8,128)S(1)} collective-permute-done((f32[4,3,192,128]{3,2,1,0:T(8,128)S(1)}, f32[4,3,192,128]{3,2,1,0:T(8,128)S(1)}, u32[]{:S(2)}, u32[]{:S(2)}) %collective-permute-start.9) | collective-permute-done | bytes 1179680 | tf_op jit(solution)/shard_map/ppermute | solution.py:42
  66.9 0.7 shard_map.63
  67.6 1.0 copy-done.13
  68.6 8.6 %collective-permute-done.6.refs_5_.refs_0_ = bf16[41,128,128]{2,1,0:T(8,128)(2,1)} collective-permute-done((bf16[41,128,128]{2,1,0:T(8,128)(2,1)S(1)}, bf16[41,128,128]{2,1,0:T(8,128)(2,1)}, u32[]{:S(2)}, u32[]{:S(2)}) %collective-permute-start.6) | collective-permute-done | bytes 1343520 | tf_op jit(solution)/shard_map/ppermute | solution.py:34
  77.3 2.7 %collective-permute-start.11 = (bf16[41,128,128]{2,1,0:T(8,128)(2,1)}, bf16[41,128,128]{2,1,0:T(8,128)(2,1)}, u32[]{:S(2)}, u32[]{:S(2)}) collective-permute-start(bf16[41,128,128]{2,1,0:T(8,128)(2,1)} %collective-permute-done.8.refs_6_.refs_1_), channel_id=1, source_target_pairs={{0,44},{32,0},{4,32},{36,4},{8,36},{40,8},{12,40},{44,12},{1,45},{... | collective-permute-start | bytes 4030472 | tf_op jit(solution)/shard_map/ppermute | solution.py:34
  80.0 4.3 %all-to-all-start = ((f32[4,3,192,128]{3,2,1,0:T(8,128)}), f32[4,3,192,128]{3,2,1,0:T(8,128)}, u32[]{:S(2)}, u32[]{:S(2)}) async-start(f32[4,3,192,128]{3,2,1,0:T(8,128)} %copy-done.13), calls=%async_computation | async-start | bytes 2359296 | tf_op jit(solution)/shard_map/all_to_all | solution.py:50
  84.2 1.3 copy-done.1
  85.6 1.1 copy-done.6
  86.7 3.4 %shard_map.64 = (f32[4,3,128,128]{3,2,1,0:T(8,128)S(1)}, f32[4,3,128,128]{3,2,1,0:T(8,128)S(1)}) custom-call(s32[3]{0:T(128)S(1)} %pad_add_fusion.place, bf16[41,128,128]{2,1,0:T(8,128)(2,1)S(1)} %shard_map.61.refs_0_.refs_5_, bf16[41,128,128]{2,1,0:T(8,128)(2,1)S(1)} %collective-permute-done.1.refs_1_, bf16[20,128,128]{2,1,0:T(8,128)(2,1)S(1)} %copy-done.6, ...), custom_call_target="tpu_custom_call" | custom-call | tf_op jit(solution)/shard_map/pallas_call | solution.py:60
  90.1 3.1 %collective-permute-start.12 = (f32[4,3,128,128]{3,2,1,0:T(8,128)S(1)}, f32[4,3,128,128]{3,2,1,0:T(8,128)S(1)}, u32[]{:S(2)}, u32[]{:S(2)}) collective-permute-start(f32[4,3,128,128]{3,2,1,0:T(8,128)S(1)} %get-tuple-element.37), channel_id=1, source_target_pairs={{0,16},{16,0},{1,17},{17,1},{2,18},{18,2},{3,19},{19,3},{4,20},{20... | collective-permute-start | bytes 2359304 | tf_op jit(solution)/shard_map/ppermute | solution.py:42
  93.9 1.2 collective-permute-done.12.refs_0_
  95.1 0.7 shard_map.65
  95.8 0.9 copy-done.14
  96.7 0.6 copy-done.21
  97.6 10.0 %collective-permute-done.10.a.refs_5_.refs_0_ = bf16[41,128,128]{2,1,0:T(8,128)(2,1)} collective-permute-done((bf16[41,128,128]{2,1,0:T(8,128)(2,1)}, bf16[41,128,128]{2,1,0:T(8,128)(2,1)}, u32[]{:S(2)}, u32[]{:S(2)}) %collective-permute-start.10) | collective-permute-done | bytes 1343520 | tf_op jit(solution)/shard_map/ppermute | solution.py:34
  107.7 2.9 %shard_map.67 = (bf16[20,128,128]{2,1,0:T(8,128)(2,1)}, bf16[21,128,128]{2,1,0:T(8,128)(2,1)}) custom-call(s32[3]{0:T(128)S(1)} %pad_add_fusion.place, bf16[41,128,128]{2,1,0:T(8,128)(2,1)} %collective-permute-done.10.a.refs_5_.refs_0_, bf16[41,128,128]{2,1,0:T(8,128)(2,1)} %collective-permute-done.11.b.refs_6_.refs_1_), custom_call_target="tpu_custom_call" | custom-call | tf_op jit(solution)/shard_map/pallas_call | solution.py:110
  110.6 2.5 %collective-permute-start.15 = (bf16[21,128,128]{2,1,0:T(8,128)(2,1)}, bf16[21,128,128]{2,1,0:T(8,128)(2,1)}, u32[]{:S(2)}, u32[]{:S(2)}) collective-permute-start(bf16[21,128,128]{2,1,0:T(8,128)(2,1)} %get-tuple-element.41), channel_id=1, source_target_pairs={{0,44},{32,0},{4,32},{36,4},{8,36},{40,8},{12,40},{44,12},{1,45},{... | collective-permute-start | bytes 2064392 | tf_op jit(solution)/shard_map/ppermute | solution.py:34
  113.1 4.2 %all-to-all-start.1 = ((f32[4,3,128,128]{3,2,1,0:T(8,128)}), f32[4,3,128,128]{3,2,1,0:T(8,128)}, u32[]{:S(2)}, u32[]{:S(2)}) async-start(f32[4,3,128,128]{3,2,1,0:T(8,128)} %copy-done.14), calls=%async_computation.1 | async-start | bytes 1572864 | tf_op jit(solution)/shard_map/all_to_all | solution.py:50
  117.3 1.3 copy-done.3
  118.6 1.1 copy-done.7
  119.7 3.4 %shard_map.68 = (f32[4,3,128,128]{3,2,1,0:T(8,128)S(1)}, f32[4,1,128,128]{3,2,1,0:T(8,128)S(1)}, f32[4,1,128,128]{3,2,1,0:T(8,128)S(1)}, f32[4,1,128,128]{3,2,1,0:T(8,128)S(1)}) custom-call(s32[3]{0:T(128)S(1)} %pad_add_fusion.place, bf16[41,128,128]{2,1,0:T(8,128)(2,1)S(1)} %shard_map.61.refs_0_.refs_5_, ...), custom_call_target="tpu_custom_call" | custom-call | tf_op jit(solution)/shard_map/pallas_call | solution.py:60
  123.1 4.0 %collective-permute-start.16 = (f32[4,1,128,128]{3,2,1,0:T(8,128)S(1)}, f32[4,1,128,128]{3,2,1,0:T(8,128)S(1)}, u32[]{:S(2)}, u32[]{:S(2)}) collective-permute-start(f32[4,1,128,128]{3,2,1,0:T(8,128)S(1)} %get-tuple-element.44), channel_id=1, source_target_pairs={{0,16},{16,0},{1,17},{17,1},{2,18},{18,2},{3,19},{19,3},{4,20},{20... | collective-permute-start | bytes 786440 | tf_op jit(solution)/shard_map/ppermute | solution.py:42
  127.6 1.5 shard_map.70.p1
  129.2 0.6 copy-done.19
  129.8 0.7 shard_map.69
  130.5 0.9 copy-done.15
  131.4 4.5 %all-to-all-start.2 = ((f32[4,3,128,128]{3,2,1,0:T(8,128)}), f32[4,3,128,128]{3,2,1,0:T(8,128)}, u32[]{:S(2)}, u32[]{:S(2)}) async-start(f32[4,3,128,128]{3,2,1,0:T(8,128)} %copy-done.15), calls=%async_computation.2 | async-start | bytes 1572864 | tf_op jit(solution)/shard_map/all_to_all | solution.py:50
  135.9 1.3 copy-done.4
  137.3 1.1 copy-done.8
  138.3 3.1 %shard_map.71 = (f32[4,3,64,128]{3,2,1,0:T(8,128)S(1)}, f32[4,3,64,128]{3,2,1,0:T(8,128)S(1)}) custom-call(s32[3]{0:T(128)S(1)} %pad_add_fusion.place, bf16[41,128,128]{2,1,0:T(8,128)(2,1)S(1)} %shard_map.61.refs_0_.refs_5_, bf16[41,128,128]{2,1,0:T(8,128)(2,1)S(1)} %collective-permute-done.1.refs_1_, bf16[20,128,128]{2,1,0:T(8,128)(2,1)S(1)} %copy-done.8, ...), custom_call_target="tpu_custom_call" | custom-call | tf_op jit(solution)/shard_map/pallas_call | solution.py:60
  141.9 1.4 collective-permute-done.19.b
  143.2 0.6 shard_map.72
  143.8 1.8 collective-permute-start.20
  145.6 2.4 %collective-permute-start.21 = (f32[3,64,128]{2,1,0:T(8,128)S(1)}, f32[3,64,128]{2,1,0:T(8,128)S(1)}, u32[]{:S(2)}, u32[]{:S(2)}) collective-permute-start(f32[3,64,128]{2,1,0:T(8,128)S(1)} %get-tuple-element.54), channel_id=1, source_target_pairs={{0,2},{1,3},{2,0},{3,1},{4,6},{5,7},{6,4},{7,5},{8,10},{9,11},{10,... | collective-permute-start | bytes 294920 | tf_op jit(solution)/shard_map/ppermute | solution.py:232
  148.0 1.2 collective-permute-start.22
  149.2 1.4 shard_map.73.p2
  150.6 1.4 shard_map.74.p3
  152.1 0.6 collective-permute-done.21.s2
  152.7 1.0 shard_map.75
  153.7 10.7 %all_to_all.25 = f32[8,24,256]{2,1,0:T(8,128)S(1)} all-to-all(f32[8,24,256]{2,1,0:T(8,128)S(1)} %shard_map.75), channel_id=1, replica_groups=mesh['x'=4,'l'=2,'c'=2,'h'=4,'y'=4] {'x','c'}, dimensions={0} | all-to-all | bytes 393216 | tf_op jit(solution)/shard_map/all_to_all | solution.py:350
  164.5 0.6 broadcast_in_dim.4
  165.1 8.1 %all-to-all-start.4 = ((f32[32,1,256]{2,1,0:T(1,128)}), f32[32,1,256]{2,1,0:T(1,128)S(1)}, u32[]{:S(2)}, u32[]{:S(2)}) async-start(f32[32,1,256]{2,1,0:T(1,128)} %broadcast_in_dim.4), calls=%async_computation.4 | async-start | bytes 65536 | tf_op jit(solution)/shard_map/all_to_all | solution.py:46
  173.2 0.6 slice_reduce_fusion
  173.8 8.1 %all-to-all-done.4 = f32[32,1,256]{2,1,0:T(1,128)S(1)} async-done(((f32[32,1,256]{2,1,0:T(1,128)}), f32[32,1,256]{2,1,0:T(1,128)S(1)}, u32[]{:S(2)}, u32[]{:S(2)}) %all-to-all-start.4) | async-done | bytes 32800 | tf_op jit(solution)/shard_map/all_to_all | solution.py:46
  181.9 0.6 reduce_sum.29
  (63 shorter events, 2.3 us)
Async XLA Ops:
  0.7 1.1 copy-start.16
  1.8 1.0 copy-start.17
  2.8 0.9 copy-start.18
  4.5 5.1 %copy-start.23 = (bf16[64,256]{1,0:T(8,128)(2,1)S(1)}, bf16[64,256]{1,0:T(8,128)(2,1)}, u32[]{:S(2)}) copy-start(bf16[64,256]{1,0:T(8,128)(2,1)} %occ.1) | copy-start | bytes 98308
  4.5 5.1 %collective-permute-start = (bf16[40,64,128]{2,1,0:T(8,128)(2,1)S(1)}, bf16[40,64,128]{2,1,0:T(8,128)(2,1)S(1)}, u32[]{:S(2)}, u32[]{:S(2)}) collective-permute-start(bf16[40,64,128]{2,1,0:T(8,128)(2,1)S(1)} %shard_map.60), channel_id=1, source_target_pairs={{0,16},{16,0},{1,17},{17,1},{2,18},{18,2},{3,19},{19,3},{4,20},{20... | collective-permute-start | bytes 1966088 | tf_op jit(solution)/shard_map/ppermute | solution.py:42
  10.2 30.8 %collective-permute-start.1 = (bf16[41,128,128]{2,1,0:T(8,128)(2,1)S(1)}, bf16[41,128,128]{2,1,0:T(8,128)(2,1)S(1)}, u32[]{:S(2)}, u32[]{:S(2)}) collective-permute-start(bf16[41,128,128]{2,1,0:T(8,128)(2,1)S(1)} %shard_map.61.refs_0_.refs_5_), channel_id=1, source_target_pairs={{0,192},{64,0},{128,64},{192,128},{1,193},{65,1},{129,65},{193,129... | collective-permute-start | bytes 4030472 | tf_op jit(solution)/shard_map/ppermute | solution.py:38
  11.0 32.0 %collective-permute-start.2 = (bf16[41,128,128]{2,1,0:T(8,128)(2,1)S(1)}, bf16[41,128,128]{2,1,0:T(8,128)(2,1)S(1)}, u32[]{:S(2)}, u32[]{:S(2)}) collective-permute-start(bf16[41,128,128]{2,1,0:T(8,128)(2,1)S(1)} %shard_map.61.refs_0_.refs_5_), channel_id=1, source_target_pairs={{0,64},{64,128},{128,192},{192,0},{1,65},{65,129},{129,193},{193,1... | collective-permute-start | bytes 4030472 | tf_op jit(solution)/shard_map/ppermute | solution.py:38
  11.7 34.1 %collective-permute-start.5 = (bf16[41,128,128]{2,1,0:T(8,128)(2,1)S(1)}, bf16[41,128,128]{2,1,0:T(8,128)(2,1)S(1)}, u32[]{:S(2)}, u32[]{:S(2)}) collective-permute-start(bf16[41,128,128]{2,1,0:T(8,128)(2,1)S(1)} %shard_map.61.refs_0_.refs_5_), channel_id=1, source_target_pairs={{0,32},{32,4},{4,36},{36,8},{8,40},{40,12},{12,44},{44,0},{1,33},{... | collective-permute-start | bytes 4030472 | tf_op jit(solution)/shard_map/ppermute | solution.py:34
  12.6 33.2 %collective-permute-start.7 = (bf16[41,128,128]{2,1,0:T(8,128)(2,1)S(1)}, bf16[41,128,128]{2,1,0:T(8,128)(2,1)S(1)}, u32[]{:S(2)}, u32[]{:S(2)}) collective-permute-start(bf16[41,128,128]{2,1,0:T(8,128)(2,1)S(1)} %shard_map.61.refs_0_.refs_5_), channel_id=1, source_target_pairs={{0,44},{32,0},{4,32},{36,4},{8,36},{40,8},{12,40},{44,12},{1,45},{... | collective-permute-start | bytes 4030472 | tf_op jit(solution)/shard_map/ppermute | solution.py:34
  41.0 18.2 %collective-permute-start.4 = (bf16[21,128,128]{2,1,0:T(8,128)(2,1)S(1)}, bf16[21,128,128]{2,1,0:T(8,128)(2,1)S(1)}, u32[]{:S(2)}, u32[]{:S(2)}) collective-permute-start(bf16[21,128,128]{2,1,0:T(8,128)(2,1)S(1)} %slice.17), channel_id=1, source_target_pairs={{0,192},{64,0},{128,64},{192,128},{1,193},{65,1},{129,65},{193,129... | collective-permute-start | bytes 2064392 | tf_op jit(solution)/shard_map/ppermute | solution.py:38
  43.0 19.0 %copy-start = (bf16[41,128,128]{2,1,0:T(8,128)(2,1)}, bf16[41,128,128]{2,1,0:T(8,128)(2,1)S(1)}, u32[]{:S(2)}) copy-start(bf16[41,128,128]{2,1,0:T(8,128)(2,1)S(1)} %collective-permute-done.2.refs_4_.refs_3_) | copy-start | bytes 4030468
  43.1 16.1 %collective-permute-start.3 = (bf16[20,128,128]{2,1,0:T(8,128)(2,1)S(1)}, bf16[20,128,128]{2,1,0:T(8,128)(2,1)S(1)}, u32[]{:S(2)}, u32[]{:S(2)}) collective-permute-start(bf16[20,128,128]{2,1,0:T(8,128)(2,1)S(1)} %slice.16), channel_id=1, source_target_pairs={{0,64},{64,128},{128,192},{192,0},{1,65},{65,129},{129,193},{193,1... | collective-permute-start | bytes 1966088 | tf_op jit(solution)/shard_map/ppermute | solution.py:38
  45.8 16.2 %copy-start.9 = (bf16[41,128,128]{2,1,0:T(8,128)(2,1)}, bf16[41,128,128]{2,1,0:T(8,128)(2,1)S(1)}, u32[]{:S(2)}) copy-start(bf16[41,128,128]{2,1,0:T(8,128)(2,1)S(1)} %collective-permute-done.5.refs_6_.refs_1_) | copy-start | bytes 4030468
  45.8 31.5 %collective-permute-start.6 = (bf16[41,128,128]{2,1,0:T(8,128)(2,1)S(1)}, bf16[41,128,128]{2,1,0:T(8,128)(2,1)}, u32[]{:S(2)}, u32[]{:S(2)}) collective-permute-start(bf16[41,128,128]{2,1,0:T(8,128)(2,1)S(1)} %collective-permute-done.5.refs_6_.refs_1_), channel_id=1, source_target_pairs={{0,32},{32,4},{4,36},{36,8},{8,40},{40,12},{12,44},{44,0},{1,33},{... | collective-permute-start | bytes 4030472 | tf_op jit(solution)/shard_map/ppermute | solution.py:34
  45.8 16.2 %copy-start.11 = (bf16[41,128,128]{2,1,0:T(8,128)(2,1)}, bf16[41,128,128]{2,1,0:T(8,128)(2,1)S(1)}, u32[]{:S(2)}) copy-start(bf16[41,128,128]{2,1,0:T(8,128)(2,1)S(1)} %collective-permute-done.7.refs_7_.refs_2_) | copy-start | bytes 4030468
  45.8 31.4 %collective-permute-start.8 = (bf16[41,128,128]{2,1,0:T(8,128)(2,1)S(1)}, bf16[41,128,128]{2,1,0:T(8,128)(2,1)}, u32[]{:S(2)}, u32[]{:S(2)}) collective-permute-start(bf16[41,128,128]{2,1,0:T(8,128)(2,1)S(1)} %collective-permute-done.7.refs_7_.refs_2_), channel_id=1, source_target_pairs={{0,44},{32,0},{4,32},{36,4},{8,36},{40,8},{12,40},{44,12},{1,45},{... | collective-permute-start | bytes 4030472 | tf_op jit(solution)/shard_map/ppermute | solution.py:34
  59.2 2.8 %copy-start.5 = (bf16[20,128,128]{2,1,0:T(8,128)(2,1)}, bf16[20,128,128]{2,1,0:T(8,128)(2,1)S(1)}, u32[]{:S(2)}) copy-start(bf16[20,128,128]{2,1,0:T(8,128)(2,1)S(1)} %collective-permute-done.3.refs_2_) | copy-start | bytes 1966084
  62.0 4.9 %collective-permute-start.9 = (f32[4,3,192,128]{3,2,1,0:T(8,128)S(1)}, f32[4,3,192,128]{3,2,1,0:T(8,128)S(1)}, u32[]{:S(2)}, u32[]{:S(2)}) collective-permute-start(f32[4,3,192,128]{3,2,1,0:T(8,128)S(1)} %get-tuple-element.32), channel_id=1, source_target_pairs={{0,16},{16,0},{1,17},{17,1},{2,18},{18,2},{3,19},{19,3},{4,20},{20... | collective-permute-start | bytes 3538952 | tf_op jit(solution)/shard_map/ppermute | solution.py:42
  67.6 1.0 copy-start.13
  77.3 30.4 %collective-permute-start.10 = (bf16[41,128,128]{2,1,0:T(8,128)(2,1)}, bf16[41,128,128]{2,1,0:T(8,128)(2,1)}, u32[]{:S(2)}, u32[]{:S(2)}) collective-permute-start(bf16[41,128,128]{2,1,0:T(8,128)(2,1)} %collective-permute-done.6.refs_5_.refs_0_), channel_id=1, source_target_pairs={{0,32},{32,4},{4,36},{36,8},{8,40},{40,12},{12,44},{44,0},{1,33},{... | collective-permute-start | bytes 4030472 | tf_op jit(solution)/shard_map/ppermute | solution.py:34
  77.3 30.4 %collective-permute-start.11 = (bf16[41,128,128]{2,1,0:T(8,128)(2,1)}, bf16[41,128,128]{2,1,0:T(8,128)(2,1)}, u32[]{:S(2)}, u32[]{:S(2)}) collective-permute-start(bf16[41,128,128]{2,1,0:T(8,128)(2,1)} %collective-permute-done.8.refs_6_.refs_1_), channel_id=1, source_target_pairs={{0,44},{32,0},{4,32},{36,4},{8,36},{40,8},{12,40},{44,12},{1,45},{... | collective-permute-start | bytes 4030472 | tf_op jit(solution)/shard_map/ppermute | solution.py:34
  80.0 17.7 %all-to-all-start = ((f32[4,3,192,128]{3,2,1,0:T(8,128)}), f32[4,3,192,128]{3,2,1,0:T(8,128)}, u32[]{:S(2)}, u32[]{:S(2)}) async-start(f32[4,3,192,128]{3,2,1,0:T(8,128)} %copy-done.13), calls=%async_computation | async-start | bytes 2359296 | tf_op jit(solution)/shard_map/all_to_all | solution.py:50
  84.2 1.3 copy-start.1
  85.6 1.1 copy-start.6
  86.7 6.5 %copy-start.2 = (bf16[41,128,128]{2,1,0:T(8,128)(2,1)S(1)}, bf16[41,128,128]{2,1,0:T(8,128)(2,1)}, u32[]{:S(2)}) copy-start(bf16[41,128,128]{2,1,0:T(8,128)(2,1)} %copy-done) | copy-start | bytes 4030468
  90.1 5.0 %collective-permute-start.12 = (f32[4,3,128,128]{3,2,1,0:T(8,128)S(1)}, f32[4,3,128,128]{3,2,1,0:T(8,128)S(1)}, u32[]{:S(2)}, u32[]{:S(2)}) collective-permute-start(f32[4,3,128,128]{3,2,1,0:T(8,128)S(1)} %get-tuple-element.37), channel_id=1, source_target_pairs={{0,16},{16,0},{1,17},{17,1},{2,18},{18,2},{3,19},{19,3},{4,20},{20... | collective-permute-start | bytes 2359304 | tf_op jit(solution)/shard_map/ppermute | solution.py:42
  93.8 2.9 %collective-permute-start.13 = (bf16[4,128,128]{2,1,0:T(8,128)(2,1)S(1)}, bf16[4,128,128]{2,1,0:T(8,128)(2,1)S(1)}, u32[]{:S(2)}, u32[]{:S(2)}) collective-permute-start(bf16[4,128,128]{2,1,0:T(8,128)(2,1)S(1)} %shard_map.66.own), channel_id=1, source_target_pairs={{0,16},{16,0},{1,17},{17,1},{2,18},{18,2},{3,19},{19,3},{4,20},{20... | collective-permute-start | bytes 393224 | tf_op jit(solution)/shard_map/ppermute | solution.py:42
  95.8 0.9 copy-start.14
  96.7 0.7 copy-start.21
  110.6 20.8 %collective-permute-start.15 = (bf16[21,128,128]{2,1,0:T(8,128)(2,1)}, bf16[21,128,128]{2,1,0:T(8,128)(2,1)}, u32[]{:S(2)}, u32[]{:S(2)}) collective-permute-start(bf16[21,128,128]{2,1,0:T(8,128)(2,1)} %get-tuple-element.41), channel_id=1, source_target_pairs={{0,44},{32,0},{4,32},{36,4},{8,36},{40,8},{12,40},{44,12},{1,45},{... | collective-permute-start | bytes 2064392 | tf_op jit(solution)/shard_map/ppermute | solution.py:34
  113.1 18.3 %collective-permute-start.14 = (bf16[20,128,128]{2,1,0:T(8,128)(2,1)}, bf16[20,128,128]{2,1,0:T(8,128)(2,1)}, u32[]{:S(2)}, u32[]{:S(2)}) collective-permute-start(bf16[20,128,128]{2,1,0:T(8,128)(2,1)} %get-tuple-element.40), channel_id=1, source_target_pairs={{0,32},{32,4},{4,36},{36,8},{8,40},{40,12},{12,44},{44,0},{1,33},{... | collective-permute-start | bytes 1966088 | tf_op jit(solution)/shard_map/ppermute | solution.py:34
  113.1 18.3 %all-to-all-start.1 = ((f32[4,3,128,128]{3,2,1,0:T(8,128)}), f32[4,3,128,128]{3,2,1,0:T(8,128)}, u32[]{:S(2)}, u32[]{:S(2)}) async-start(f32[4,3,128,128]{3,2,1,0:T(8,128)} %copy-done.14), calls=%async_computation.1 | async-start | bytes 1572864 | tf_op jit(solution)/shard_map/all_to_all | solution.py:50
  117.3 1.3 copy-start.3
  118.6 1.1 copy-start.7
  119.7 7.9 %copy-start.10 = (bf16[41,128,128]{2,1,0:T(8,128)(2,1)S(1)}, bf16[41,128,128]{2,1,0:T(8,128)(2,1)}, u32[]{:S(2)}) copy-start(bf16[41,128,128]{2,1,0:T(8,128)(2,1)} %copy-done.9) | copy-start | bytes 4030468
  119.7 7.9 %copy-start.12 = (bf16[41,128,128]{2,1,0:T(8,128)(2,1)S(1)}, bf16[41,128,128]{2,1,0:T(8,128)(2,1)}, u32[]{:S(2)}) copy-start(bf16[41,128,128]{2,1,0:T(8,128)(2,1)} %copy-done.11) | copy-start | bytes 4030468
  123.1 6.7 %collective-permute-start.16 = (f32[4,1,128,128]{3,2,1,0:T(8,128)S(1)}, f32[4,1,128,128]{3,2,1,0:T(8,128)S(1)}, u32[]{:S(2)}, u32[]{:S(2)}) collective-permute-start(f32[4,1,128,128]{3,2,1,0:T(8,128)S(1)} %get-tuple-element.44), channel_id=1, source_target_pairs={{0,16},{16,0},{1,17},{17,1},{2,18},{18,2},{3,19},{19,3},{4,20},{20... | collective-permute-start | bytes 786440 | tf_op jit(solution)/shard_map/ppermute | solution.py:42
  127.1 2.7 %collective-permute-start.17 = (f32[4,1,128,128]{3,2,1,0:T(8,128)S(1)}, f32[4,1,128,128]{3,2,1,0:T(8,128)S(1)}, u32[]{:S(2)}, u32[]{:S(2)}) collective-permute-start(f32[4,1,128,128]{3,2,1,0:T(8,128)S(1)} %get-tuple-element.45), channel_id=1, source_target_pairs={{0,16},{16,0},{1,17},{17,1},{2,18},{18,2},{3,19},{19,3},{4,20},{20... | collective-permute-start | bytes 786440 | tf_op jit(solution)/shard_map/ppermute | solution.py:42
  127.2 2.6 %collective-permute-start.18 = (f32[4,1,128,128]{3,2,1,0:T(8,128)S(1)}, f32[4,1,128,128]{3,2,1,0:T(8,128)S(1)}, u32[]{:S(2)}, u32[]{:S(2)}) collective-permute-start(f32[4,1,128,128]{3,2,1,0:T(8,128)S(1)} %get-tuple-element.46), channel_id=1, source_target_pairs={{0,16},{16,0},{1,17},{17,1},{2,18},{18,2},{3,19},{19,3},{4,20},{20... | collective-permute-start | bytes 786440 | tf_op jit(solution)/shard_map/ppermute | solution.py:42
  129.1 0.7 copy-start.19
  130.5 0.9 copy-start.15
  131.4 19.2 %all-to-all-start.2 = ((f32[4,3,128,128]{3,2,1,0:T(8,128)}), f32[4,3,128,128]{3,2,1,0:T(8,128)}, u32[]{:S(2)}, u32[]{:S(2)}) async-start(f32[4,3,128,128]{3,2,1,0:T(8,128)} %copy-done.15), calls=%async_computation.2 | async-start | bytes 1572864 | tf_op jit(solution)/shard_map/all_to_all | solution.py:50
  135.9 1.3 copy-start.4
  137.2 1.1 copy-start.8
  141.4 1.8 collective-permute-start.19
  143.8 8.2 %collective-permute-start.20 = (f32[3,64,128]{2,1,0:T(8,128)S(1)}, f32[3,64,128]{2,1,0:T(8,128)S(1)}, u32[]{:S(2)}, u32[]{:S(2)}) collective-permute-start(f32[3,64,128]{2,1,0:T(8,128)S(1)} %get-tuple-element.53), channel_id=1, source_target_pairs={{0,1},{1,2},{2,3},{3,0},{4,5},{5,6},{6,7},{7,4},{8,9},{9,10},{10,1... | collective-permute-start | bytes 294920 | tf_op jit(solution)/shard_map/ppermute | solution.py:232
  145.6 7.0 %collective-permute-start.21 = (f32[3,64,128]{2,1,0:T(8,128)S(1)}, f32[3,64,128]{2,1,0:T(8,128)S(1)}, u32[]{:S(2)}, u32[]{:S(2)}) collective-permute-start(f32[3,64,128]{2,1,0:T(8,128)S(1)} %get-tuple-element.54), channel_id=1, source_target_pairs={{0,2},{1,3},{2,0},{3,1},{4,6},{5,7},{6,4},{7,5},{8,10},{9,11},{10,... | collective-permute-start | bytes 294920 | tf_op jit(solution)/shard_map/ppermute | solution.py:232
  148.0 4.7 %collective-permute-start.22 = (f32[3,64,128]{2,1,0:T(8,128)S(1)}, f32[3,64,128]{2,1,0:T(8,128)S(1)}, u32[]{:S(2)}, u32[]{:S(2)}) collective-permute-start(f32[3,64,128]{2,1,0:T(8,128)S(1)} %get-tuple-element.55), channel_id=1, source_target_pairs={{0,3},{1,0},{2,1},{3,2},{4,7},{5,4},{6,5},{7,6},{8,11},{9,8},{10,9... | collective-permute-start | bytes 294920 | tf_op jit(solution)/shard_map/ppermute | solution.py:232
  150.6 2.1 %copy-start.20 = (f32[128,256]{1,0:T(8,128)S(1)}, f32[128,256]{1,0:T(8,128)}, u32[]{:S(2)}) copy-start(f32[128,256]{1,0:T(8,128)} %copy-done.19) | copy-start | bytes 393220
  150.6 2.1 %copy-start.22 = (bf16[4,128,128]{2,1,0:T(8,128)(2,1)S(1)}, bf16[4,128,128]{2,1,0:T(8,128)(2,1)}, u32[]{:S(2)}) copy-start(bf16[4,128,128]{2,1,0:T(8,128)(2,1)} %copy-done.21) | copy-start | bytes 393220
  165.1 16.8 %all-to-all-start.4 = ((f32[32,1,256]{2,1,0:T(1,128)}), f32[32,1,256]{2,1,0:T(1,128)S(1)}, u32[]{:S(2)}, u32[]{:S(2)}) async-start(f32[32,1,256]{2,1,0:T(1,128)} %broadcast_in_dim.4), calls=%async_computation.4 | async-start | bytes 65536 | tf_op jit(solution)/shard_map/all_to_all | solution.py:46

commit v5 on v2

v5 whole, which is shorter than its diff:
```python
import functools
import math

import jax
import jax.numpy as jnp
from jax import lax
from jax.experimental import pallas as pl
from jax.experimental.pallas import tpu as pltpu
from jax.sharding import Mesh, PartitionSpec as P

NBAS = 4096
NAUXC = 16384
NAUXF = 20480
NGRID = 4096
ZN = 8
XN = 4
YN = 4
LANES = 128
GROUP = 4
SCALES = (math.sqrt(NAUXF), math.sqrt(NAUXC), math.sqrt(NBAS))
VMEM = pl.BlockSpec(memory_space=pltpu.VMEM)
SMEM = pl.BlockSpec(memory_space=pltpu.SMEM)


def tie(*values):
    return lax.optimization_barrier(values)


def z_slot(z):
    return (z % 2) * (ZN // 2) + z // 2


def shift_z(v, d):
    return lax.ppermute(v, ("l", "h"), [(z_slot(z), z_slot((z + d) % ZN)) for z in range(ZN)])


def shift_x(v, d):
    return lax.ppermute(v, "x", [(i, (i + d) % XN) for i in range(XN)])


def swap_core(v):
    return lax.ppermute(v, "c", [(0, 1), (1, 0)])


def spread(v, axes, count):
    return lax.all_to_all(jnp.broadcast_to(v, (count,) + v.shape), axes, 0, 0, tiled=True)


def over_y(t):
    return lax.all_to_all(t, "y", 0, 0, tiled=True)


def squared(v):
    v = v.astype(jnp.float32)
    return (v * v).astype(jnp.bfloat16)


def call(body, out, args):
    several = isinstance(out, tuple)
    return pl.pallas_call(
        body,
        out_shape=out,
        in_specs=[SMEM] + [VMEM] * (len(args) - 1),
        out_specs=tuple(VMEM for _ in out) if several else VMEM,
        cost_estimate=pl.CostEstimate(flops=0, bytes_accessed=0, transcendentals=0),
        compiler_params=pltpu.CompilerParams(vmem_limit_bytes=32 * 1024 * 1024),
    )(*args)


def pack_body(given, place, *refs):
    parts, out = refs[:-1], refs[-1]
    which = 1 - place[0] if given else place[0]
    slab = 0
    for ref in parts:
        width = ref.shape[1] // 2
        for i in range(width // LANES):
            out[slab] = ref[:, pl.ds(pl.multiple_of(which * width + i * LANES, LANES), LANES)]
            slab += 1


def pack(place, parts, given):
    slabs = sum(v.shape[1] for v in parts) // (2 * LANES)
    out = jax.ShapeDtypeStruct((slabs, parts[0].shape[0], LANES), parts[0].dtype)
    return call(functools.partial(pack_body, given), out, (place,) + parts)


def merge_body(place, kept, got, occ, *outs):
    core = place[0]
    _, points, _ = kept.shape
    start = 0
    for out in outs:
        n = out.shape[0] - 1
        for ref, which in ((kept, core), (got, 1 - core)):
            at = pl.ds(pl.multiple_of(which * points, points), points)
            out[:n, at] = ref[start : start + n]
        out[n, :points] = occ[:, :LANES]
        out[n, points:] = occ[:, LANES:]
        start += n


def fetch_body(cuts, count, place, *refs):
    sources, (keep, send), held, sems = refs[:count], refs[count : count + 2], refs[count + 2 : -1], refs[-1]
    copies = [pltpu.make_async_copy(a, b, sems.at[i]) for i, (a, b) in enumerate(zip(sources, held))]
    n = count // 2 - XN
    kinds = tuple(range(XN)) + tuple(range(2 * XN, 2 * XN + n)), tuple(range(XN, 2 * XN)) + tuple(range(2 * XN + n, count))
    for kind in kinds:
        for i in kind:
            copies[i].start()
    tile_body(cuts, place, *held, keep, send, ready=[[copies[i] for i in kind] for kind in kinds])


def tile_body(cuts, place, *refs, ready=None):
    keep, send = refs[-2:]
    n = (len(refs) - 2) // 2 - XN
    rows, cols = (refs[:XN], refs[XN : 2 * XN]), (refs[2 * XN : 2 * XN + n], refs[2 * XN + n : -2])
    points = keep.shape[2] // n
    core, twist = place[0], 2 * lax.rem(place[2], 2)
    for j, (kind, a, b) in enumerate(cuts):
        if ready and a == 0:
            for copy in ready[kind]:
                copy.wait()
        acc = None
        for s in range(a, b, GROUP):
            group = range(s, s + GROUP)
            r = jnp.concatenate([jnp.concatenate([x[t] for x in rows[kind]]) for t in group], axis=1)
            q = jnp.concatenate([jnp.concatenate([x[t] for x in cols[kind]]) for t in group], axis=1)
            part = lax.dot_general(q, r, (((1,), (1,)), ((), ())), preferred_element_type=jnp.float32)
            acc = part if acc is None else acc + part
        for i in range(n):
            first = acc[2 * i * points : (2 * i + 1) * points]
            second = acc[(2 * i + 1) * points : (2 * i + 2) * points]
            for out, t in (
                (keep, jnp.where(core == 0, first, second)),
                (send, jnp.where(core == 0, second, first)),
            ):
                for e in range(XN):
                    y = lax.rem(e + twist, YN)
                    out[y, j, i * points : (i + 1) * points] = t[:, 2 * e * points : 2 * (e + 1) * points]


def tiles(cuts, place, rows, cols, fetch=False):
    points = rows[0][0].shape[1] // 2
    out = jax.ShapeDtypeStruct((YN, 3, len(cols) * points, 2 * points), jnp.float32)
    args = [b[kind] for blocks in (rows, cols) for kind in range(2) for b in blocks]
    if not fetch:
        return call(functools.partial(tile_body, cuts), (out, out), (place, *args))
    return pl.pallas_call(
        functools.partial(fetch_body, cuts, len(args)),
        out_shape=(out, out),
        in_specs=[SMEM] + [pl.BlockSpec(memory_space=pl.ANY)] * len(args),
        out_specs=(VMEM, VMEM),
        scratch_shapes=[pltpu.VMEM(v.shape, v.dtype) for v in args] + [pltpu.SemaphoreType.DMA((len(args),))],
        cost_estimate=pl.CostEstimate(flops=0, bytes_accessed=0, transcendentals=0),
        compiler_params=pltpu.CompilerParams(vmem_limit_bytes=56 * 1024 * 1024),
    )(place, *args)


def add_body(place, a, b, out):
    out[...] = a[...] + b[...]


def add(place, a, b):
    return call(add_body, jax.ShapeDtypeStruct(a.shape, a.dtype), (place, a, b))


def call_last(body, out, args, blocks):
    def whole(v):
        zeros = (0,) * len(v.shape)
        return pl.BlockSpec(v.shape, lambda i: zeros)

    def last(b):
        at = b.shape[0] - 1
        return pl.BlockSpec((1,) + b.shape[1:], lambda i: (at, 0, 0))

    return pl.pallas_call(
        body,
        out_shape=out,
        grid=(1,),
        in_specs=[SMEM] + [whole(v) for v in args[1:]] + [last(b) for b in blocks],
        out_specs=whole(out),
        cost_estimate=pl.CostEstimate(flops=0, bytes_accessed=0, transcendentals=0),
        compiler_params=pltpu.CompilerParams(vmem_limit_bytes=32 * 1024 * 1024),
    )(*args, *blocks)


def orbitals_body(place, *refs):
    for i, ref in enumerate(refs[:-1]):
        refs[-1][i] = ref[0]


def orbitals(place, blocks):
    out = jax.ShapeDtypeStruct((len(blocks),) + blocks[0].shape[1:], blocks[0].dtype)
    return call_last(orbitals_body, out, (place,), blocks)


def shift_y(v, d):
    return lax.ppermute(v, "y", [(i, (i + d) % YN) for i in range(YN)])


def add_ring_body(place, a, b, *outs):
    for k, out in enumerate(outs):
        i = (place[1] + k) % YN
        out[...] = a[i] + b[i]


def over_y_ring(place, a, b):
    out = jax.ShapeDtypeStruct(a.shape[1:], a.dtype)
    terms = call(add_ring_body, (out,) * YN, (place, a, b))
    return tuple(shift_y(v, k) if k else v for k, v in enumerate(terms))


def shift_pair(v, d):
    pairs = []
    for x in range(XN):
        for z in range(ZN):
            for y in range(YN):
                to = (y - x) % XN
                source = (x * ZN + z_slot(z)) * YN + y
                pairs.append((source, (to * ZN + z_slot((z + d) % ZN)) * YN + y))
    return lax.ppermute(v, ("x", "l", "h", "y"), pairs)


def geminal_and_rest(t):
    bas = t[2] / SCALES[2]
    return t[0] / SCALES[0], bas * bas * (t[1] / SCALES[1])


def turn_body(place, s, zero, own_g, own_r, *outs):
    core = place[0]
    t = s[0] + s[1] + s[2] + s[3]
    g, r = geminal_and_rest(t)
    points = g.shape[1] // 2
    steps = g.shape[0] // points - 1
    zero[0] = g[:points]
    zero[1] = r[:points]
    own_g[...] = g[points:]
    own_r[...] = r[points:]
    mine, give = outs
    for kind, v in enumerate((g, r)):
        for i in range(steps):
            turned = v[(i + 1) * points : (i + 2) * points].T
            lo, hi = turned[:points], turned[points:]
            mine[kind * steps + i] = jnp.where(core == 0, lo, hi)
            give[kind * steps + i] = jnp.where(core == 0, hi, lo)


def turn(place, s):
    rows, lanes = s.shape[2:]
    points = lanes // 2
    steps = rows // points - 1

    def f32(*shape):
        return jax.ShapeDtypeStruct(shape, jnp.float32)

    outs = (f32(2, points, lanes),) + (f32(rows - points, lanes),) * 2 + (f32(2 * steps, points, points),) * 2
    return call(turn_body, outs, (place, s))


def join_body(place, mine, got, *outs):
    core = place[0]
    for i, out in enumerate(outs):
        a, b = mine[i], got[i]
        out[...] = jnp.concatenate([jnp.where(core == 0, a, b), jnp.where(core == 0, b, a)], axis=1)


def join(place, mine, got):
    n, points, _ = mine.shape
    return call(join_body, (jax.ShapeDtypeStruct((points, 2 * points), jnp.float32),) * n, (place, mine, got))


def last_body(steps, place, zero, own_g, own_r, *refs):
    far, others = refs[:YN], refs[YN : YN + 2 * steps]
    own, other, cols, out = refs[YN + 2 * steps :]
    core, y, x = place[0], place[1], place[2]
    points = zero.shape[1]
    sub = points // YN
    e = lax.rem(y + 2 * lax.rem(x, 2), XN)
    k0 = zero[0] * zero[1]
    q = lax.broadcasted_iota(jnp.int32, k0.shape, 0)
    p = lax.broadcasted_iota(jnp.int32, k0.shape, 1) - core * points
    k0 = jnp.where((e == 0) & (p == q), jnp.float32(0.0), k0)
    g4, r4 = geminal_and_rest(far[0][...] + far[1][...] + far[2][...] + far[3][...])
    kerns = [k0, g4 * r4]
    for i in range(steps):
        at = slice(i * points, (i + 1) * points)
        kerns.append(own_g[at] * others[steps + i][...])
        kerns.append(others[i][...] * own_r[at])
    slabs = [cols[i] for i in range(cols.shape[0])]
    w = squared(jnp.concatenate([jnp.concatenate([c[:points], c[points:]], axis=1) for c in slabs]))
    part = lax.dot_general(
        jnp.concatenate(kerns).astype(jnp.bfloat16), w, (((0,), (0,)), ((), ())), preferred_element_type=jnp.float32
    ) / math.sqrt(NGRID)
    a, b = own[e], other[e]
    w_row = []
    for c in range(2):
        v = jnp.where(core == c, a, b)
        w_row.append(jnp.concatenate([v[:points], v[points:]], axis=1))
    w_row = squared(jnp.concatenate(w_row)).astype(jnp.float32)
    total = jnp.sum(w_row * part, axis=0, keepdims=True) / math.sqrt(NGRID)
    for i in range(2 * YN):
        out[i, :sub] = part[i * sub : (i + 1) * sub]
        out[i, sub:] = jnp.broadcast_to(total, (out.shape[1] - sub, total.shape[1]))


def shards(colloc, coulomb, geminal, occupied):
    points = colloc.shape[0]
    sub = points // YN
    place = jnp.stack([lax.axis_index("c"), lax.axis_index("y"), lax.axis_index("x")]).astype(jnp.int32)

    n_gem = geminal.shape[1] // (2 * LANES)
    n_coul = coulomb.shape[1] // (2 * LANES)
    n_rest = n_coul + colloc.shape[1] // (2 * LANES)
    cuts = ((0, 0, n_gem), (1, 0, n_coul), (1, n_coul, n_rest))
    parts = (geminal, coulomb, colloc)
    given = swap_core(pack(place, parts, True))
    gem, rest = call(
        merge_body,
        tuple(jax.ShapeDtypeStruct((n + 1, 2 * points, LANES), jnp.bfloat16) for n in (n_gem, n_rest)),
        (place, pack(place, parts, False), given, occupied),
    )

    g1, r1 = shift_z(gem, 1), shift_z(rest, -1)
    xfg, xbr = shift_x(gem, 1), shift_x(rest, -1)
    g1, r1, xfg, xbr = tie(g1, r1, xfg, xbr)
    g2, r2 = shift_z(g1, 1), shift_z(r1, -1)
    xfr, xbg = shift_x(rest, 1), shift_x(gem, -1)
    g2, r2, xfr, xbg = tie(g2, r2, xfr, xbg)
    g3, r3 = shift_z(g2, 1), shift_z(r2, -1)
    x2g, x2r = shift_x(xfg, 1), shift_x(xbr, -1)
    g3, r3, x2g, x2r = tie(g3, r3, x2g, x2r)
    rows = ((gem, rest), (xbg, xbr), (x2g, x2r), (xfg, xfr))

    g4, r4 = shift_z(g3, 1), shift_z(r3, -1)
    keep, send = tiles(cuts, place, rows, ((gem, rest), (g1, r1), (g2, r2), (g3, r3)))
    t = add(place, keep, swap_core(send))
    own = orbitals(place, tuple(b[0] for b in rows))
    other = swap_core(own)
    s = over_y(t)

    keep, send = tiles(cuts, place, rows, ((g4, r4),), fetch=True)
    far = over_y_ring(place, keep, swap_core(send))

    orbs = orbitals(place, (gem, g4, g1, r1, g2, r2, g3, r3))
    s, far, orbs, own, other = tie(s, far, orbs, own, other)

    zero, own_g, own_r, mine, give = turn(place, s)
    joined = join(place, mine, swap_core(give))
    steps = len(joined) // 2
    others = [shift_pair(joined[i], -(i + 1)) for i in range(steps)]
    others += [shift_pair(joined[steps + i], i + 1) for i in range(steps)]
    sent = call(
        functools.partial(last_body, steps),
        jax.ShapeDtypeStruct((2 * YN, sub + 8, 2 * LANES), jnp.float32),
        (place, zero, own_g, own_r) + far + tuple(others) + (own, other, orbs),
    )
    sent = lax.ppermute(
        sent, ("x", "y"), [(x * YN + y, (y - x) % XN * YN + y) for x in range(XN) for y in range(YN)]
    )
    got = lax.all_to_all(sent, ("c", "y"), 0, 0, tiled=True)
    pair_field = got[:, :sub].sum(0)
    energy = got[:, sub].sum(0)
    energy = spread(energy[None], ("x", "l", "h"), XN * ZN).sum((0, 1))
    return pair_field, energy


def solution(mesh):
    fine = Mesh(mesh.devices.reshape(4, 2, 2, 4, 4), ("x", "l", "c", "h", "y"))
    grid = ("x", "l", "c", "h")
    in_specs = (P(grid, "y"), P(grid, "y"), P(grid, "y"), P(grid, None))
    out_specs = (P(grid + ("y",), None), P())
    return jax.shard_map(shards, mesh=fine, in_specs=in_specs, out_specs=out_specs, check_vma=False)
```

time: 230 us -> 175 us (0.76)
  matrix products: 31.1 us -> 0 us
  local copies, waits for them, and re-layouts: 26.1 us -> 5.61 us
  waiting for transfers between devices: 83.7 us -> 64.1 us
  blocking collectives: 9.06 us -> 27.6 us
  Pallas kernels: 0 us -> 17.8 us
  starting transfers between devices: 71.6 us -> 56.7 us
  other arithmetic: 5.53 us -> 1.33 us
    dot_general x16 -> x0, matrix products: 31.1 us -> none  [the longest x5 14.5 us: gram(): jnp.einsum('qk,ypk->yqp', cg, row_g, preferred_element_type=jnp.float32)]
    all_to_all x6 -> x1, waiting for transfers between devices: 21.5 us -> 0.01 us  [over_y(): return lax.all_to_all(t, 'y', 0, 0, tiled=True)]
    all_to_all x6 -> x1, starting transfers between devices: 25.4 us -> 4.18 us  [over_y(): return lax.all_to_all(t, 'y', 0, 0, tiled=True)]
    ppermute x4 -> x16, starting transfers between devices: 3.58 us -> 23.5 us  [the longest x6 8.93 us: shift_x(): return lax.ppermute(v, 'x', [(i, (i + d) % XN) for i in range(XN)])]
    all_to_all x1, blocking collectives: 9.06 us -> 27.6 us  [shards(): got = lax.all_to_all(sent, ('c', 'y'), 0, 0, tiled=True)]
    pallas_call x0 -> x12, Pallas kernels: none -> 17.8 us  [the longest x9 10.9 us: call(): pl.pallas_call(body, out_shape=out, in_specs=[SMEM] + [VMEM] * (len(args)...]
    ppermute x8, waiting for transfers between devices: 38.3 us -> 23.9 us  [shift_z(): lax.ppermute(v, ('l', 'h'), [(z_slot(z), z_slot((z + d) % ZN)) for z in r...]
    ppermute x4 -> x16, waiting for transfers between devices: 18.7 us -> 28.9 us  [the longest x6 22.7 us: shift_x(): return lax.ppermute(v, 'x', [(i, (i + d) % XN) for i in range(XN)])]
  transfers between devices with their start and end apart: 25 -> 31, of which waited for: 15 -> 16; matrix products, arithmetic and copies ran while one was open for 25% -> 0% of each run, Pallas kernels for 0% -> 6%
where the time goes in v5:
time: 175 us; the launch traced here: 174 us
  waiting for transfers between devices  64.1 us (37%)
  starting transfers between devices  56.7 us (32%)
  blocking collectives  27.6 us (16%)
  Pallas kernels  17.8 us (10%)
  local copies, waits for them, and re-layouts  5.61 us (3%)
    all_to_all x1, blocking collectives, shards(): got = lax.all_to_all(sent, ('c', 'y'), 0, 0, tiled=True)  27.6 us
    ppermute x8, waiting for transfers between devices, shift_z(): lax.ppermute(v, ('l', 'h'), [(z_slot(z), z_slot((z + d) % ZN)) for z in r...  23.9 us
    ppermute x6, waiting for transfers between devices, shift_x(): return lax.ppermute(v, 'x', [(i, (i + d) % XN) for i in range(XN)])  22.7 us
    ppermute x8, starting transfers between devices, shift_z(): lax.ppermute(v, ('l', 'h'), [(z_slot(z), z_slot((z + d) % ZN)) for z in r...  11 us
    pallas_call x9, Pallas kernels, call(): pl.pallas_call(body, out_shape=out, in_specs=[SMEM] + [VMEM] * (len(args)...  10.9 us
    ppermute x5, starting transfers between devices, swap_core(): return lax.ppermute(v, 'c', [(0, 1), (1, 0)])  10.1 us
    ppermute x6, starting transfers between devices, shift_x(): return lax.ppermute(v, 'x', [(i, (i + d) % XN) for i in range(XN)])  8.93 us
    ppermute x6, starting transfers between devices, shift_pair(): return lax.ppermute(v, ('x', 'l', 'h', 'y'), pairs)  8.84 us
  transfers between devices with their start and end apart: 31, of which 16 were waited for; matrix products, arithmetic and copies ran while one was open for 0% of the time, Pallas kernels for 6%

profile of v5, /device:TPU:1, one launch (start us, length us, event | category | flops | bytes accessed | tf_op | source)
XLA Modules:
  0.0 174.2 jit_solution(16693987586883361599)
XLA Ops:
  0.6 0.1 pad_add_fusion.place
  0.7 1.1 copy-done.22
  1.8 1.0 copy-done.23
  2.8 0.9 copy-done.24
  3.8 0.7 shard_map.60
  4.5 3.3 %collective-permute-start = (bf16[40,64,128]{2,1,0:T(8,128)(2,1)S(1)}, bf16[40,64,128]{2,1,0:T(8,128)(2,1)S(1)}, u32[]{:S(2)}, u32[]{:S(2)}) collective-permute-start(bf16[40,64,128]{2,1,0:T(8,128)(2,1)S(1)} %shard_map.60), channel_id=1, source_target_pairs={{0,16},{16,0},{1,17},{17,1},{2,18},{18,2},{3,19},{19,3},{4,20},{20... | collective-permute-start | bytes 1966088 | tf_op jit(solution)/shard_map/ppermute | solution.py:42
  7.8 0.7 shard_map.59.kept
  8.5 1.0 collective-permute-done.got
  9.5 0.6 shard_map.61
  10.2 0.1 collective-permute-start.1
  10.3 1.1 collective-permute-start.3
  11.4 4.0 %collective-permute-start.2 = (bf16[21,128,128]{2,1,0:T(8,128)(2,1)S(1)}, bf16[21,128,128]{2,1,0:T(8,128)(2,1)S(1)}, u32[]{:S(2)}, u32[]{:S(2)}) collective-permute-start(bf16[21,128,128]{2,1,0:T(8,128)(2,1)S(1)} %get-tuple-element.44.refs_4_.refs_12_), channel_id=1, source_target_pairs={{0,44},{32,0},{4,32},{36,4},{8,36},{40,8},{12,40},{44,12},{1,45},{... | collective-permute-start | bytes 2064392 | tf_op jit(solution)/shard_map/ppermute | solution.py:34
  15.4 1.5 collective-permute-start.4
  16.9 1.3 collective-permute-start.8
  18.1 11.5 %collective-permute-done.1.refs_9_.refs_2_ = bf16[21,128,128]{2,1,0:T(8,128)(2,1)S(1)} collective-permute-done((bf16[21,128,128]{2,1,0:T(8,128)(2,1)S(1)}, bf16[21,128,128]{2,1,0:T(8,128)(2,1)S(1)}, u32[]{:S(2)}, u32[]{:S(2)}) %collective-permute-start.1) | collective-permute-done | bytes 688160 | tf_op jit(solution)/shard_map/ppermute | solution.py:34
  29.6 1.2 collective-permute-start.7
  30.9 0.6 collective-permute-done.4.refs_5_
  31.4 2.7 %collective-permute-start.6 = (bf16[21,128,128]{2,1,0:T(8,128)(2,1)S(1)}, bf16[21,128,128]{2,1,0:T(8,128)(2,1)S(1)}, u32[]{:S(2)}, u32[]{:S(2)}) collective-permute-start(bf16[21,128,128]{2,1,0:T(8,128)(2,1)S(1)} %collective-permute-done.2.refs_13_.refs_3_), channel_id=1, source_target_pairs={{0,44},{32,0},{4,32},{36,4},{8,36},{40,8},{12,40},{44,12},{1,45},{... | collective-permute-start | bytes 2064392 | tf_op jit(solution)/shard_map/ppermute | solution.py:34
  34.1 1.2 collective-permute-start.11
  35.3 10.9 %collective-permute-done.8.refs_1_ = bf16[21,128,128]{2,1,0:T(8,128)(2,1)S(1)} collective-permute-done((bf16[21,128,128]{2,1,0:T(8,128)(2,1)S(1)}, bf16[21,128,128]{2,1,0:T(8,128)(2,1)S(1)}, u32[]{:S(2)}, u32[]{:S(2)}) %collective-permute-start.8) | collective-permute-done | bytes 688160 | tf_op jit(solution)/shard_map/ppermute | solution.py:38
  46.2 2.7 %collective-permute-start.12 = (bf16[21,128,128]{2,1,0:T(8,128)(2,1)S(1)}, bf16[21,128,128]{2,1,0:T(8,128)(2,1)S(1)}, u32[]{:S(2)}, u32[]{:S(2)}) collective-permute-start(bf16[21,128,128]{2,1,0:T(8,128)(2,1)S(1)} %collective-permute-done.4.refs_5_), channel_id=1, source_target_pairs={{0,192},{64,0},{128,64},{192,128},{1,193},{65,1},{129,65},{193,129... | collective-permute-start | bytes 2064392 | tf_op jit(solution)/shard_map/ppermute | solution.py:38
  48.9 1.2 collective-permute-start.10
  50.0 0.4 collective-permute-start.9
  50.4 11.3 %collective-permute-done.11.refs_2_ = bf16[21,128,128]{2,1,0:T(8,128)(2,1)S(1)} collective-permute-done((bf16[21,128,128]{2,1,0:T(8,128)(2,1)S(1)}, bf16[21,128,128]{2,1,0:T(8,128)(2,1)S(1)}, u32[]{:S(2)}, u32[]{:S(2)}) %collective-permute-start.11) | collective-permute-done | bytes 688160 | tf_op jit(solution)/shard_map/ppermute | solution.py:38
  61.8 2.1 %collective-permute-done.10.refs_15_.refs_7_ = bf16[21,128,128]{2,1,0:T(8,128)(2,1)} collective-permute-done((bf16[21,128,128]{2,1,0:T(8,128)(2,1)S(1)}, bf16[21,128,128]{2,1,0:T(8,128)(2,1)}, u32[]{:S(2)}, u32[]{:S(2)}) %collective-permute-start.10) | collective-permute-done | bytes 688160 | tf_op jit(solution)/shard_map/ppermute | solution.py:34
  63.9 1.0 collective-permute-done.9.refs_11_.refs_6_
  64.9 4.2 %shard_map.62 = (f32[4,3,256,128]{3,2,1,0:T(8,128)S(1)}, f32[4,3,256,128]{3,2,1,0:T(8,128)S(1)}) custom-call(s32[3]{0:T(128)S(1)} %pad_add_fusion.place, bf16[21,128,128]{2,1,0:T(8,128)(2,1)S(1)} %get-tuple-element.43.refs_0_.refs_8_, bf16[21,128,128]{2,1,0:T(8,128)(2,1)S(1)} %collective-permute-done.8.refs_1_, ...), custom_call_target="tpu_custom_call" | custom-call | tf_op jit(solution)/shard_map/pallas_call | solution.py:60
  69.2 4.4 %collective-permute-start.13 = (f32[4,3,256,128]{3,2,1,0:T(8,128)S(1)}, f32[4,3,256,128]{3,2,1,0:T(8,128)S(1)}, u32[]{:S(2)}, u32[]{:S(2)}) collective-permute-start(f32[4,3,256,128]{3,2,1,0:T(8,128)S(1)} %get-tuple-element.58), channel_id=1, source_target_pairs={{0,16},{16,0},{1,17},{17,1},{2,18},{18,2},{3,19},{19,3},{4,20},{20... | collective-permute-start | bytes 4718600 | tf_op jit(solution)/shard_map/ppermute | solution.py:42
  73.7 2.7 %collective-permute-start.15 = (bf16[21,128,128]{2,1,0:T(8,128)(2,1)}, bf16[21,128,128]{2,1,0:T(8,128)(2,1)}, u32[]{:S(2)}, u32[]{:S(2)}) collective-permute-start(bf16[21,128,128]{2,1,0:T(8,128)(2,1)} %collective-permute-done.10.refs_15_.refs_7_), channel_id=1, source_target_pairs={{0,44},{32,0},{4,32},{36,4},{8,36},{40,8},{12,40},{44,12},{1,45},{... | collective-permute-start | bytes 2064392 | tf_op jit(solution)/shard_map/ppermute | solution.py:34
  76.3 0.3 collective-permute-done.13.b
  76.7 1.9 %shard_map.63 = f32[4,3,256,128]{3,2,1,0:T(8,128)} custom-call(s32[3]{0:T(128)S(1)} %pad_add_fusion.place, f32[4,3,256,128]{3,2,1,0:T(8,128)S(1)} %get-tuple-element.57.a, f32[4,3,256,128]{3,2,1,0:T(8,128)S(1)} %collective-permute-done.13.b), custom_call_target="tpu_custom_call" | custom-call | tf_op jit(solution)/shard_map/pallas_call | solution.py:60
  78.6 4.2 %all-to-all-start = ((f32[4,3,256,128]{3,2,1,0:T(8,128)}), f32[4,3,256,128]{3,2,1,0:T(8,128)S(1)}, u32[]{:S(2)}, u32[]{:S(2)}) async-start(f32[4,3,256,128]{3,2,1,0:T(8,128)} %shard_map.63), calls=%async_computation | async-start | bytes 3145728 | tf_op jit(solution)/shard_map/all_to_all | solution.py:50
  82.8 9.3 %collective-permute-done.14.refs_8_.refs_1_ = bf16[21,128,128]{2,1,0:T(8,128)(2,1)S(1)} collective-permute-done((bf16[21,128,128]{2,1,0:T(8,128)(2,1)}, bf16[21,128,128]{2,1,0:T(8,128)(2,1)S(1)}, u32[]{:S(2)}, u32[]{:S(2)}) %collective-permute-start.14) | collective-permute-done | bytes 688160 | tf_op jit(solution)/shard_map/ppermute | solution.py:34
  92.1 0.8 copy-done.17
  92.9 5.6 %shard_map.64 = (f32[4,3,64,128]{3,2,1,0:T(8,128)}, f32[4,3,64,128]{3,2,1,0:T(8,128)}) custom-call(s32[3]{0:T(128)} %copy-done.26, bf16[21,128,128]{2,1,0:T(8,128)(2,1)} %copy-done, bf16[21,128,128]{2,1,0:T(8,128)(2,1)} %copy-done.4, bf16[21,128,128]{2,1,0:T(8,128)(2,1)} %copy-done.6, bf16[21,128,128]{2,1,0:T(8,128)(2,1)} %copy-done.2, ...), custom_call_target="tpu_custom_call" | custom-call | tf_op jit(solution)/shard_map/pallas_call | solution.py:147
  98.5 1.0 collective-permute-start.16
  99.5 0.6 shard_map.67.refs_10_
  100.1 0.1 collective-permute-start.20
  100.2 0.9 collective-permute-done.16.b
  101.1 1.0 copy-done.25
  102.1 0.6 shard_map.65
  102.7 1.4 collective-permute-start.17
  104.0 2.6 %collective-permute-start.18 = (f32[3,64,128]{2,1,0:T(8,128)S(1)}, f32[3,64,128]{2,1,0:T(8,128)S(1)}, u32[]{:S(2)}, u32[]{:S(2)}) collective-permute-start(f32[3,64,128]{2,1,0:T(8,128)S(1)} %get-tuple-element.63), channel_id=1, source_target_pairs={{0,2},{1,3},{2,0},{3,1},{4,6},{5,7},{6,4},{7,5},{8,10},{9,11},{10,... | collective-permute-start | bytes 294920 | tf_op jit(solution)/shard_map/ppermute | solution.py:197
  106.7 1.1 collective-permute-start.19
  107.7 0.8 shard_map.66.refs_12_
  108.6 2.7 %collective-permute-done.18.refs_2_ = f32[3,64,128]{2,1,0:T(8,128)S(1)} collective-permute-done((f32[3,64,128]{2,1,0:T(8,128)S(1)}, f32[3,64,128]{2,1,0:T(8,128)S(1)}, u32[]{:S(2)}, u32[]{:S(2)}) %collective-permute-start.18) | collective-permute-done | bytes 98336 | tf_op jit(solution)/shard_map/ppermute | solution.py:197
  111.3 0.7 shard_map.68
  112.0 1.3 collective-permute-start.21
  113.3 1.1 collective-permute-done.21.got
  114.4 0.7 shard_map.69
  115.1 2.0 %collective-permute-start.22 = (f32[64,128]{1,0:T(8,128)S(1)}, f32[64,128]{1,0:T(8,128)S(1)}, u32[]{:S(2)}, u32[]{:S(2)}) collective-permute-start(f32[64,128]{1,0:T(8,128)S(1)} %get-tuple-element.75), channel_id=1, source_target_pairs={{0,44},{1,109},{2,174},{3,239},{32,0},{33,65},{34,130},{35,195},{4... | collective-permute-start | bytes 98312 | tf_op jit(solution)/shard_map/ppermute | solution.py:220
  117.1 2.9 %collective-permute-start.24 = (f32[64,128]{1,0:T(8,128)S(1)}, f32[64,128]{1,0:T(8,128)S(1)}, u32[]{:S(2)}, u32[]{:S(2)}) collective-permute-start(f32[64,128]{1,0:T(8,128)S(1)} %get-tuple-element.77), channel_id=1, source_target_pairs={{0,40},{1,105},{2,170},{3,235},{32,12},{33,77},{34,142},{35,207},{... | collective-permute-start | bytes 98312 | tf_op jit(solution)/shard_map/ppermute | solution.py:220
  120.0 1.4 collective-permute-start.25
  121.4 2.5 %collective-permute-start.27 = (f32[64,128]{1,0:T(8,128)S(1)}, f32[64,128]{1,0:T(8,128)S(1)}, u32[]{:S(2)}, u32[]{:S(2)}) collective-permute-start(f32[64,128]{1,0:T(8,128)S(1)} %get-tuple-element.80), channel_id=1, source_target_pairs={{0,36},{1,101},{2,166},{3,231},{32,8},{33,73},{34,138},{35,203},{4... | collective-permute-start | bytes 98312 | tf_op jit(solution)/shard_map/ppermute | solution.py:220
  124.0 2.5 %collective-permute-done.26.refs_8_ = f32[64,128]{1,0:T(8,128)S(1)} collective-permute-done((f32[64,128]{1,0:T(8,128)S(1)}, f32[64,128]{1,0:T(8,128)S(1)}, u32[]{:S(2)}, u32[]{:S(2)}) %collective-permute-start.26) | collective-permute-done | bytes 32800 | tf_op jit(solution)/shard_map/ppermute | solution.py:220
  126.5 0.9 collective-permute-done.27.refs_9_
  127.3 0.8 shard_map.70
  128.1 0.7 collective-permute-start.28
  128.8 27.6 %all_to_all.15 = f32[8,24,256]{2,1,0:T(8,128)S(1)} all-to-all(f32[8,24,256]{2,1,0:T(8,128)S(1)} %collective-permute-done.28), channel_id=1, replica_groups=mesh['x'=4,'l'=2,'c'=2,'h'=4,'y'=4] {'c','y'}, dimensions={0} | all-to-all | bytes 393216 | tf_op jit(solution)/shard_map/all_to_all | solution.py:359
  156.4 0.6 broadcast_in_dim.4
  157.1 7.9 %all-to-all-start.2 = ((f32[32,1,256]{2,1,0:T(1,128)}), f32[32,1,256]{2,1,0:T(1,128)S(1)}, u32[]{:S(2)}, u32[]{:S(2)}) async-start(f32[32,1,256]{2,1,0:T(1,128)} %broadcast_in_dim.4), calls=%async_computation.2 | async-start | bytes 65536 | tf_op jit(solution)/shard_map/all_to_all | solution.py:46
  165.0 0.6 slice_reduce_fusion
  165.6 8.0 %all-to-all-done.2 = f32[32,1,256]{2,1,0:T(1,128)S(1)} async-done(((f32[32,1,256]{2,1,0:T(1,128)}), f32[32,1,256]{2,1,0:T(1,128)S(1)}, u32[]{:S(2)}, u32[]{:S(2)}) %all-to-all-start.2) | async-done | bytes 32800 | tf_op jit(solution)/shard_map/all_to_all | solution.py:46
  173.6 0.6 reduce_sum.29
  (74 shorter events, 0.2 us)
Async XLA Ops:
  0.7 1.1 copy-start.22
  1.8 1.0 copy-start.23
  2.8 0.9 copy-start.24
  3.7 72.9 %copy-start.26 = (s32[3]{0:T(128)}, s32[3]{0:T(128)S(1)}, u32[]{:S(2)}) copy-start(s32[3]{0:T(128)S(1)} %pad_add_fusion.place) | copy-start | bytes 40
  3.8 5.8 %copy-start.28 = (bf16[64,256]{1,0:T(8,128)(2,1)S(1)}, bf16[64,256]{1,0:T(8,128)(2,1)}, u32[]{:S(2)}) copy-start(bf16[64,256]{1,0:T(8,128)(2,1)} %occ.1) | copy-start | bytes 98308
  4.5 5.1 %collective-permute-start = (bf16[40,64,128]{2,1,0:T(8,128)(2,1)S(1)}, bf16[40,64,128]{2,1,0:T(8,128)(2,1)S(1)}, u32[]{:S(2)}, u32[]{:S(2)}) collective-permute-start(bf16[40,64,128]{2,1,0:T(8,128)(2,1)S(1)} %shard_map.60), channel_id=1, source_target_pairs={{0,16},{16,0},{1,17},{17,1},{2,18},{18,2},{3,19},{19,3},{4,20},{20... | collective-permute-start | bytes 1966088 | tf_op jit(solution)/shard_map/ppermute | solution.py:42
  10.2 59.0 %copy-start = (bf16[21,128,128]{2,1,0:T(8,128)(2,1)}, bf16[21,128,128]{2,1,0:T(8,128)(2,1)S(1)}, u32[]{:S(2)}) copy-start(bf16[21,128,128]{2,1,0:T(8,128)(2,1)S(1)} %get-tuple-element.43.refs_0_.refs_8_) | copy-start | bytes 2064388
  10.2 59.0 %copy-start.8 = (bf16[21,128,128]{2,1,0:T(8,128)(2,1)}, bf16[21,128,128]{2,1,0:T(8,128)(2,1)S(1)}, u32[]{:S(2)}) copy-start(bf16[21,128,128]{2,1,0:T(8,128)(2,1)S(1)} %get-tuple-element.44.refs_4_.refs_12_) | copy-start | bytes 2064388
  10.2 19.4 %collective-permute-start.1 = (bf16[21,128,128]{2,1,0:T(8,128)(2,1)S(1)}, bf16[21,128,128]{2,1,0:T(8,128)(2,1)S(1)}, u32[]{:S(2)}, u32[]{:S(2)}) collective-permute-start(bf16[21,128,128]{2,1,0:T(8,128)(2,1)S(1)} %get-tuple-element.43.refs_0_.refs_8_), channel_id=1, source_target_pairs={{0,32},{32,4},{4,36},{36,8},{8,40},{40,12},{12,44},{44,0},{1,33},{... | collective-permute-start | bytes 2064392 | tf_op jit(solution)/shard_map/ppermute | solution.py:34
  10.3 20.5 %collective-permute-start.3 = (bf16[21,128,128]{2,1,0:T(8,128)(2,1)S(1)}, bf16[21,128,128]{2,1,0:T(8,128)(2,1)S(1)}, u32[]{:S(2)}, u32[]{:S(2)}) collective-permute-start(bf16[21,128,128]{2,1,0:T(8,128)(2,1)S(1)} %get-tuple-element.43.refs_0_.refs_8_), channel_id=1, source_target_pairs={{0,64},{64,128},{128,192},{192,0},{1,65},{65,129},{129,193},{193,1... | collective-permute-start | bytes 2064392 | tf_op jit(solution)/shard_map/ppermute | solution.py:38
  11.4 19.5 %collective-permute-start.2 = (bf16[21,128,128]{2,1,0:T(8,128)(2,1)S(1)}, bf16[21,128,128]{2,1,0:T(8,128)(2,1)S(1)}, u32[]{:S(2)}, u32[]{:S(2)}) collective-permute-start(bf16[21,128,128]{2,1,0:T(8,128)(2,1)S(1)} %get-tuple-element.44.refs_4_.refs_12_), channel_id=1, source_target_pairs={{0,44},{32,0},{4,32},{36,4},{8,36},{40,8},{12,40},{44,12},{1,45},{... | collective-permute-start | bytes 2064392 | tf_op jit(solution)/shard_map/ppermute | solution.py:34
  15.4 16.0 %collective-permute-start.4 = (bf16[21,128,128]{2,1,0:T(8,128)(2,1)S(1)}, bf16[21,128,128]{2,1,0:T(8,128)(2,1)S(1)}, u32[]{:S(2)}, u32[]{:S(2)}) collective-permute-start(bf16[21,128,128]{2,1,0:T(8,128)(2,1)S(1)} %get-tuple-element.44.refs_4_.refs_12_), channel_id=1, source_target_pairs={{0,192},{64,0},{128,64},{192,128},{1,193},{65,1},{129,65},{193,129... | collective-permute-start | bytes 2064392 | tf_op jit(solution)/shard_map/ppermute | solution.py:38
  16.9 29.3 %collective-permute-start.8 = (bf16[21,128,128]{2,1,0:T(8,128)(2,1)S(1)}, bf16[21,128,128]{2,1,0:T(8,128)(2,1)S(1)}, u32[]{:S(2)}, u32[]{:S(2)}) collective-permute-start(bf16[21,128,128]{2,1,0:T(8,128)(2,1)S(1)} %get-tuple-element.43.refs_0_.refs_8_), channel_id=1, source_target_pairs={{0,192},{64,0},{128,64},{192,128},{1,193},{65,1},{129,65},{193,129... | collective-permute-start | bytes 2064392 | tf_op jit(solution)/shard_map/ppermute | solution.py:38
  29.6 39.5 %copy-start.9 = (bf16[21,128,128]{2,1,0:T(8,128)(2,1)}, bf16[21,128,128]{2,1,0:T(8,128)(2,1)S(1)}, u32[]{:S(2)}) copy-start(bf16[21,128,128]{2,1,0:T(8,128)(2,1)S(1)} %collective-permute-done.1.refs_9_.refs_2_) | copy-start | bytes 2064388
  29.6 19.2 %collective-permute-start.7 = (bf16[21,128,128]{2,1,0:T(8,128)(2,1)S(1)}, bf16[21,128,128]{2,1,0:T(8,128)(2,1)S(1)}, u32[]{:S(2)}, u32[]{:S(2)}) collective-permute-start(bf16[21,128,128]{2,1,0:T(8,128)(2,1)S(1)} %get-tuple-element.44.refs_4_.refs_12_), channel_id=1, source_target_pairs={{0,64},{64,128},{128,192},{192,0},{1,65},{65,129},{129,193},{193,1... | collective-permute-start | bytes 2064392 | tf_op jit(solution)/shard_map/ppermute | solution.py:38
  30.8 38.3 %copy-start.2 = (bf16[21,128,128]{2,1,0:T(8,128)(2,1)}, bf16[21,128,128]{2,1,0:T(8,128)(2,1)S(1)}, u32[]{:S(2)}) copy-start(bf16[21,128,128]{2,1,0:T(8,128)(2,1)S(1)} %collective-permute-done.3.refs_3_) | copy-start | bytes 2064388
  30.8 38.3 %copy-start.11 = (bf16[21,128,128]{2,1,0:T(8,128)(2,1)}, bf16[21,128,128]{2,1,0:T(8,128)(2,1)S(1)}, u32[]{:S(2)}) copy-start(bf16[21,128,128]{2,1,0:T(8,128)(2,1)S(1)} %collective-permute-done.2.refs_13_.refs_3_) | copy-start | bytes 2064388
  31.4 37.8 %copy-start.19 = (bf16[21,128,128]{2,1,0:T(8,128)(2,1)}, bf16[21,128,128]{2,1,0:T(8,128)(2,1)S(1)}, u32[]{:S(2)}) copy-start(bf16[21,128,128]{2,1,0:T(8,128)(2,1)S(1)} %collective-permute-done.4.refs_5_) | copy-start | bytes 2064388
  31.4 17.4 %collective-permute-start.5 = (bf16[21,128,128]{2,1,0:T(8,128)(2,1)S(1)}, bf16[21,128,128]{2,1,0:T(8,128)(2,1)S(1)}, u32[]{:S(2)}, u32[]{:S(2)}) collective-permute-start(bf16[21,128,128]{2,1,0:T(8,128)(2,1)S(1)} %collective-permute-done.1.refs_9_.refs_2_), channel_id=1, source_target_pairs={{0,32},{32,4},{4,36},{36,8},{8,40},{40,12},{12,44},{44,0},{1,33},{... | collective-permute-start | bytes 2064392 | tf_op jit(solution)/shard_map/ppermute | solution.py:34
  31.4 17.4 %collective-permute-start.6 = (bf16[21,128,128]{2,1,0:T(8,128)(2,1)S(1)}, bf16[21,128,128]{2,1,0:T(8,128)(2,1)S(1)}, u32[]{:S(2)}, u32[]{:S(2)}) collective-permute-start(bf16[21,128,128]{2,1,0:T(8,128)(2,1)S(1)} %collective-permute-done.2.refs_13_.refs_3_), channel_id=1, source_target_pairs={{0,44},{32,0},{4,32},{36,4},{8,36},{40,8},{12,40},{44,12},{1,45},{... | collective-permute-start | bytes 2064392 | tf_op jit(solution)/shard_map/ppermute | solution.py:34
  34.1 27.7 %collective-permute-start.11 = (bf16[21,128,128]{2,1,0:T(8,128)(2,1)S(1)}, bf16[21,128,128]{2,1,0:T(8,128)(2,1)S(1)}, u32[]{:S(2)}, u32[]{:S(2)}) collective-permute-start(bf16[21,128,128]{2,1,0:T(8,128)(2,1)S(1)} %collective-permute-done.3.refs_3_), channel_id=1, source_target_pairs={{0,64},{64,128},{128,192},{192,0},{1,65},{65,129},{129,193},{193,1... | collective-permute-start | bytes 2064392 | tf_op jit(solution)/shard_map/ppermute | solution.py:38
  46.2 23.0 %copy-start.4 = (bf16[21,128,128]{2,1,0:T(8,128)(2,1)}, bf16[21,128,128]{2,1,0:T(8,128)(2,1)S(1)}, u32[]{:S(2)}) copy-start(bf16[21,128,128]{2,1,0:T(8,128)(2,1)S(1)} %collective-permute-done.8.refs_1_) | copy-start | bytes 2064388
  46.2 15.6 %collective-permute-start.12 = (bf16[21,128,128]{2,1,0:T(8,128)(2,1)S(1)}, bf16[21,128,128]{2,1,0:T(8,128)(2,1)S(1)}, u32[]{:S(2)}, u32[]{:S(2)}) collective-permute-start(bf16[21,128,128]{2,1,0:T(8,128)(2,1)S(1)} %collective-permute-done.4.refs_5_), channel_id=1, source_target_pairs={{0,192},{64,0},{128,64},{192,128},{1,193},{65,1},{129,65},{193,129... | collective-permute-start | bytes 2064392 | tf_op jit(solution)/shard_map/ppermute | solution.py:38
  48.8 20.4 %copy-start.20 = (bf16[21,128,128]{2,1,0:T(8,128)(2,1)}, bf16[21,128,128]{2,1,0:T(8,128)(2,1)S(1)}, u32[]{:S(2)}) copy-start(bf16[21,128,128]{2,1,0:T(8,128)(2,1)S(1)} %collective-permute-done.7.refs_7_) | copy-start | bytes 2064388
  48.9 20.4 %copy-start.13 = (bf16[21,128,128]{2,1,0:T(8,128)(2,1)}, bf16[21,128,128]{2,1,0:T(8,128)(2,1)S(1)}, u32[]{:S(2)}) copy-start(bf16[21,128,128]{2,1,0:T(8,128)(2,1)S(1)} %collective-permute-done.5.refs_10_.refs_4_) | copy-start | bytes 2064388
  48.9 20.3 %copy-start.15 = (bf16[21,128,128]{2,1,0:T(8,128)(2,1)}, bf16[21,128,128]{2,1,0:T(8,128)(2,1)S(1)}, u32[]{:S(2)}) copy-start(bf16[21,128,128]{2,1,0:T(8,128)(2,1)S(1)} %collective-permute-done.6.refs_14_.refs_5_) | copy-start | bytes 2064388
  48.9 15.0 %collective-permute-start.10 = (bf16[21,128,128]{2,1,0:T(8,128)(2,1)S(1)}, bf16[21,128,128]{2,1,0:T(8,128)(2,1)}, u32[]{:S(2)}, u32[]{:S(2)}) collective-permute-start(bf16[21,128,128]{2,1,0:T(8,128)(2,1)S(1)} %collective-permute-done.6.refs_14_.refs_5_), channel_id=1, source_target_pairs={{0,44},{32,0},{4,32},{36,4},{8,36},{40,8},{12,40},{44,12},{1,45},{... | collective-permute-start | bytes 2064392 | tf_op jit(solution)/shard_map/ppermute | solution.py:34
  50.0 14.8 %collective-permute-start.9 = (bf16[21,128,128]{2,1,0:T(8,128)(2,1)S(1)}, bf16[21,128,128]{2,1,0:T(8,128)(2,1)}, u32[]{:S(2)}, u32[]{:S(2)}) collective-permute-start(bf16[21,128,128]{2,1,0:T(8,128)(2,1)S(1)} %collective-permute-done.5.refs_10_.refs_4_), channel_id=1, source_target_pairs={{0,32},{32,4},{4,36},{36,8},{8,40},{40,12},{12,44},{44,0},{1,33},{... | collective-permute-start | bytes 2064392 | tf_op jit(solution)/shard_map/ppermute | solution.py:34
  61.8 7.5 %copy-start.6 = (bf16[21,128,128]{2,1,0:T(8,128)(2,1)}, bf16[21,128,128]{2,1,0:T(8,128)(2,1)S(1)}, u32[]{:S(2)}) copy-start(bf16[21,128,128]{2,1,0:T(8,128)(2,1)S(1)} %collective-permute-done.11.refs_2_) | copy-start | bytes 2064388
  61.8 7.5 %copy-start.21 = (bf16[21,128,128]{2,1,0:T(8,128)(2,1)}, bf16[21,128,128]{2,1,0:T(8,128)(2,1)S(1)}, u32[]{:S(2)}) copy-start(bf16[21,128,128]{2,1,0:T(8,128)(2,1)S(1)} %collective-permute-done.12.refs_6_) | copy-start | bytes 2064388
  69.2 7.4 %collective-permute-start.13 = (f32[4,3,256,128]{3,2,1,0:T(8,128)S(1)}, f32[4,3,256,128]{3,2,1,0:T(8,128)S(1)}, u32[]{:S(2)}, u32[]{:S(2)}) collective-permute-start(f32[4,3,256,128]{3,2,1,0:T(8,128)S(1)} %get-tuple-element.58), channel_id=1, source_target_pairs={{0,16},{16,0},{1,17},{17,1},{2,18},{18,2},{3,19},{19,3},{4,20},{20... | collective-permute-start | bytes 4718600 | tf_op jit(solution)/shard_map/ppermute | solution.py:42
  73.7 18.4 %collective-permute-start.14 = (bf16[21,128,128]{2,1,0:T(8,128)(2,1)}, bf16[21,128,128]{2,1,0:T(8,128)(2,1)S(1)}, u32[]{:S(2)}, u32[]{:S(2)}) collective-permute-start(bf16[21,128,128]{2,1,0:T(8,128)(2,1)} %collective-permute-done.9.refs_11_.refs_6_), channel_id=1, source_target_pairs={{0,32},{32,4},{4,36},{36,8},{8,40},{40,12},{12,44},{44,0},{1,33},{... | collective-permute-start | bytes 2064392 | tf_op jit(solution)/shard_map/ppermute | solution.py:34
  73.7 18.4 %collective-permute-start.15 = (bf16[21,128,128]{2,1,0:T(8,128)(2,1)}, bf16[21,128,128]{2,1,0:T(8,128)(2,1)}, u32[]{:S(2)}, u32[]{:S(2)}) collective-permute-start(bf16[21,128,128]{2,1,0:T(8,128)(2,1)} %collective-permute-done.10.refs_15_.refs_7_), channel_id=1, source_target_pairs={{0,44},{32,0},{4,32},{36,4},{8,36},{40,8},{12,40},{44,12},{1,45},{... | collective-permute-start | bytes 2064392 | tf_op jit(solution)/shard_map/ppermute | solution.py:34
  78.6 32.7 %all-to-all-start = ((f32[4,3,256,128]{3,2,1,0:T(8,128)}), f32[4,3,256,128]{3,2,1,0:T(8,128)S(1)}, u32[]{:S(2)}, u32[]{:S(2)}) async-start(f32[4,3,256,128]{3,2,1,0:T(8,128)} %shard_map.63), calls=%async_computation | async-start | bytes 3145728 | tf_op jit(solution)/shard_map/all_to_all | solution.py:50
  82.7 16.8 %copy-start.1 = (bf16[21,128,128]{2,1,0:T(8,128)(2,1)S(1)}, bf16[21,128,128]{2,1,0:T(8,128)(2,1)}, u32[]{:S(2)}) copy-start(bf16[21,128,128]{2,1,0:T(8,128)(2,1)} %copy-done) | copy-start | bytes 2064388
  82.7 16.8 %copy-start.3 = (bf16[21,128,128]{2,1,0:T(8,128)(2,1)S(1)}, bf16[21,128,128]{2,1,0:T(8,128)(2,1)}, u32[]{:S(2)}) copy-start(bf16[21,128,128]{2,1,0:T(8,128)(2,1)} %copy-done.2) | copy-start | bytes 2064388
  82.7 16.8 %copy-start.5 = (bf16[21,128,128]{2,1,0:T(8,128)(2,1)S(1)}, bf16[21,128,128]{2,1,0:T(8,128)(2,1)}, u32[]{:S(2)}) copy-start(bf16[21,128,128]{2,1,0:T(8,128)(2,1)} %copy-done.4) | copy-start | bytes 2064388
  82.8 16.8 %copy-start.7 = (bf16[21,128,128]{2,1,0:T(8,128)(2,1)S(1)}, bf16[21,128,128]{2,1,0:T(8,128)(2,1)}, u32[]{:S(2)}) copy-start(bf16[21,128,128]{2,1,0:T(8,128)(2,1)} %copy-done.6) | copy-start | bytes 2064388
  82.8 16.8 %copy-start.27 = (s32[3]{0:T(128)S(1)}, s32[3]{0:T(128)}, u32[]{:S(2)}) copy-start(s32[3]{0:T(128)} %copy-done.26) | copy-start | bytes 40
  92.1 0.8 copy-start.17
  98.5 9.2 %copy-start.10 = (bf16[21,128,128]{2,1,0:T(8,128)(2,1)S(1)}, bf16[21,128,128]{2,1,0:T(8,128)(2,1)}, u32[]{:S(2)}) copy-start(bf16[21,128,128]{2,1,0:T(8,128)(2,1)} %copy-done.9) | copy-start | bytes 2064388
  98.5 9.2 %copy-start.12 = (bf16[21,128,128]{2,1,0:T(8,128)(2,1)S(1)}, bf16[21,128,128]{2,1,0:T(8,128)(2,1)}, u32[]{:S(2)}) copy-start(bf16[21,128,128]{2,1,0:T(8,128)(2,1)} %copy-done.11) | copy-start | bytes 2064388
  98.5 9.2 %copy-start.14 = (bf16[21,128,128]{2,1,0:T(8,128)(2,1)S(1)}, bf16[21,128,128]{2,1,0:T(8,128)(2,1)}, u32[]{:S(2)}) copy-start(bf16[21,128,128]{2,1,0:T(8,128)(2,1)} %copy-done.13) | copy-start | bytes 2064388
  98.5 9.2 %copy-start.16 = (bf16[21,128,128]{2,1,0:T(8,128)(2,1)S(1)}, bf16[21,128,128]{2,1,0:T(8,128)(2,1)}, u32[]{:S(2)}) copy-start(bf16[21,128,128]{2,1,0:T(8,128)(2,1)} %copy-done.15) | copy-start | bytes 2064388
  98.5 9.2 %copy-start.18 = (bf16[21,128,128]{2,1,0:T(8,128)(2,1)S(1)}, bf16[21,128,128]{2,1,0:T(8,128)(2,1)}, u32[]{:S(2)}) copy-start(bf16[21,128,128]{2,1,0:T(8,128)(2,1)} %copy-done.17) | copy-start | bytes 2064388
  98.5 2.5 %collective-permute-start.16 = (f32[4,3,64,128]{3,2,1,0:T(8,128)}, f32[4,3,64,128]{3,2,1,0:T(8,128)S(1)}, u32[]{:S(2)}, u32[]{:S(2)}) collective-permute-start(f32[4,3,64,128]{3,2,1,0:T(8,128)} %get-tuple-element.60), channel_id=1, source_target_pairs={{0,16},{16,0},{1,17},{17,1},{2,18},{18,2},{3,19},{19,3},{4,20},{20... | collective-permute-start | bytes 1179656 | tf_op jit(solution)/shard_map/ppermute | solution.py:42
  100.1 8.5 %collective-permute-start.20 = (bf16[4,128,128]{2,1,0:T(8,128)(2,1)S(1)}, bf16[4,128,128]{2,1,0:T(8,128)(2,1)S(1)}, u32[]{:S(2)}, u32[]{:S(2)}) collective-permute-start(bf16[4,128,128]{2,1,0:T(8,128)(2,1)S(1)} %shard_map.67.refs_10_), channel_id=1, source_target_pairs={{0,16},{16,0},{1,17},{17,1},{2,18},{18,2},{3,19},{19,3},{4,20},{20... | collective-permute-start | bytes 393224 | tf_op jit(solution)/shard_map/ppermute | solution.py:42
  101.1 1.0 copy-start.25
  102.7 5.9 %collective-permute-start.17 = (f32[3,64,128]{2,1,0:T(8,128)S(1)}, f32[3,64,128]{2,1,0:T(8,128)S(1)}, u32[]{:S(2)}, u32[]{:S(2)}) collective-permute-start(f32[3,64,128]{2,1,0:T(8,128)S(1)} %get-tuple-element.62), channel_id=1, source_target_pairs={{0,1},{1,2},{2,3},{3,0},{4,5},{5,6},{6,7},{7,4},{8,9},{9,10},{10,1... | collective-permute-start | bytes 294920 | tf_op jit(solution)/shard_map/ppermute | solution.py:197
  104.0 7.3 %collective-permute-start.18 = (f32[3,64,128]{2,1,0:T(8,128)S(1)}, f32[3,64,128]{2,1,0:T(8,128)S(1)}, u32[]{:S(2)}, u32[]{:S(2)}) collective-permute-start(f32[3,64,128]{2,1,0:T(8,128)S(1)} %get-tuple-element.63), channel_id=1, source_target_pairs={{0,2},{1,3},{2,0},{3,1},{4,6},{5,7},{6,4},{7,5},{8,10},{9,11},{10,... | collective-permute-start | bytes 294920 | tf_op jit(solution)/shard_map/ppermute | solution.py:197
  106.7 4.7 %collective-permute-start.19 = (f32[3,64,128]{2,1,0:T(8,128)S(1)}, f32[3,64,128]{2,1,0:T(8,128)S(1)}, u32[]{:S(2)}, u32[]{:S(2)}) collective-permute-start(f32[3,64,128]{2,1,0:T(8,128)S(1)} %get-tuple-element.64), channel_id=1, source_target_pairs={{0,3},{1,0},{2,1},{3,2},{4,7},{5,4},{6,5},{7,6},{8,11},{9,8},{10,9... | collective-permute-start | bytes 294920 | tf_op jit(solution)/shard_map/ppermute | solution.py:197
  112.0 2.4 %collective-permute-start.21 = (f32[6,64,64]{2,1,0:T(8,128)S(1)}, f32[6,64,64]{2,1,0:T(8,128)S(1)}, u32[]{:S(2)}, u32[]{:S(2)}) collective-permute-start(f32[6,64,64]{2,1,0:T(8,128)S(1)} %get-tuple-element.74), channel_id=1, source_target_pairs={{0,16},{16,0},{1,17},{17,1},{2,18},{18,2},{3,19},{19,3},{4,20},{20... | collective-permute-start | bytes 294920 | tf_op jit(solution)/shard_map/ppermute | solution.py:42
  115.1 6.3 %collective-permute-start.22 = (f32[64,128]{1,0:T(8,128)S(1)}, f32[64,128]{1,0:T(8,128)S(1)}, u32[]{:S(2)}, u32[]{:S(2)}) collective-permute-start(f32[64,128]{1,0:T(8,128)S(1)} %get-tuple-element.75), channel_id=1, source_target_pairs={{0,44},{1,109},{2,174},{3,239},{32,0},{33,65},{34,130},{35,195},{4... | collective-permute-start | bytes 98312 | tf_op jit(solution)/shard_map/ppermute | solution.py:220
  117.1 6.9 %collective-permute-start.23 = (f32[64,128]{1,0:T(8,128)S(1)}, f32[64,128]{1,0:T(8,128)S(1)}, u32[]{:S(2)}, u32[]{:S(2)}) collective-permute-start(f32[64,128]{1,0:T(8,128)S(1)} %get-tuple-element.76), channel_id=1, source_target_pairs={{0,12},{1,77},{2,142},{3,207},{32,44},{33,109},{34,174},{35,239},{... | collective-permute-start | bytes 98312 | tf_op jit(solution)/shard_map/ppermute | solution.py:220
  117.1 6.9 %collective-permute-start.24 = (f32[64,128]{1,0:T(8,128)S(1)}, f32[64,128]{1,0:T(8,128)S(1)}, u32[]{:S(2)}, u32[]{:S(2)}) collective-permute-start(f32[64,128]{1,0:T(8,128)S(1)} %get-tuple-element.77), channel_id=1, source_target_pairs={{0,40},{1,105},{2,170},{3,235},{32,12},{33,77},{34,142},{35,207},{... | collective-permute-start | bytes 98312 | tf_op jit(solution)/shard_map/ppermute | solution.py:220
  120.0 4.0 %collective-permute-start.25 = (f32[64,128]{1,0:T(8,128)S(1)}, f32[64,128]{1,0:T(8,128)S(1)}, u32[]{:S(2)}, u32[]{:S(2)}) collective-permute-start(f32[64,128]{1,0:T(8,128)S(1)} %get-tuple-element.78), channel_id=1, source_target_pairs={{0,32},{1,97},{2,162},{3,227},{32,4},{33,69},{34,134},{35,199},{4,... | collective-permute-start | bytes 98312 | tf_op jit(solution)/shard_map/ppermute | solution.py:220
  121.4 5.1 %collective-permute-start.26 = (f32[64,128]{1,0:T(8,128)S(1)}, f32[64,128]{1,0:T(8,128)S(1)}, u32[]{:S(2)}, u32[]{:S(2)}) collective-permute-start(f32[64,128]{1,0:T(8,128)S(1)} %get-tuple-element.79), channel_id=1, source_target_pairs={{0,4},{1,69},{2,134},{3,199},{32,36},{33,101},{34,166},{35,231},{4... | collective-permute-start | bytes 98312 | tf_op jit(solution)/shard_map/ppermute | solution.py:220
  121.4 6.0 %collective-permute-start.27 = (f32[64,128]{1,0:T(8,128)S(1)}, f32[64,128]{1,0:T(8,128)S(1)}, u32[]{:S(2)}, u32[]{:S(2)}) collective-permute-start(f32[64,128]{1,0:T(8,128)S(1)} %get-tuple-element.80), channel_id=1, source_target_pairs={{0,36},{1,101},{2,166},{3,231},{32,8},{33,73},{34,138},{35,203},{4... | collective-permute-start | bytes 98312 | tf_op jit(solution)/shard_map/ppermute | solution.py:220
  128.1 0.7 collective-permute-start.28
  157.1 16.6 %all-to-all-start.2 = ((f32[32,1,256]{2,1,0:T(1,128)}), f32[32,1,256]{2,1,0:T(1,128)S(1)}, u32[]{:S(2)}, u32[]{:S(2)}) async-start(f32[32,1,256]{2,1,0:T(1,128)} %broadcast_in_dim.4), calls=%async_computation.2 | async-start | bytes 65536 | tf_op jit(solution)/shard_map/all_to_all | solution.py:46

commit v6 on v5

--- a/solution.py
+++ b/solution.py
@@ -155,12 +155,16 @@
     )(place, *args)
 
 
-def add_body(place, a, b, out):
-    out[...] = a[...] + b[...]
-
-
-def add(place, a, b):
-    return call(add_body, jax.ShapeDtypeStruct(a.shape, a.dtype), (place, a, b))
+def near_body(place, a, b, near, zero):
+    points = zero.shape[2]
+    zero[...] = a[:, :, :points] + b[:, :, :points]
+    near[...] = a[:, :, points:] + b[:, :, points:]
+
+
+def rest_body(place, zero, a, b, out):
+    points = zero.shape[2]
+    out[:, :, :points] = zero[...]
+    out[:, :, points:] = a[...] + b[...]
 
 
 def call_last(body, out, args, blocks):
@@ -193,22 +197,6 @@
     return call_last(orbitals_body, out, (place,), blocks)
 
 
-def shift_y(v, d):
-    return lax.ppermute(v, "y", [(i, (i + d) % YN) for i in range(YN)])
-
-
-def add_ring_body(place, a, b, *outs):
-    for k, out in enumerate(outs):
-        i = (place[1] + k) % YN
-        out[...] = a[i] + b[i]
-
-
-def over_y_ring(place, a, b):
-    out = jax.ShapeDtypeStruct(a.shape[1:], a.dtype)
-    terms = call(add_ring_body, (out,) * YN, (place, a, b))
-    return tuple(shift_y(v, k) if k else v for k, v in enumerate(terms))
-
-
 def shift_pair(v, d):
     pairs = []
     for x in range(XN):
@@ -225,20 +213,18 @@
     return t[0] / SCALES[0], bas * bas * (t[1] / SCALES[1])
 
 
-def turn_body(place, s, zero, own_g, own_r, *outs):
+def turn_body(place, s, own_g, own_r, *outs):
     core = place[0]
     t = s[0] + s[1] + s[2] + s[3]
     g, r = geminal_and_rest(t)
     points = g.shape[1] // 2
-    steps = g.shape[0] // points - 1
-    zero[0] = g[:points]
-    zero[1] = r[:points]
-    own_g[...] = g[points:]
-    own_r[...] = r[points:]
+    steps = g.shape[0] // points
+    own_g[...] = g
+    own_r[...] = r
     mine, give = outs
     for kind, v in enumerate((g, r)):
         for i in range(steps):
-            turned = v[(i + 1) * points : (i + 2) * points].T
+            turned = v[i * points : (i + 1) * points].T
             lo, hi = turned[:points], turned[points:]
             mine[kind * steps + i] = jnp.where(core == 0, lo, hi)
             give[kind * steps + i] = jnp.where(core == 0, hi, lo)
@@ -247,12 +233,12 @@
 def turn(place, s):
     rows, lanes = s.shape[2:]
     points = lanes // 2
-    steps = rows // points - 1
+    steps = rows // points
 
     def f32(*shape):
         return jax.ShapeDtypeStruct(shape, jnp.float32)
 
-    outs = (f32(2, points, lanes),) + (f32(rows - points, lanes),) * 2 + (f32(2 * steps, points, points),) * 2
+    outs = (f32(rows, lanes),) * 2 + (f32(2 * steps, points, points),) * 2
     return call(turn_body, outs, (place, s))
 
 
@@ -268,19 +254,19 @@
     return call(join_body, (jax.ShapeDtypeStruct((points, 2 * points), jnp.float32),) * n, (place, mine, got))
 
 
-def last_body(steps, place, zero, own_g, own_r, *refs):
-    far, others = refs[:YN], refs[YN : YN + 2 * steps]
-    own, other, cols, out = refs[YN + 2 * steps :]
+def last_body(steps, place, s, own_g, own_r, *refs):
+    others = refs[: 2 * steps]
+    own, other, cols, out = refs[2 * steps :]
     core, y, x = place[0], place[1], place[2]
-    points = zero.shape[1]
+    points = own.shape[1] // 2
     sub = points // YN
     e = lax.rem(y + 2 * lax.rem(x, 2), XN)
-    k0 = zero[0] * zero[1]
+    g, r = geminal_and_rest(s[0] + s[1] + s[2] + s[3])
+    k0 = g[:points] * r[:points]
     q = lax.broadcasted_iota(jnp.int32, k0.shape, 0)
     p = lax.broadcasted_iota(jnp.int32, k0.shape, 1) - core * points
     k0 = jnp.where((e == 0) & (p == q), jnp.float32(0.0), k0)
-    g4, r4 = geminal_and_rest(far[0][...] + far[1][...] + far[2][...] + far[3][...])
-    kerns = [k0, g4 * r4]
+    kerns = [k0, g[points:] * r[points:]]
     for i in range(steps):
         at = slice(i * points, (i + 1) * points)
         kerns.append(own_g[at] * others[steps + i][...])
@@ -297,9 +283,12 @@
         w_row.append(jnp.concatenate([v[:points], v[points:]], axis=1))
     w_row = squared(jnp.concatenate(w_row)).astype(jnp.float32)
     total = jnp.sum(w_row * part, axis=0, keepdims=True) / math.sqrt(NGRID)
+    to = lax.rem(y - x + XN, XN)
+    out[:, :sub] = jnp.zeros_like(out[:, :sub])
+    for i in range(out.shape[0]):
+        out[i, sub:] = jnp.broadcast_to(total, (out.shape[1] - sub, total.shape[1]))
     for i in range(2 * YN):
-        out[i, :sub] = part[i * sub : (i + 1) * sub]
-        out[i, sub:] = jnp.broadcast_to(total, (out.shape[1] - sub, total.shape[1]))
+        out[to * 2 * YN + i, :sub] = part[i * sub : (i + 1) * sub]
 
 
 def shards(colloc, coulomb, geminal, occupied):
@@ -332,34 +321,37 @@
 
     g4, r4 = shift_z(g3, 1), shift_z(r3, -1)
     keep, send = tiles(cuts, place, rows, ((gem, rest), (g1, r1), (g2, r2), (g3, r3)))
-    t = add(place, keep, swap_core(send))
+    y, n, _, lanes = keep.shape
+
+    def terms(steps):
+        return jax.ShapeDtypeStruct((y, n, steps * points, lanes), jnp.float32)
+
+    near, zero = call(near_body, (terms(3), terms(1)), (place, keep, swap_core(send)))
     own = orbitals(place, tuple(b[0] for b in rows))
     other = swap_core(own)
-    s = over_y(t)
+    s = over_y(near)
 
     keep, send = tiles(cuts, place, rows, ((g4, r4),), fetch=True)
-    far = over_y_ring(place, keep, swap_core(send))
+    rest_terms = call(rest_body, terms(2), (place, zero, keep, swap_core(send)))
 
     orbs = orbitals(place, (gem, g4, g1, r1, g2, r2, g3, r3))
-    s, far, orbs, own, other = tie(s, far, orbs, own, other)
-
-    zero, own_g, own_r, mine, give = turn(place, s)
+    s, rest_terms, orbs, own, other = tie(s, rest_terms, orbs, own, other)
+    rest = over_y(rest_terms)
+
+    own_g, own_r, mine, give = turn(place, s)
     joined = join(place, mine, swap_core(give))
     steps = len(joined) // 2
     others = [shift_pair(joined[i], -(i + 1)) for i in range(steps)]
     others += [shift_pair(joined[steps + i], i + 1) for i in range(steps)]
     sent = call(
         functools.partial(last_body, steps),
-        jax.ShapeDtypeStruct((2 * YN, sub + 8, 2 * LANES), jnp.float32),
-        (place, zero, own_g, own_r) + far + tuple(others) + (own, other, orbs),
+        jax.ShapeDtypeStruct((2 * XN * YN, sub + 8, 2 * LANES), jnp.float32),
+        (place, rest, own_g, own_r) + tuple(others) + (own, other, orbs),
     )
-    sent = lax.ppermute(
-        sent, ("x", "y"), [(x * YN + y, (y - x) % XN * YN + y) for x in range(XN) for y in range(YN)]
-    )
-    got = lax.all_to_all(sent, ("c", "y"), 0, 0, tiled=True)
+    got = lax.all_to_all(sent, ("x", "c", "y"), 0, 0, tiled=True)
     pair_field = got[:, :sub].sum(0)
     energy = got[:, sub].sum(0)
-    energy = spread(energy[None], ("x", "l", "h"), XN * ZN).sum((0, 1))
+    energy = spread(energy[None], ("l", "h"), ZN).sum((0, 1))
     return pair_field, energy
 
 

time: 175 us -> 168 us (0.960)
  starting transfers between devices: 56.7 us -> 50.6 us
  waiting for transfers between devices: 64.1 us -> 59.6 us
  blocking collectives: 27.6 us -> 30 us
    ppermute x6, waiting for transfers between devices: 22.7 us -> 36.4 us  [shift_x(): return lax.ppermute(v, 'x', [(i, (i + d) % XN) for i in range(XN)])]
    ppermute x8, waiting for transfers between devices: 23.9 us -> 11.4 us  [shift_z(): lax.ppermute(v, ('l', 'h'), [(z_slot(z), z_slot((z + d) % ZN)) for z in r...]
    ppermute x4 -> x0, starting transfers between devices: 5.74 us -> none  [the longest x3 5.06 us: shift_y(): return lax.ppermute(v, 'y', [(i, (i + d) % YN) for i in range(YN)])]
    all_to_all x1 -> x2, starting transfers between devices: 4.18 us -> 8.36 us  [over_y(): return lax.all_to_all(t, 'y', 0, 0, tiled=True)]
    ppermute x6, starting transfers between devices: 8.93 us -> 5.28 us  [shift_x(): return lax.ppermute(v, 'x', [(i, (i + d) % XN) for i in range(XN)])]
    ppermute x4 -> x0, waiting for transfers between devices: 2.73 us -> none  [the longest x3 2.73 us: shift_y(): return lax.ppermute(v, 'y', [(i, (i + d) % YN) for i in range(YN)])]
    ppermute x8, starting transfers between devices: 11 us -> 13.8 us  [shift_z(): lax.ppermute(v, ('l', 'h'), [(z_slot(z), z_slot((z + d) % ZN)) for z in r...]
    all_to_all x1, blocking collectives: 27.6 us -> 30 us  [shards(): got = lax.all_to_all(sent, ('x', 'c', 'y'), 0, 0, tiled=True)]
  transfers between devices with their start and end apart: 31 -> 28, of which waited for: 16 -> 15; matrix products, arithmetic and copies ran while one was open for 0% -> 0% of each run, Pallas kernels for 6% -> 7%
where the time goes in v6:
time: 168 us; the launch traced here: 167 us
  waiting for transfers between devices  59.6 us (35%)
  starting transfers between devices  50.6 us (30%)
  blocking collectives  30 us (18%)
  Pallas kernels  19 us (11%)
  local copies, waits for them, and re-layouts  5.85 us (3%)
    ppermute x6, waiting for transfers between devices, shift_x(): return lax.ppermute(v, 'x', [(i, (i + d) % XN) for i in range(XN)])  36.4 us
    all_to_all x1, blocking collectives, shards(): got = lax.all_to_all(sent, ('x', 'c', 'y'), 0, 0, tiled=True)  30 us
    ppermute x8, starting transfers between devices, shift_z(): lax.ppermute(v, ('l', 'h'), [(z_slot(z), z_slot((z + d) % ZN)) for z in r...  13.8 us
    pallas_call x9, Pallas kernels, call(): pl.pallas_call(body, out_shape=out, in_specs=[SMEM] + [VMEM] * (len(args)...  12 us
    ppermute x8, waiting for transfers between devices, shift_z(): lax.ppermute(v, ('l', 'h'), [(z_slot(z), z_slot((z + d) % ZN)) for z in r...  11.4 us
    ppermute x6, starting transfers between devices, shift_pair(): return lax.ppermute(v, ('x', 'l', 'h', 'y'), pairs)  8.85 us
    ppermute x5, starting transfers between devices, swap_core(): return lax.ppermute(v, 'c', [(0, 1), (1, 0)])  8.48 us
    all_to_all x2, starting transfers between devices, over_y(): return lax.all_to_all(t, 'y', 0, 0, tiled=True)  8.36 us
  transfers between devices with their start and end apart: 28, of which 15 were waited for; matrix products, arithmetic and copies ran while one was open for 0% of the time, Pallas kernels for 7%

profile of v6, /device:TPU:1, one launch (start us, length us, event | category | flops | bytes accessed | tf_op | source)
XLA Modules:
  0.0 167.3 jit_solution(15419388096560418335)
XLA Ops:
  0.6 0.1 pad_add_fusion.place
  0.7 1.1 copy-done.22
  1.8 1.0 copy-done.23
  2.8 0.9 copy-done.24
  3.8 0.7 shard_map.60
  4.5 3.3 %collective-permute-start = (bf16[40,64,128]{2,1,0:T(8,128)(2,1)S(1)}, bf16[40,64,128]{2,1,0:T(8,128)(2,1)S(1)}, u32[]{:S(2)}, u32[]{:S(2)}) collective-permute-start(bf16[40,64,128]{2,1,0:T(8,128)(2,1)S(1)} %shard_map.60), channel_id=1, source_target_pairs={{0,16},{16,0},{1,17},{17,1},{2,18},{18,2},{3,19},{19,3},{4,20},{20... | collective-permute-start | bytes 1966088 | tf_op jit(solution)/shard_map/ppermute | solution.py:42
  7.8 0.7 shard_map.59.kept
  8.5 1.0 collective-permute-done.got
  9.5 0.6 shard_map.61
  10.2 0.8 collective-permute-start.4
  11.0 5.6 %collective-permute-start.2 = (bf16[21,128,128]{2,1,0:T(8,128)(2,1)S(1)}, bf16[21,128,128]{2,1,0:T(8,128)(2,1)S(1)}, u32[]{:S(2)}, u32[]{:S(2)}) collective-permute-start(bf16[21,128,128]{2,1,0:T(8,128)(2,1)S(1)} %get-tuple-element.38.refs_4_.refs_12_), channel_id=1, source_target_pairs={{0,44},{32,0},{4,32},{36,4},{8,36},{40,8},{12,40},{44,12},{1,45},{... | collective-permute-start | bytes 2064392 | tf_op jit(solution)/shard_map/ppermute | solution.py:34
  16.6 0.2 collective-permute-start.7
  16.8 10.1 %collective-permute-done.4.refs_5_ = bf16[21,128,128]{2,1,0:T(8,128)(2,1)S(1)} collective-permute-done((bf16[21,128,128]{2,1,0:T(8,128)(2,1)S(1)}, bf16[21,128,128]{2,1,0:T(8,128)(2,1)S(1)}, u32[]{:S(2)}, u32[]{:S(2)}) %collective-permute-start.4) | collective-permute-done | bytes 688160 | tf_op jit(solution)/shard_map/ppermute | solution.py:38
  26.9 2.0 %collective-permute-start.8 = (bf16[21,128,128]{2,1,0:T(8,128)(2,1)S(1)}, bf16[21,128,128]{2,1,0:T(8,128)(2,1)S(1)}, u32[]{:S(2)}, u32[]{:S(2)}) collective-permute-start(bf16[21,128,128]{2,1,0:T(8,128)(2,1)S(1)} %get-tuple-element.37.refs_0_.refs_8_), channel_id=1, source_target_pairs={{0,192},{64,0},{128,64},{192,128},{1,193},{65,1},{129,65},{193,129... | collective-permute-start | bytes 2064392 | tf_op jit(solution)/shard_map/ppermute | solution.py:38
  28.9 1.8 %collective-permute-done.2.refs_13_.refs_3_ = bf16[21,128,128]{2,1,0:T(8,128)(2,1)S(1)} collective-permute-done((bf16[21,128,128]{2,1,0:T(8,128)(2,1)S(1)}, bf16[21,128,128]{2,1,0:T(8,128)(2,1)S(1)}, u32[]{:S(2)}, u32[]{:S(2)}) %collective-permute-start.2) | collective-permute-done | bytes 688160 | tf_op jit(solution)/shard_map/ppermute | solution.py:34
  30.7 3.1 %collective-permute-done.3.refs_3_ = bf16[21,128,128]{2,1,0:T(8,128)(2,1)S(1)} collective-permute-done((bf16[21,128,128]{2,1,0:T(8,128)(2,1)S(1)}, bf16[21,128,128]{2,1,0:T(8,128)(2,1)S(1)}, u32[]{:S(2)}, u32[]{:S(2)}) %collective-permute-start.3) | collective-permute-done | bytes 688160 | tf_op jit(solution)/shard_map/ppermute | solution.py:38
  33.8 0.1 collective-permute-start.5
  33.9 2.7 %collective-permute-start.6 = (bf16[21,128,128]{2,1,0:T(8,128)(2,1)S(1)}, bf16[21,128,128]{2,1,0:T(8,128)(2,1)S(1)}, u32[]{:S(2)}, u32[]{:S(2)}) collective-permute-start(bf16[21,128,128]{2,1,0:T(8,128)(2,1)S(1)} %collective-permute-done.2.refs_13_.refs_3_), channel_id=1, source_target_pairs={{0,44},{32,0},{4,32},{36,4},{8,36},{40,8},{12,40},{44,12},{1,45},{... | collective-permute-start | bytes 2064392 | tf_op jit(solution)/shard_map/ppermute | solution.py:34
  36.6 2.3 %collective-permute-start.12 = (bf16[21,128,128]{2,1,0:T(8,128)(2,1)S(1)}, bf16[21,128,128]{2,1,0:T(8,128)(2,1)S(1)}, u32[]{:S(2)}, u32[]{:S(2)}) collective-permute-start(bf16[21,128,128]{2,1,0:T(8,128)(2,1)S(1)} %collective-permute-done.4.refs_5_), channel_id=1, source_target_pairs={{0,192},{64,0},{128,64},{192,128},{1,193},{65,1},{129,65},{193,129... | collective-permute-start | bytes 2064392 | tf_op jit(solution)/shard_map/ppermute | solution.py:38
  38.9 9.7 %collective-permute-done.7.refs_7_ = bf16[21,128,128]{2,1,0:T(8,128)(2,1)S(1)} collective-permute-done((bf16[21,128,128]{2,1,0:T(8,128)(2,1)S(1)}, bf16[21,128,128]{2,1,0:T(8,128)(2,1)S(1)}, u32[]{:S(2)}, u32[]{:S(2)}) %collective-permute-start.7) | collective-permute-done | bytes 688160 | tf_op jit(solution)/shard_map/ppermute | solution.py:38
  48.6 0.2 collective-permute-done.5.refs_10_.refs_4_
  48.7 0.1 collective-permute-start.9
  48.8 2.7 %collective-permute-start.10 = (bf16[21,128,128]{2,1,0:T(8,128)(2,1)S(1)}, bf16[21,128,128]{2,1,0:T(8,128)(2,1)}, u32[]{:S(2)}, u32[]{:S(2)}) collective-permute-start(bf16[21,128,128]{2,1,0:T(8,128)(2,1)S(1)} %collective-permute-done.6.refs_14_.refs_5_), channel_id=1, source_target_pairs={{0,44},{32,0},{4,32},{36,4},{8,36},{40,8},{12,40},{44,12},{1,45},{... | collective-permute-start | bytes 2064392 | tf_op jit(solution)/shard_map/ppermute | solution.py:34
  51.5 6.0 %collective-permute-done.12.refs_6_ = bf16[21,128,128]{2,1,0:T(8,128)(2,1)S(1)} collective-permute-done((bf16[21,128,128]{2,1,0:T(8,128)(2,1)S(1)}, bf16[21,128,128]{2,1,0:T(8,128)(2,1)S(1)}, u32[]{:S(2)}, u32[]{:S(2)}) %collective-permute-start.12) | collective-permute-done | bytes 688160 | tf_op jit(solution)/shard_map/ppermute | solution.py:38
  57.5 7.4 %collective-permute-done.11.refs_2_ = bf16[21,128,128]{2,1,0:T(8,128)(2,1)S(1)} collective-permute-done((bf16[21,128,128]{2,1,0:T(8,128)(2,1)S(1)}, bf16[21,128,128]{2,1,0:T(8,128)(2,1)S(1)}, u32[]{:S(2)}, u32[]{:S(2)}) %collective-permute-start.11) | collective-permute-done | bytes 688160 | tf_op jit(solution)/shard_map/ppermute | solution.py:38
  65.0 4.5 %shard_map.62 = (f32[4,3,256,128]{3,2,1,0:T(8,128)S(1)}, f32[4,3,256,128]{3,2,1,0:T(8,128)S(1)}) custom-call(s32[3]{0:T(128)S(1)} %pad_add_fusion.place, bf16[21,128,128]{2,1,0:T(8,128)(2,1)S(1)} %get-tuple-element.37.refs_0_.refs_8_, bf16[21,128,128]{2,1,0:T(8,128)(2,1)S(1)} %collective-permute-done.8.refs_1_, ...), custom_call_target="tpu_custom_call" | custom-call | tf_op jit(solution)/shard_map/pallas_call | solution.py:60
  69.6 2.8 %collective-permute-start.13 = (f32[4,3,256,128]{3,2,1,0:T(8,128)S(1)}, f32[4,3,256,128]{3,2,1,0:T(8,128)S(1)}, u32[]{:S(2)}, u32[]{:S(2)}) collective-permute-start(f32[4,3,256,128]{3,2,1,0:T(8,128)S(1)} %get-tuple-element.52), channel_id=1, source_target_pairs={{0,16},{16,0},{1,17},{17,1},{2,18},{18,2},{3,19},{19,3},{4,20},{20... | collective-permute-start | bytes 4718600 | tf_op jit(solution)/shard_map/ppermute | solution.py:42
  72.4 0.7 collective-permute-start.14
  73.2 1.9 %collective-permute-start.15 = (bf16[21,128,128]{2,1,0:T(8,128)(2,1)}, bf16[21,128,128]{2,1,0:T(8,128)(2,1)}, u32[]{:S(2)}, u32[]{:S(2)}) collective-permute-start(bf16[21,128,128]{2,1,0:T(8,128)(2,1)} %collective-permute-done.10.refs_15_.refs_7_), channel_id=1, source_target_pairs={{0,44},{32,0},{4,32},{36,4},{8,36},{40,8},{12,40},{44,12},{1,45},{... | collective-permute-start | bytes 2064392 | tf_op jit(solution)/shard_map/ppermute | solution.py:34
  75.1 0.3 collective-permute-done.13.b
  75.5 1.8 %shard_map.63 = (f32[4,3,192,128]{3,2,1,0:T(8,128)}, f32[4,3,64,128]{3,2,1,0:T(8,128)S(1)}) custom-call(s32[3]{0:T(128)S(1)} %pad_add_fusion.place, f32[4,3,256,128]{3,2,1,0:T(8,128)S(1)} %get-tuple-element.51.a, f32[4,3,256,128]{3,2,1,0:T(8,128)S(1)} %collective-permute-done.13.b), custom_call_target="tpu_custom_call" | custom-call | tf_op jit(solution)/shard_map/pallas_call | solution.py:60
  77.2 4.2 %all-to-all-start = ((f32[4,3,192,128]{3,2,1,0:T(8,128)}), f32[4,3,192,128]{3,2,1,0:T(8,128)S(1)}, u32[]{:S(2)}, u32[]{:S(2)}) async-start(f32[4,3,192,128]{3,2,1,0:T(8,128)} %get-tuple-element.53), calls=%async_computation | async-start | bytes 2359296 | tf_op jit(solution)/shard_map/all_to_all | solution.py:50
  81.4 0.0 copy-start.27
  81.4 9.4 %collective-permute-done.14.refs_8_.refs_1_ = bf16[21,128,128]{2,1,0:T(8,128)(2,1)S(1)} collective-permute-done((bf16[21,128,128]{2,1,0:T(8,128)(2,1)}, bf16[21,128,128]{2,1,0:T(8,128)(2,1)S(1)}, u32[]{:S(2)}, u32[]{:S(2)}) %collective-permute-start.14) | collective-permute-done | bytes 688160 | tf_op jit(solution)/shard_map/ppermute | solution.py:34
  90.8 0.8 copy-done.17
  91.7 5.6 %shard_map.64 = (f32[4,3,64,128]{3,2,1,0:T(8,128)}, f32[4,3,64,128]{3,2,1,0:T(8,128)}) custom-call(s32[3]{0:T(128)} %copy-done.26, bf16[21,128,128]{2,1,0:T(8,128)(2,1)} %copy-done, bf16[21,128,128]{2,1,0:T(8,128)(2,1)} %copy-done.4, bf16[21,128,128]{2,1,0:T(8,128)(2,1)} %copy-done.6, bf16[21,128,128]{2,1,0:T(8,128)(2,1)} %copy-done.2, ...), custom_call_target="tpu_custom_call" | custom-call | tf_op jit(solution)/shard_map/pallas_call | solution.py:147
  97.3 0.9 collective-permute-start.16
  98.3 0.6 shard_map.67.refs_6_
  98.9 0.1 collective-permute-start.17
  99.0 0.0 copy-done.16
  99.0 1.1 copy-done.18
  100.1 0.9 shard_map.66.refs_8_
  101.0 0.2 copy-done.25
  101.2 1.5 shard_map.65
  102.7 4.2 %all-to-all-start.1 = ((f32[4,3,128,128]{3,2,1,0:T(8,128)}), f32[4,3,128,128]{3,2,1,0:T(8,128)S(1)}, u32[]{:S(2)}, u32[]{:S(2)}) async-start(f32[4,3,128,128]{3,2,1,0:T(8,128)} %shard_map.65), calls=%async_computation.1 | async-start | bytes 1572864 | tf_op jit(solution)/shard_map/all_to_all | solution.py:50
  106.9 0.7 shard_map.68
  107.6 1.2 collective-permute-start.18
  108.8 1.1 collective-permute-done.18.got
  109.9 0.7 shard_map.69
  110.5 2.0 %collective-permute-start.19 = (f32[64,128]{1,0:T(8,128)S(1)}, f32[64,128]{1,0:T(8,128)S(1)}, u32[]{:S(2)}, u32[]{:S(2)}) collective-permute-start(f32[64,128]{1,0:T(8,128)S(1)} %get-tuple-element.63), channel_id=1, source_target_pairs={{0,44},{1,109},{2,174},{3,239},{32,0},{33,65},{34,130},{35,195},{4... | collective-permute-start | bytes 98312 | tf_op jit(solution)/shard_map/ppermute | solution.py:208
  112.6 0.1 collective-permute-start.20
  112.6 3.1 %collective-permute-start.21 = (f32[64,128]{1,0:T(8,128)S(1)}, f32[64,128]{1,0:T(8,128)S(1)}, u32[]{:S(2)}, u32[]{:S(2)}) collective-permute-start(f32[64,128]{1,0:T(8,128)S(1)} %get-tuple-element.65), channel_id=1, source_target_pairs={{0,40},{1,105},{2,170},{3,235},{32,12},{33,77},{34,142},{35,207},{... | collective-permute-start | bytes 98312 | tf_op jit(solution)/shard_map/ppermute | solution.py:208
  115.7 1.2 collective-permute-start.22
  117.0 2.5 %collective-permute-start.24 = (f32[64,128]{1,0:T(8,128)S(1)}, f32[64,128]{1,0:T(8,128)S(1)}, u32[]{:S(2)}, u32[]{:S(2)}) collective-permute-start(f32[64,128]{1,0:T(8,128)S(1)} %get-tuple-element.68), channel_id=1, source_target_pairs={{0,36},{1,101},{2,166},{3,231},{32,8},{33,73},{34,138},{35,203},{4... | collective-permute-start | bytes 98312 | tf_op jit(solution)/shard_map/ppermute | solution.py:208
  119.4 0.3 collective-permute-done.22.refs_3_
  119.7 2.4 %collective-permute-done.23.refs_4_ = f32[64,128]{1,0:T(8,128)S(1)} collective-permute-done((f32[64,128]{1,0:T(8,128)S(1)}, f32[64,128]{1,0:T(8,128)S(1)}, u32[]{:S(2)}, u32[]{:S(2)}) %collective-permute-start.23) | collective-permute-done | bytes 32800 | tf_op jit(solution)/shard_map/ppermute | solution.py:208
  122.2 0.8 collective-permute-done.24.refs_5_
  122.9 0.8 shard_map.70
  123.7 30.0 %all_to_all.20 = f32[32,24,256]{2,1,0:T(8,128)S(1)} all-to-all(f32[32,24,256]{2,1,0:T(8,128)S(1)} %shard_map.70), channel_id=1, replica_groups=mesh['x'=4,'l'=2,'c'=2,'h'=4,'y'=4] {'x','c','y'}, dimensions={0} | all-to-all | bytes 1572864 | tf_op jit(solution)/shard_map/all_to_all | solution.py:351
  153.7 0.6 broadcast_in_dim.4
  154.4 5.9 %all-to-all-start.3 = ((f32[8,1,256]{2,1,0:T(1,128)}), f32[8,1,256]{2,1,0:T(1,128)S(1)}, u32[]{:S(2)}, u32[]{:S(2)}) async-start(f32[8,1,256]{2,1,0:T(1,128)} %broadcast_in_dim.4), calls=%async_computation.3 | async-start | bytes 16384 | tf_op jit(solution)/shard_map/all_to_all | solution.py:46
  160.2 0.6 slice_reduce_fusion
  160.9 5.9 %all-to-all-done.3 = f32[8,1,256]{2,1,0:T(1,128)S(1)} async-done(((f32[8,1,256]{2,1,0:T(1,128)}), f32[8,1,256]{2,1,0:T(1,128)S(1)}, u32[]{:S(2)}, u32[]{:S(2)}) %all-to-all-start.3) | async-done | bytes 8224 | tf_op jit(solution)/shard_map/all_to_all | solution.py:46
  166.7 0.6 reduce_sum.29
  (68 shorter events, 0.2 us)
Async XLA Ops:
  0.7 1.1 copy-start.22
  1.8 1.0 copy-start.23
  2.8 0.9 copy-start.24
  3.7 71.7 %copy-start.26 = (s32[3]{0:T(128)}, s32[3]{0:T(128)S(1)}, u32[]{:S(2)}) copy-start(s32[3]{0:T(128)S(1)} %pad_add_fusion.place) | copy-start | bytes 40
  3.8 5.8 %copy-start.28 = (bf16[64,256]{1,0:T(8,128)(2,1)S(1)}, bf16[64,256]{1,0:T(8,128)(2,1)}, u32[]{:S(2)}) copy-start(bf16[64,256]{1,0:T(8,128)(2,1)} %occ.1) | copy-start | bytes 98308
  4.5 5.1 %collective-permute-start = (bf16[40,64,128]{2,1,0:T(8,128)(2,1)S(1)}, bf16[40,64,128]{2,1,0:T(8,128)(2,1)S(1)}, u32[]{:S(2)}, u32[]{:S(2)}) collective-permute-start(bf16[40,64,128]{2,1,0:T(8,128)(2,1)S(1)} %shard_map.60), channel_id=1, source_target_pairs={{0,16},{16,0},{1,17},{17,1},{2,18},{18,2},{3,19},{19,3},{4,20},{20... | collective-permute-start | bytes 1966088 | tf_op jit(solution)/shard_map/ppermute | solution.py:42
  10.2 59.3 %copy-start = (bf16[21,128,128]{2,1,0:T(8,128)(2,1)}, bf16[21,128,128]{2,1,0:T(8,128)(2,1)S(1)}, u32[]{:S(2)}) copy-start(bf16[21,128,128]{2,1,0:T(8,128)(2,1)S(1)} %get-tuple-element.37.refs_0_.refs_8_) | copy-start | bytes 2064388
  10.2 59.3 %copy-start.8 = (bf16[21,128,128]{2,1,0:T(8,128)(2,1)}, bf16[21,128,128]{2,1,0:T(8,128)(2,1)S(1)}, u32[]{:S(2)}) copy-start(bf16[21,128,128]{2,1,0:T(8,128)(2,1)S(1)} %get-tuple-element.38.refs_4_.refs_12_) | copy-start | bytes 2064388
  10.2 16.7 %collective-permute-start.4 = (bf16[21,128,128]{2,1,0:T(8,128)(2,1)S(1)}, bf16[21,128,128]{2,1,0:T(8,128)(2,1)S(1)}, u32[]{:S(2)}, u32[]{:S(2)}) collective-permute-start(bf16[21,128,128]{2,1,0:T(8,128)(2,1)S(1)} %get-tuple-element.38.refs_4_.refs_12_), channel_id=1, source_target_pairs={{0,192},{64,0},{128,64},{192,128},{1,193},{65,1},{129,65},{193,129... | collective-permute-start | bytes 2064392 | tf_op jit(solution)/shard_map/ppermute | solution.py:38
  11.0 19.7 %collective-permute-start.2 = (bf16[21,128,128]{2,1,0:T(8,128)(2,1)S(1)}, bf16[21,128,128]{2,1,0:T(8,128)(2,1)S(1)}, u32[]{:S(2)}, u32[]{:S(2)}) collective-permute-start(bf16[21,128,128]{2,1,0:T(8,128)(2,1)S(1)} %get-tuple-element.38.refs_4_.refs_12_), channel_id=1, source_target_pairs={{0,44},{32,0},{4,32},{36,4},{8,36},{40,8},{12,40},{44,12},{1,45},{... | collective-permute-start | bytes 2064392 | tf_op jit(solution)/shard_map/ppermute | solution.py:34
  16.6 17.2 %collective-permute-start.3 = (bf16[21,128,128]{2,1,0:T(8,128)(2,1)S(1)}, bf16[21,128,128]{2,1,0:T(8,128)(2,1)S(1)}, u32[]{:S(2)}, u32[]{:S(2)}) collective-permute-start(bf16[21,128,128]{2,1,0:T(8,128)(2,1)S(1)} %get-tuple-element.37.refs_0_.refs_8_), channel_id=1, source_target_pairs={{0,64},{64,128},{128,192},{192,0},{1,65},{65,129},{129,193},{193,1... | collective-permute-start | bytes 2064392 | tf_op jit(solution)/shard_map/ppermute | solution.py:38
  16.6 17.2 %collective-permute-start.1 = (bf16[21,128,128]{2,1,0:T(8,128)(2,1)S(1)}, bf16[21,128,128]{2,1,0:T(8,128)(2,1)S(1)}, u32[]{:S(2)}, u32[]{:S(2)}) collective-permute-start(bf16[21,128,128]{2,1,0:T(8,128)(2,1)S(1)} %get-tuple-element.37.refs_0_.refs_8_), channel_id=1, source_target_pairs={{0,32},{32,4},{4,36},{36,8},{8,40},{40,12},{12,44},{44,0},{1,33},{... | collective-permute-start | bytes 2064392 | tf_op jit(solution)/shard_map/ppermute | solution.py:34
  16.6 32.0 %collective-permute-start.7 = (bf16[21,128,128]{2,1,0:T(8,128)(2,1)S(1)}, bf16[21,128,128]{2,1,0:T(8,128)(2,1)S(1)}, u32[]{:S(2)}, u32[]{:S(2)}) collective-permute-start(bf16[21,128,128]{2,1,0:T(8,128)(2,1)S(1)} %get-tuple-element.38.refs_4_.refs_12_), channel_id=1, source_target_pairs={{0,64},{64,128},{128,192},{192,0},{1,65},{65,129},{129,193},{193,1... | collective-permute-start | bytes 2064392 | tf_op jit(solution)/shard_map/ppermute | solution.py:38
  26.9 42.5 %copy-start.19 = (bf16[21,128,128]{2,1,0:T(8,128)(2,1)}, bf16[21,128,128]{2,1,0:T(8,128)(2,1)S(1)}, u32[]{:S(2)}) copy-start(bf16[21,128,128]{2,1,0:T(8,128)(2,1)S(1)} %collective-permute-done.4.refs_5_) | copy-start | bytes 2064388
  26.9 21.6 %collective-permute-start.8 = (bf16[21,128,128]{2,1,0:T(8,128)(2,1)S(1)}, bf16[21,128,128]{2,1,0:T(8,128)(2,1)S(1)}, u32[]{:S(2)}, u32[]{:S(2)}) collective-permute-start(bf16[21,128,128]{2,1,0:T(8,128)(2,1)S(1)} %get-tuple-element.37.refs_0_.refs_8_), channel_id=1, source_target_pairs={{0,192},{64,0},{128,64},{192,128},{1,193},{65,1},{129,65},{193,129... | collective-permute-start | bytes 2064392 | tf_op jit(solution)/shard_map/ppermute | solution.py:38
  30.7 38.8 %copy-start.9 = (bf16[21,128,128]{2,1,0:T(8,128)(2,1)}, bf16[21,128,128]{2,1,0:T(8,128)(2,1)S(1)}, u32[]{:S(2)}) copy-start(bf16[21,128,128]{2,1,0:T(8,128)(2,1)S(1)} %collective-permute-done.2.refs_13_.refs_3_) | copy-start | bytes 2064388
  33.8 35.7 %copy-start.2 = (bf16[21,128,128]{2,1,0:T(8,128)(2,1)}, bf16[21,128,128]{2,1,0:T(8,128)(2,1)S(1)}, u32[]{:S(2)}) copy-start(bf16[21,128,128]{2,1,0:T(8,128)(2,1)S(1)} %collective-permute-done.3.refs_3_) | copy-start | bytes 2064388
  33.8 35.7 %copy-start.11 = (bf16[21,128,128]{2,1,0:T(8,128)(2,1)}, bf16[21,128,128]{2,1,0:T(8,128)(2,1)S(1)}, u32[]{:S(2)}) copy-start(bf16[21,128,128]{2,1,0:T(8,128)(2,1)S(1)} %collective-permute-done.1.refs_9_.refs_2_) | copy-start | bytes 2064388
  33.8 14.9 %collective-permute-start.5 = (bf16[21,128,128]{2,1,0:T(8,128)(2,1)S(1)}, bf16[21,128,128]{2,1,0:T(8,128)(2,1)S(1)}, u32[]{:S(2)}, u32[]{:S(2)}) collective-permute-start(bf16[21,128,128]{2,1,0:T(8,128)(2,1)S(1)} %collective-permute-done.1.refs_9_.refs_2_), channel_id=1, source_target_pairs={{0,32},{32,4},{4,36},{36,8},{8,40},{40,12},{12,44},{44,0},{1,33},{... | collective-permute-start | bytes 2064392 | tf_op jit(solution)/shard_map/ppermute | solution.py:34
  33.9 14.8 %collective-permute-start.6 = (bf16[21,128,128]{2,1,0:T(8,128)(2,1)S(1)}, bf16[21,128,128]{2,1,0:T(8,128)(2,1)S(1)}, u32[]{:S(2)}, u32[]{:S(2)}) collective-permute-start(bf16[21,128,128]{2,1,0:T(8,128)(2,1)S(1)} %collective-permute-done.2.refs_13_.refs_3_), channel_id=1, source_target_pairs={{0,44},{32,0},{4,32},{36,4},{8,36},{40,8},{12,40},{44,12},{1,45},{... | collective-permute-start | bytes 2064392 | tf_op jit(solution)/shard_map/ppermute | solution.py:34
  36.6 20.9 %collective-permute-start.12 = (bf16[21,128,128]{2,1,0:T(8,128)(2,1)S(1)}, bf16[21,128,128]{2,1,0:T(8,128)(2,1)S(1)}, u32[]{:S(2)}, u32[]{:S(2)}) collective-permute-start(bf16[21,128,128]{2,1,0:T(8,128)(2,1)S(1)} %collective-permute-done.4.refs_5_), channel_id=1, source_target_pairs={{0,192},{64,0},{128,64},{192,128},{1,193},{65,1},{129,65},{193,129... | collective-permute-start | bytes 2064392 | tf_op jit(solution)/shard_map/ppermute | solution.py:38
  48.6 21.0 %copy-start.20 = (bf16[21,128,128]{2,1,0:T(8,128)(2,1)}, bf16[21,128,128]{2,1,0:T(8,128)(2,1)S(1)}, u32[]{:S(2)}) copy-start(bf16[21,128,128]{2,1,0:T(8,128)(2,1)S(1)} %collective-permute-done.7.refs_7_) | copy-start | bytes 2064388
  48.6 16.4 %collective-permute-start.11 = (bf16[21,128,128]{2,1,0:T(8,128)(2,1)S(1)}, bf16[21,128,128]{2,1,0:T(8,128)(2,1)S(1)}, u32[]{:S(2)}, u32[]{:S(2)}) collective-permute-start(bf16[21,128,128]{2,1,0:T(8,128)(2,1)S(1)} %collective-permute-done.3.refs_3_), channel_id=1, source_target_pairs={{0,64},{64,128},{128,192},{192,0},{1,65},{65,129},{129,193},{193,1... | collective-permute-start | bytes 2064392 | tf_op jit(solution)/shard_map/ppermute | solution.py:38
  48.6 21.0 %copy-start.4 = (bf16[21,128,128]{2,1,0:T(8,128)(2,1)}, bf16[21,128,128]{2,1,0:T(8,128)(2,1)S(1)}, u32[]{:S(2)}) copy-start(bf16[21,128,128]{2,1,0:T(8,128)(2,1)S(1)} %collective-permute-done.8.refs_1_) | copy-start | bytes 2064388
  48.7 20.8 %copy-start.13 = (bf16[21,128,128]{2,1,0:T(8,128)(2,1)}, bf16[21,128,128]{2,1,0:T(8,128)(2,1)S(1)}, u32[]{:S(2)}) copy-start(bf16[21,128,128]{2,1,0:T(8,128)(2,1)S(1)} %collective-permute-done.5.refs_10_.refs_4_) | copy-start | bytes 2064388
  48.7 20.8 %copy-start.15 = (bf16[21,128,128]{2,1,0:T(8,128)(2,1)}, bf16[21,128,128]{2,1,0:T(8,128)(2,1)S(1)}, u32[]{:S(2)}) copy-start(bf16[21,128,128]{2,1,0:T(8,128)(2,1)S(1)} %collective-permute-done.6.refs_14_.refs_5_) | copy-start | bytes 2064388
  48.7 16.2 %collective-permute-start.9 = (bf16[21,128,128]{2,1,0:T(8,128)(2,1)S(1)}, bf16[21,128,128]{2,1,0:T(8,128)(2,1)}, u32[]{:S(2)}, u32[]{:S(2)}) collective-permute-start(bf16[21,128,128]{2,1,0:T(8,128)(2,1)S(1)} %collective-permute-done.5.refs_10_.refs_4_), channel_id=1, source_target_pairs={{0,32},{32,4},{4,36},{36,8},{8,40},{40,12},{12,44},{44,0},{1,33},{... | collective-permute-start | bytes 2064392 | tf_op jit(solution)/shard_map/ppermute | solution.py:34
  48.8 16.1 %collective-permute-start.10 = (bf16[21,128,128]{2,1,0:T(8,128)(2,1)S(1)}, bf16[21,128,128]{2,1,0:T(8,128)(2,1)}, u32[]{:S(2)}, u32[]{:S(2)}) collective-permute-start(bf16[21,128,128]{2,1,0:T(8,128)(2,1)S(1)} %collective-permute-done.6.refs_14_.refs_5_), channel_id=1, source_target_pairs={{0,44},{32,0},{4,32},{36,4},{8,36},{40,8},{12,40},{44,12},{1,45},{... | collective-permute-start | bytes 2064392 | tf_op jit(solution)/shard_map/ppermute | solution.py:34
  57.5 12.0 %copy-start.21 = (bf16[21,128,128]{2,1,0:T(8,128)(2,1)}, bf16[21,128,128]{2,1,0:T(8,128)(2,1)S(1)}, u32[]{:S(2)}) copy-start(bf16[21,128,128]{2,1,0:T(8,128)(2,1)S(1)} %collective-permute-done.12.refs_6_) | copy-start | bytes 2064388
  64.9 4.6 %copy-start.6 = (bf16[21,128,128]{2,1,0:T(8,128)(2,1)}, bf16[21,128,128]{2,1,0:T(8,128)(2,1)S(1)}, u32[]{:S(2)}) copy-start(bf16[21,128,128]{2,1,0:T(8,128)(2,1)S(1)} %collective-permute-done.11.refs_2_) | copy-start | bytes 2064388
  69.6 5.9 %collective-permute-start.13 = (f32[4,3,256,128]{3,2,1,0:T(8,128)S(1)}, f32[4,3,256,128]{3,2,1,0:T(8,128)S(1)}, u32[]{:S(2)}, u32[]{:S(2)}) collective-permute-start(f32[4,3,256,128]{3,2,1,0:T(8,128)S(1)} %get-tuple-element.52), channel_id=1, source_target_pairs={{0,16},{16,0},{1,17},{17,1},{2,18},{18,2},{3,19},{19,3},{4,20},{20... | collective-permute-start | bytes 4718600 | tf_op jit(solution)/shard_map/ppermute | solution.py:42
  72.4 18.4 %collective-permute-start.14 = (bf16[21,128,128]{2,1,0:T(8,128)(2,1)}, bf16[21,128,128]{2,1,0:T(8,128)(2,1)S(1)}, u32[]{:S(2)}, u32[]{:S(2)}) collective-permute-start(bf16[21,128,128]{2,1,0:T(8,128)(2,1)} %collective-permute-done.9.refs_11_.refs_6_), channel_id=1, source_target_pairs={{0,32},{32,4},{4,36},{36,8},{8,40},{40,12},{12,44},{44,0},{1,33},{... | collective-permute-start | bytes 2064392 | tf_op jit(solution)/shard_map/ppermute | solution.py:34
  73.2 17.7 %collective-permute-start.15 = (bf16[21,128,128]{2,1,0:T(8,128)(2,1)}, bf16[21,128,128]{2,1,0:T(8,128)(2,1)}, u32[]{:S(2)}, u32[]{:S(2)}) collective-permute-start(bf16[21,128,128]{2,1,0:T(8,128)(2,1)} %collective-permute-done.10.refs_15_.refs_7_), channel_id=1, source_target_pairs={{0,44},{32,0},{4,32},{36,4},{8,36},{40,8},{12,40},{44,12},{1,45},{... | collective-permute-start | bytes 2064392 | tf_op jit(solution)/shard_map/ppermute | solution.py:34
  77.2 25.5 %all-to-all-start = ((f32[4,3,192,128]{3,2,1,0:T(8,128)}), f32[4,3,192,128]{3,2,1,0:T(8,128)S(1)}, u32[]{:S(2)}, u32[]{:S(2)}) async-start(f32[4,3,192,128]{3,2,1,0:T(8,128)} %get-tuple-element.53), calls=%async_computation | async-start | bytes 2359296 | tf_op jit(solution)/shard_map/all_to_all | solution.py:50
  81.4 16.9 %copy-start.1 = (bf16[21,128,128]{2,1,0:T(8,128)(2,1)S(1)}, bf16[21,128,128]{2,1,0:T(8,128)(2,1)}, u32[]{:S(2)}) copy-start(bf16[21,128,128]{2,1,0:T(8,128)(2,1)} %copy-done) | copy-start | bytes 2064388
  81.4 16.9 %copy-start.3 = (bf16[21,128,128]{2,1,0:T(8,128)(2,1)S(1)}, bf16[21,128,128]{2,1,0:T(8,128)(2,1)}, u32[]{:S(2)}) copy-start(bf16[21,128,128]{2,1,0:T(8,128)(2,1)} %copy-done.2) | copy-start | bytes 2064388
  81.4 16.9 %copy-start.5 = (bf16[21,128,128]{2,1,0:T(8,128)(2,1)S(1)}, bf16[21,128,128]{2,1,0:T(8,128)(2,1)}, u32[]{:S(2)}) copy-start(bf16[21,128,128]{2,1,0:T(8,128)(2,1)} %copy-done.4) | copy-start | bytes 2064388
  81.4 16.9 %copy-start.7 = (bf16[21,128,128]{2,1,0:T(8,128)(2,1)S(1)}, bf16[21,128,128]{2,1,0:T(8,128)(2,1)}, u32[]{:S(2)}) copy-start(bf16[21,128,128]{2,1,0:T(8,128)(2,1)} %copy-done.6) | copy-start | bytes 2064388
  81.4 16.9 %copy-start.27 = (s32[3]{0:T(128)S(1)}, s32[3]{0:T(128)}, u32[]{:S(2)}) copy-start(s32[3]{0:T(128)} %copy-done.26) | copy-start | bytes 40
  90.8 0.8 copy-start.17
  97.3 1.7 %copy-start.10 = (bf16[21,128,128]{2,1,0:T(8,128)(2,1)S(1)}, bf16[21,128,128]{2,1,0:T(8,128)(2,1)}, u32[]{:S(2)}) copy-start(bf16[21,128,128]{2,1,0:T(8,128)(2,1)} %copy-done.9) | copy-start | bytes 2064388
  97.3 1.7 %copy-start.12 = (bf16[21,128,128]{2,1,0:T(8,128)(2,1)S(1)}, bf16[21,128,128]{2,1,0:T(8,128)(2,1)}, u32[]{:S(2)}) copy-start(bf16[21,128,128]{2,1,0:T(8,128)(2,1)} %copy-done.11) | copy-start | bytes 2064388
  97.3 1.7 %copy-start.14 = (bf16[21,128,128]{2,1,0:T(8,128)(2,1)S(1)}, bf16[21,128,128]{2,1,0:T(8,128)(2,1)}, u32[]{:S(2)}) copy-start(bf16[21,128,128]{2,1,0:T(8,128)(2,1)} %copy-done.13) | copy-start | bytes 2064388
  97.3 1.7 %copy-start.16 = (bf16[21,128,128]{2,1,0:T(8,128)(2,1)S(1)}, bf16[21,128,128]{2,1,0:T(8,128)(2,1)}, u32[]{:S(2)}) copy-start(bf16[21,128,128]{2,1,0:T(8,128)(2,1)} %copy-done.15) | copy-start | bytes 2064388
  97.3 3.7 %collective-permute-start.16 = (f32[4,3,64,128]{3,2,1,0:T(8,128)}, f32[4,3,64,128]{3,2,1,0:T(8,128)S(1)}, u32[]{:S(2)}, u32[]{:S(2)}) collective-permute-start(f32[4,3,64,128]{3,2,1,0:T(8,128)} %get-tuple-element.56), channel_id=1, source_target_pairs={{0,16},{16,0},{1,17},{17,1},{2,18},{18,2},{3,19},{19,3},{4,20},{20... | collective-permute-start | bytes 1179656 | tf_op jit(solution)/shard_map/ppermute | solution.py:42
  98.9 3.8 %collective-permute-start.17 = (bf16[4,128,128]{2,1,0:T(8,128)(2,1)S(1)}, bf16[4,128,128]{2,1,0:T(8,128)(2,1)S(1)}, u32[]{:S(2)}, u32[]{:S(2)}) collective-permute-start(bf16[4,128,128]{2,1,0:T(8,128)(2,1)S(1)} %shard_map.67.refs_6_), channel_id=1, source_target_pairs={{0,16},{16,0},{1,17},{17,1},{2,18},{18,2},{3,19},{19,3},{4,20},{20... | collective-permute-start | bytes 393224 | tf_op jit(solution)/shard_map/ppermute | solution.py:42
  99.0 1.1 copy-start.18
  100.1 1.0 copy-start.25
  102.7 20.2 %all-to-all-start.1 = ((f32[4,3,128,128]{3,2,1,0:T(8,128)}), f32[4,3,128,128]{3,2,1,0:T(8,128)S(1)}, u32[]{:S(2)}, u32[]{:S(2)}) async-start(f32[4,3,128,128]{3,2,1,0:T(8,128)} %shard_map.65), calls=%async_computation.1 | async-start | bytes 1572864 | tf_op jit(solution)/shard_map/all_to_all | solution.py:50
  107.6 2.3 %collective-permute-start.18 = (f32[6,64,64]{2,1,0:T(8,128)S(1)}, f32[6,64,64]{2,1,0:T(8,128)S(1)}, u32[]{:S(2)}, u32[]{:S(2)}) collective-permute-start(f32[6,64,64]{2,1,0:T(8,128)S(1)} %get-tuple-element.62), channel_id=1, source_target_pairs={{0,16},{16,0},{1,17},{17,1},{2,18},{18,2},{3,19},{19,3},{4,20},{20... | collective-permute-start | bytes 294920 | tf_op jit(solution)/shard_map/ppermute | solution.py:42
  110.5 6.4 %collective-permute-start.19 = (f32[64,128]{1,0:T(8,128)S(1)}, f32[64,128]{1,0:T(8,128)S(1)}, u32[]{:S(2)}, u32[]{:S(2)}) collective-permute-start(f32[64,128]{1,0:T(8,128)S(1)} %get-tuple-element.63), channel_id=1, source_target_pairs={{0,44},{1,109},{2,174},{3,239},{32,0},{33,65},{34,130},{35,195},{4... | collective-permute-start | bytes 98312 | tf_op jit(solution)/shard_map/ppermute | solution.py:208
  112.6 6.9 %collective-permute-start.20 = (f32[64,128]{1,0:T(8,128)S(1)}, f32[64,128]{1,0:T(8,128)S(1)}, u32[]{:S(2)}, u32[]{:S(2)}) collective-permute-start(f32[64,128]{1,0:T(8,128)S(1)} %get-tuple-element.64), channel_id=1, source_target_pairs={{0,12},{1,77},{2,142},{3,207},{32,44},{33,109},{34,174},{35,239},{... | collective-permute-start | bytes 98312 | tf_op jit(solution)/shard_map/ppermute | solution.py:208
  112.6 6.8 %collective-permute-start.21 = (f32[64,128]{1,0:T(8,128)S(1)}, f32[64,128]{1,0:T(8,128)S(1)}, u32[]{:S(2)}, u32[]{:S(2)}) collective-permute-start(f32[64,128]{1,0:T(8,128)S(1)} %get-tuple-element.65), channel_id=1, source_target_pairs={{0,40},{1,105},{2,170},{3,235},{32,12},{33,77},{34,142},{35,207},{... | collective-permute-start | bytes 98312 | tf_op jit(solution)/shard_map/ppermute | solution.py:208
  115.7 4.0 %collective-permute-start.22 = (f32[64,128]{1,0:T(8,128)S(1)}, f32[64,128]{1,0:T(8,128)S(1)}, u32[]{:S(2)}, u32[]{:S(2)}) collective-permute-start(f32[64,128]{1,0:T(8,128)S(1)} %get-tuple-element.66), channel_id=1, source_target_pairs={{0,32},{1,97},{2,162},{3,227},{32,4},{33,69},{34,134},{35,199},{4,... | collective-permute-start | bytes 98312 | tf_op jit(solution)/shard_map/ppermute | solution.py:208
  116.9 5.2 %collective-permute-start.23 = (f32[64,128]{1,0:T(8,128)S(1)}, f32[64,128]{1,0:T(8,128)S(1)}, u32[]{:S(2)}, u32[]{:S(2)}) collective-permute-start(f32[64,128]{1,0:T(8,128)S(1)} %get-tuple-element.67), channel_id=1, source_target_pairs={{0,4},{1,69},{2,134},{3,199},{32,36},{33,101},{34,166},{35,231},{4... | collective-permute-start | bytes 98312 | tf_op jit(solution)/shard_map/ppermute | solution.py:208
  117.0 6.0 %collective-permute-start.24 = (f32[64,128]{1,0:T(8,128)S(1)}, f32[64,128]{1,0:T(8,128)S(1)}, u32[]{:S(2)}, u32[]{:S(2)}) collective-permute-start(f32[64,128]{1,0:T(8,128)S(1)} %get-tuple-element.68), channel_id=1, source_target_pairs={{0,36},{1,101},{2,166},{3,231},{32,8},{33,73},{34,138},{35,203},{4... | collective-permute-start | bytes 98312 | tf_op jit(solution)/shard_map/ppermute | solution.py:208
  154.4 12.4 %all-to-all-start.3 = ((f32[8,1,256]{2,1,0:T(1,128)}), f32[8,1,256]{2,1,0:T(1,128)S(1)}, u32[]{:S(2)}, u32[]{:S(2)}) async-start(f32[8,1,256]{2,1,0:T(1,128)} %broadcast_in_dim.4), calls=%async_computation.3 | async-start | bytes 16384 | tf_op jit(solution)/shard_map/all_to_all | solution.py:46
